TPU v7x, 32 devices: a whole 2x2x4 slice. The times are simulated.
32 devices in a mesh: exp: 4 (over y, core), ctx: 8 (over z, x).
Axes of the slice: x: 2, y: 2, z: 4, core: 2. Of those that a mesh axis runs over, the one named last changes fastest.
Arguments:
- activations: bfloat16 [4, 1024, 768], P('exp', 'ctx'), may hold values from -6 to 6
- cotangent: bfloat16 [4, 1024, 768], P('exp', 'ctx'), may hold values from -6 to 6
- query_key_weight: bfloat16 [768, 1536], P(('exp', 'ctx')), may hold values from -0.109375 to 0.109375
- value_weight: bfloat16 [768, 768], P(('exp', 'ctx')), may hold values from -0.21875 to 0.21875
- output_weight: bfloat16 [768, 768], P(('exp', 'ctx')), may hold values from -0.875 to 0.875
- norm_first: bfloat16 [768], P(('exp', 'ctx')), may hold values from 0.5 to 1.5
- norm_second: bfloat16 [768], P(('exp', 'ctx')), may hold values from 0.5 to 1.5
- router_weight: bfloat16 [768, 4], P(('exp', 'ctx')), may hold values from -0.109375 to 0.109375
- bias_table: bfloat16 [32, 12], replicated, may hold values from -4 to 4
- w_in: bfloat16 [768, 4, 3072], P('ctx', 'exp'), may hold values from -0.21875 to 0.21875
- w_out: bfloat16 [3072, 4, 768], P('ctx', 'exp'), may hold values from -0.625 to 0.625
- routes: int32 [4, 1024], P('exp', 'ctx'), may hold values from 0 to 3, as said below
- slots: int32 [4, 1024], P('exp', 'ctx'), may hold values from 0 to 39, as said below
Outputs:
- layer_output: bfloat16 [4, 1024, 768], P('exp', 'ctx')
- grad_activations: bfloat16 [4, 1024, 768], P('exp', 'ctx')
- grad_qk: float32 [768, 1536], P(('exp', 'ctx'))
- grad_v: float32 [768, 768], P(('exp', 'ctx'))
- grad_o: float32 [768, 768], P(('exp', 'ctx'))
- grad_norm_first: float32 [768], P(('exp', 'ctx'))
- grad_norm_second: float32 [768], P(('exp', 'ctx'))
- grad_router: float32 [768, 4], P(('exp', 'ctx'))
- grad_table: float32 [32, 12], replicated
- grad_in: float32 [768, 4, 3072], P('ctx', 'exp')
- grad_out: float32 [3072, 4, 768], P('ctx', 'exp')
Inputs may be any that keep to these rules, and one draw needn't show every extreme that they name: `routes`: within each aligned block of 128 tokens (the tokens of one device) no expert is named more than 40 times; in every block one expert is named exactly 40 times, the same expert for all 4 blocks at one position along the sequences. Tokens of one block that name the same expert have different slots.
All inputs are finite; a program needn't handle non-finite values.
Results may differ from a plain program's by a relative error of at most 0.024.
Values may be sent and summed in bfloat16 or wider, within the bound.
No kernel may reach another device: no remote copies, remote signals or barrier semaphores. Data moves between devices by JAX's collectives and lax.ppermute only.
A program may use at most 128 MiB of HBM per device.

v0:
```python
import math

import jax
import jax.numpy as jnp
import numpy as np
from jax import lax
from jax.sharding import PartitionSpec as P

EPS = 1e-06


def from_behind(value, axis, steps):
    count = lax.axis_size(axis)
    pairs = [(source, (source + steps) % count) for source in range(count)]
    return lax.ppermute(value, axis, pairs)


def t5_buckets(length):
    relative = np.arange(-(length - 1), length)
    flipped = -relative
    result = np.where(flipped < 0, 16, 0)
    magnitude = np.abs(flipped)
    spread = 8 + (np.log(np.maximum(magnitude, 1) / 8.0) / np.log(16.0) * 8.0).astype(np.int64)
    spread = np.minimum(spread, 15)
    result = result + np.where(magnitude < 8, magnitude, spread)
    return jnp.asarray(result.astype(np.int32))


def rms_norm(hidden, gain):
    return hidden * lax.rsqrt(jnp.mean(hidden * hidden, axis=-1, keepdims=True) + EPS) * gain


def exact_gelu(preact):
    return jax.nn.gelu(preact, approximate=False)


def offset_terms(bucket_table, bias_table, query_start, key_start, query_rows, key_count, length):
    slice_first = key_start - query_start + length - query_rows
    bucket_ids = lax.dynamic_slice_in_dim(bucket_table, slice_first, query_rows + key_count - 1)
    selected = (
        bucket_ids[:, None] == jnp.arange(bias_table.shape[0], dtype=jnp.int32)[None, :]
    ).astype(jnp.bfloat16)
    offset_vals = jnp.dot(selected, bias_table, preferred_element_type=jnp.float32)
    return (selected, offset_vals.T)


def spread_offsets(offset_vals, query_rows, key_count):
    head_count = offset_vals.shape[0]
    span = query_rows + key_count - 1
    tiled_rows = jnp.broadcast_to(offset_vals[:, None, :], (head_count, query_rows, span))
    tiled_rows = tiled_rows.reshape(head_count, query_rows * span)
    padded = jnp.pad(tiled_rows, ((0, 0), (0, query_rows)))
    sheared = padded.reshape(head_count, query_rows, span + 1)[:, :, :key_count]
    return sheared[:, ::-1, :]


def offset_sums(grad_blocks, query_rows, key_count):
    head_count = grad_blocks.shape[0]
    span = query_rows + key_count - 1
    flipped = jnp.pad(grad_blocks[:, ::-1, :], ((0, 0), (0, 0), (0, query_rows)))
    flattened = flipped.reshape(head_count, query_rows * (span + 1))[:, : query_rows * span]
    return jnp.sum(flattened.reshape(head_count, query_rows, span), axis=1)


def table_term(grad_scores, selected, query_rows, key_count):
    diag_sums = offset_sums(grad_scores.astype(jnp.float32), query_rows, key_count)
    return jnp.dot(diag_sums, selected.astype(jnp.float32), precision=lax.Precision.HIGHEST).T


def block_grads(query_block, key_block, value_block, grad_block, log_total, row_delta, bias):
    scores = (
        jnp.einsum("qhd,khd->hqk", query_block, key_block, preferred_element_type=jnp.float32)
        + bias
    )
    chances = jnp.exp(scores - log_total[:, :, None])
    grad_chances = jnp.einsum(
        "qhd,khd->hqk", grad_block, value_block, preferred_element_type=jnp.float32
    )
    grad_scores = (chances * (grad_chances - row_delta[:, :, None])).astype(jnp.bfloat16)
    return (chances.astype(jnp.bfloat16), grad_scores)


def per_device(
    activations,
    cotangent,
    query_key_weight,
    value_weight,
    output_weight,
    norm_first,
    norm_second,
    router_weight,
    bias_table,
    w_in,
    w_out,
    routes,
    slots,
):
    block_rows = activations.shape[1]
    cycle_size = lax.axis_size("ctx")
    length = block_rows * cycle_size
    bucket_table = t5_buckets(length)
    experts = router_weight.shape[1]
    capacity = block_rows * 5 // (4 * experts)
    head_count = bias_table.shape[1]
    head_dim = query_key_weight.shape[1] // (2 * head_count)
    feature_width = head_count * head_dim
    my_start = lax.axis_index("ctx") * block_rows
    full_qk, full_v, full_o, gain_first, gain_second, full_router = (
        lax.all_gather(query_key_weight, ("exp", "ctx"), axis=0, tiled=True),
        lax.all_gather(value_weight, ("exp", "ctx"), axis=0, tiled=True),
        lax.all_gather(output_weight, ("exp", "ctx"), axis=0, tiled=True),
        lax.all_gather(norm_first, ("exp", "ctx"), axis=0, tiled=True),
        lax.all_gather(norm_second, ("exp", "ctx"), axis=0, tiled=True),
        lax.all_gather(router_weight, ("exp", "ctx"), axis=0, tiled=True),
    )
    gain_first = gain_first.astype(jnp.float32)
    gain_second = gain_second.astype(jnp.float32)
    inner_weights, outer_weights = (
        lax.all_gather(w_in, "ctx", axis=0, tiled=True),
        lax.all_gather(w_out, "ctx", axis=0, tiled=True),
    )
    hidden = activations[0].astype(jnp.float32)
    normed_low = rms_norm(hidden, gain_first).astype(jnp.bfloat16)
    output_projected = jnp.dot(normed_low, full_qk, preferred_element_type=jnp.float32).astype(
        jnp.bfloat16
    )
    queries = output_projected[:, :feature_width]
    key_rows = output_projected[:, feature_width:]
    value_tensor = jnp.dot(normed_low, full_v, preferred_element_type=jnp.float32).astype(
        jnp.bfloat16
    )
    query_heads = queries.reshape(block_rows, head_count, head_dim)
    key_heads = key_rows.reshape(block_rows, head_count, head_dim)
    value_heads = value_tensor.reshape(block_rows, head_count, head_dim)
    initial = (
        jnp.full((head_count, block_rows), -1e30, jnp.float32),
        jnp.zeros((head_count, block_rows), jnp.float32),
        jnp.zeros((head_count, block_rows, head_dim), jnp.float32),
    )
    running = initial
    key_piece = lax.all_gather(key_rows, "ctx", axis=0, tiled=True)
    value_piece = lax.all_gather(value_tensor, "ctx", axis=0, tiled=True)
    piece_rows = key_piece.shape[0]
    key_count = math.gcd(piece_rows, 512)
    block_count = piece_rows // key_count
    key_blocks = key_piece.reshape(block_count, key_count, head_count, head_dim)
    value_blocks = value_piece.reshape(block_count, key_count, head_count, head_dim)

    def fold_step(fold_state, block_item):
        key_block, value_block, block_index = block_item
        running_max, running_total, running_acc = fold_state
        selected, offset_vals = offset_terms(
            bucket_table,
            bias_table,
            my_start,
            block_index * key_count,
            block_rows,
            key_count,
            length,
        )
        scores = jnp.einsum(
            "qhd,khd->hqk", query_heads, key_block, preferred_element_type=jnp.float32
        ) + spread_offsets(offset_vals, block_rows, key_count)
        new_max = jnp.maximum(running_max, jnp.max(scores, axis=-1))
        rescale = jnp.exp(running_max - new_max)
        weights = jnp.exp(scores - new_max[:, :, None])
        running_total = running_total * rescale + jnp.sum(weights, axis=-1)
        running_acc = running_acc * rescale[:, :, None] + jnp.einsum(
            "hqk,khd->hqd",
            weights.astype(jnp.bfloat16),
            value_block,
            preferred_element_type=jnp.float32,
        )
        return ((new_max, running_total, running_acc), None)

    running, _ = lax.scan(
        fold_step, running, (key_blocks, value_blocks, jnp.arange(block_count, dtype=jnp.int32))
    )
    run_max, run_total, run_acc = running
    attention_result = run_acc / run_total[:, :, None]
    log_total = run_max + jnp.log(run_total)
    attended_low = (
        jnp.transpose(attention_result, (1, 0, 2))
        .reshape(block_rows, feature_width)
        .astype(jnp.bfloat16)
    )
    hidden_middle = hidden + jnp.dot(attended_low, full_o, preferred_element_type=jnp.float32)
    mixed_low = rms_norm(hidden_middle, gain_second).astype(jnp.bfloat16)
    router_scores = jnp.dot(mixed_low, full_router, preferred_element_type=jnp.float32)
    chances = jax.nn.softmax(router_scores, axis=-1)
    expert_ids = jnp.arange(experts, dtype=jnp.int32)
    route_mask = (routes[0][:, None] == expert_ids[None, :]).astype(jnp.float32)
    gate_value = jnp.sum(chances * route_mask, axis=-1)
    slot_ids = jnp.arange(capacity, dtype=jnp.int32)
    select = (
        (routes[0][None, None, :] == expert_ids[:, None, None])
        & (slots[0][None, None, :] == slot_ids[None, :, None])
    ).astype(jnp.bfloat16)
    group_count = lax.axis_size("exp")
    local_experts = experts // group_count
    outgoing = jnp.einsum(
        "ecb,bd->ecd", select, mixed_low, preferred_element_type=jnp.float32
    ).astype(jnp.bfloat16)
    outgoing = outgoing.reshape(group_count, local_experts, capacity, -1)
    arrived = lax.all_to_all(outgoing, "exp", split_axis=0, concat_axis=0, tiled=True)
    preact = jnp.einsum(
        "sgcd,dgf->sgcf", arrived, inner_weights, preferred_element_type=jnp.float32
    )
    activated = exact_gelu(preact).astype(jnp.bfloat16)
    produced = jnp.einsum(
        "sgcf,fgd->sgcd", activated, outer_weights, preferred_element_type=jnp.float32
    ).astype(jnp.bfloat16)
    produced, activated, preact, arrived = (produced, activated, preact, arrived)

    def group_swap(blocks):
        return lax.all_to_all(blocks, "exp", split_axis=0, concat_axis=0, tiled=True)

    returned = group_swap(produced).reshape(experts, capacity, -1)
    expert_rows = jnp.einsum("ecb,ecd->bd", select, returned, preferred_element_type=jnp.float32)
    layer_output = (hidden_middle + gate_value[:, None] * expert_rows).astype(jnp.bfloat16)[None]
    grad_z = cotangent[0].astype(jnp.float32)
    grad_gate = jnp.sum(grad_z * expert_rows, axis=-1)
    grad_rows = (gate_value[:, None] * grad_z).astype(jnp.bfloat16)
    grad_sent = jnp.einsum(
        "ecb,bd->ecd", select, grad_rows, preferred_element_type=jnp.float32
    ).astype(jnp.bfloat16)
    grad_produced = group_swap(grad_sent.reshape(group_count, local_experts, capacity, -1))
    grad_activated = jnp.einsum(
        "sgcd,fgd->sgcf", grad_produced, outer_weights, preferred_element_type=jnp.float32
    )
    _, gelu_pull = jax.vjp(exact_gelu, preact)
    grad_preact = gelu_pull(grad_activated)[0].astype(jnp.bfloat16)
    grad_arrived = jnp.einsum(
        "sgcf,dgf->sgcd", grad_preact, inner_weights, preferred_element_type=jnp.float32
    ).astype(jnp.bfloat16)
    grad_outer = jnp.einsum(
        "sgcf,sgcd->fgd", activated, grad_produced, preferred_element_type=jnp.float32
    )
    grad_inner = jnp.einsum(
        "sgcd,sgcf->dgf", arrived, grad_preact, preferred_element_type=jnp.float32
    )
    grad_inner, grad_outer = (
        lax.psum_scatter(grad_inner, "ctx", scatter_dimension=0, tiled=True),
        lax.psum_scatter(grad_outer, "ctx", scatter_dimension=0, tiled=True),
    )
    grad_back = group_swap(grad_arrived).reshape(experts, capacity, -1)
    grad_mixed = jnp.einsum("ecb,ecd->bd", select, grad_back, preferred_element_type=jnp.float32)
    grad_logits = ((gate_value * grad_gate)[:, None] * (route_mask - chances)).astype(jnp.bfloat16)
    grad_router = jnp.einsum(
        "bd,be->de", mixed_low, grad_logits, preferred_element_type=jnp.float32
    )
    grad_mixed = grad_mixed + jnp.einsum(
        "be,de->bd", grad_logits, full_router, preferred_element_type=jnp.float32
    )
    _, second_pull = jax.vjp(rms_norm, hidden_middle, gain_second)
    grad_middle, grad_gain_second = second_pull(grad_mixed)
    grad_middle = grad_middle + grad_z
    grad_branch = grad_middle.astype(jnp.bfloat16)
    grad_o = jnp.einsum("be,bd->ed", attended_low, grad_branch, preferred_element_type=jnp.float32)
    grad_attended = jnp.einsum(
        "bd,ed->be", grad_branch, full_o, preferred_element_type=jnp.float32
    ).astype(jnp.bfloat16)
    grad_heads = grad_attended.reshape(block_rows, head_count, head_dim)
    row_delta = jnp.sum(
        jnp.transpose(grad_heads.astype(jnp.float32), (1, 0, 2)) * attention_result, axis=-1
    )

    def block_update(key_block, value_block, key_start):
        selected, offset_vals = offset_terms(
            bucket_table, bias_table, my_start, key_start, block_rows, block_rows, length
        )
        weights_low, grad_scores = block_grads(
            query_heads,
            key_block,
            value_block,
            grad_heads,
            log_total,
            row_delta,
            spread_offsets(offset_vals, block_rows, block_rows),
        )
        grad_query = jnp.einsum(
            "hqk,khd->qhd", grad_scores, key_block, preferred_element_type=jnp.float32
        )
        grad_key = jnp.einsum(
            "hqk,qhd->khd", grad_scores, query_heads, preferred_element_type=jnp.float32
        )
        grad_value = jnp.einsum(
            "hqk,qhd->khd", weights_low, grad_heads, preferred_element_type=jnp.float32
        )
        return (
            grad_query,
            grad_key,
            grad_value,
            table_term(grad_scores, selected, block_rows, block_rows),
        )

    def pass_grads(grad_pair):
        return (
            from_behind(grad_pair[0].astype(jnp.bfloat16), "ctx", 1).astype(jnp.float32),
            from_behind(grad_pair[1].astype(jnp.bfloat16), "ctx", 1).astype(jnp.float32),
        )

    grad_query, grad_key, grad_value, grad_tab = block_update(key_heads, value_heads, my_start)

    def cycle_step(cycle_turn, cycle_state):
        key_block, value_block, grad_query, grad_key, grad_value, grad_tab = cycle_state
        key_block, value_block = from_behind((key_block, value_block), "ctx", 1)
        grad_key, grad_value = pass_grads((grad_key, grad_value))
        source = lax.rem(lax.axis_index("ctx") - cycle_turn + cycle_size, cycle_size)
        more_query, more_key, more_value, more_tab = block_update(
            key_block, value_block, source * block_rows
        )
        return (
            key_block,
            value_block,
            grad_query + more_query,
            grad_key + more_key,
            grad_value + more_value,
            grad_tab + more_tab,
        )

    cycle_state = lax.fori_loop(
        1,
        cycle_size,
        cycle_step,
        (key_heads, value_heads, grad_query, grad_key, grad_value, grad_tab),
    )
    grad_query = cycle_state[2]
    grad_tab = cycle_state[5]
    grad_key, grad_value = pass_grads((cycle_state[3], cycle_state[4]))
    grad_projected = jnp.concatenate(
        [
            grad_query.reshape(block_rows, feature_width),
            grad_key.reshape(block_rows, feature_width),
        ],
        axis=-1,
    ).astype(jnp.bfloat16)
    grad_values = grad_value.reshape(block_rows, feature_width).astype(jnp.bfloat16)
    grad_qk = jnp.einsum(
        "bd,be->de", normed_low, grad_projected, preferred_element_type=jnp.float32
    )
    grad_v = jnp.einsum("bd,be->de", normed_low, grad_values, preferred_element_type=jnp.float32)
    grad_normed = jnp.einsum(
        "be,de->bd", grad_projected, full_qk, preferred_element_type=jnp.float32
    )
    grad_normed = grad_normed + jnp.einsum(
        "be,de->bd", grad_values, full_v, preferred_element_type=jnp.float32
    )
    _, first_pull = jax.vjp(rms_norm, hidden, gain_first)
    grad_hidden, grad_gain_first = first_pull(grad_normed)
    grad_activations = (grad_middle + grad_hidden).astype(jnp.bfloat16)[None]
    shard_qk, shard_v, shard_o, shard_first, shard_second, shard_router = (
        lax.psum_scatter(grad_qk, ("exp", "ctx"), scatter_dimension=0, tiled=True),
        lax.psum_scatter(grad_v, ("exp", "ctx"), scatter_dimension=0, tiled=True),
        lax.psum_scatter(grad_o, ("exp", "ctx"), scatter_dimension=0, tiled=True),
        lax.psum_scatter(grad_gain_first, ("exp", "ctx"), scatter_dimension=0, tiled=True),
        lax.psum_scatter(grad_gain_second, ("exp", "ctx"), scatter_dimension=0, tiled=True),
        lax.psum_scatter(grad_router, ("exp", "ctx"), scatter_dimension=0, tiled=True),
    )
    grad_table = lax.psum(grad_tab, ("exp", "ctx"))
    return (
        layer_output,
        grad_activations,
        shard_qk,
        shard_v,
        shard_o,
        shard_first,
        shard_second,
        shard_router,
        grad_table,
        grad_inner,
        grad_outer,
    )


def solution(mesh):
    placed = (
        P("exp", "ctx", None),
        P("exp", "ctx", None),
        P(("exp", "ctx"), None),
        P(("exp", "ctx"), None),
        P(("exp", "ctx"), None),
        P(("exp", "ctx")),
        P(("exp", "ctx")),
        P(("exp", "ctx"), None),
        P(),
        P("ctx", "exp", None),
        P("ctx", "exp", None),
        P("exp", "ctx"),
        P("exp", "ctx"),
    )
    return jax.shard_map(
        per_device,
        mesh=mesh,
        in_specs=placed,
        out_specs=(
            P("exp", "ctx", None),
            P("exp", "ctx", None),
            P(("exp", "ctx"), None),
            P(("exp", "ctx"), None),
            P(("exp", "ctx"), None),
            P(("exp", "ctx")),
            P(("exp", "ctx")),
            P(("exp", "ctx"), None),
            P(),
            P("ctx", "exp", None),
            P("ctx", "exp", None),
        ),
        check_vma=False,
    )
```

profile of v0, /device:TPU:1, one launch (start us, length us, event | category | flops | bytes accessed | tf_op | source)
XLA Modules:
  0.0 1353.7 jit_solution(5150106084581513900)
XLA Ops:
  10.4 41.0 %all-reduce.12 = (bf16[768]{0:T(1024)(128)(2,1)S(1)}, bf16[768]{0:T(1024)(128)(2,1)S(1)}) all-reduce(bf16[768]{0:T(1024)(128)(2,1)S(1)} %dynamic-update-slice, bf16[768]{0:T(1024)(128)(2,1)S(1)} %dynamic-update-slice.1), channel_id=1, replica_groups=mesh['exp'=4,'ctx'=8] {'exp','ctx'}, use_global_device_ids=true, to_apply=%add.5 | all-reduce | flops 1536 | bytes 6144
  52.5 15.2 %all-gather.13.cloned.1.call-done = bf16[768,768]{1,0:T(8,128)(2,1)} async-done(((bf16[24,768]{1,0:T(8,128)(2,1)}), bf16[768,768]{1,0:T(8,128)(2,1)}) %all-gather.13.cloned.1.call-update) | async-done | bytes 1179664 | tf_op jit(solution)/shard_map/all_gather | solution.py:110
  70.2 56.8 %all-gather.9.cloned.1.call-done = bf16[768,1536]{1,0:T(8,128)(2,1)} async-done(((bf16[24,1536]{1,0:T(8,128)(2,1)}), bf16[768,1536]{1,0:T(8,128)(2,1)}) %all-gather.9.cloned.1.call-update) | async-done | bytes 2359312 | tf_op jit(solution)/shard_map/all_gather | solution.py:109
  131.9 59.4 %all-gather = bf16[32,24,4]{1,2,0:T(4,128)(2,1)S(1)} all-gather(bf16[1,24,4]{1,2,0:T(4,128)(2,1)S(1)} %bitcast.419), channel_id=1, replica_groups=mesh['exp'=4,'ctx'=8] {'exp','ctx'}, dimensions={0}, use_global_device_ids=true | all-gather | bytes 6336 | tf_op jit(solution)/shard_map/all_gather | solution.py:114
  196.0 21.3 %all-gather.11.cloned.1.call-done = bf16[1024,768]{1,0:T(8,128)(2,1)} async-done(((bf16[128,768]{1,0:T(8,128)(2,1)}), bf16[1024,768]{1,0:T(8,128)(2,1)}) %all-gather.11.cloned.1.call-update) | async-done | bytes 1572880 | tf_op jit(solution)/shard_map/all_gather | solution.py:141
  221.7 96.2 %while.49 = (s32[]{:T(128)}, f32[12,128]{1,0:T(8,128)S(1)}, f32[12,128]{1,0:T(8,128)S(1)}, f32[12,128,64]{1,2,0:T(8,128)}, bf16[2,512,12,64]{1,3,2,0:T(8,128)(2,...) while((s32[]{:T(128)}, f32[12,128]{1,0:T(8,128)S(1)}, ...), condition=%wide.region_4.5_spmd.clone.clone, body=%wide.region_1.4_spmd.sunk.clone.clone.sunk | while | flops 206858976 | bytes 73744888 | solution.py:176
  225.5 6.1 reshape.375
  238.2 25.7 %rev.55 = f32[12,128,512]{1,2,0:T(8,128)} reverse(f32[12,128,512]{1,2,0:T(8,128)} %copy.89), dimensions={1} | reverse | bytes 6291456 | tf_op jit(solution)/shard_map/while/body/eval_jaxpr/rev | solution.py:54
  273.6 6.1 reshape.375
  286.3 25.8 %rev.55 = f32[12,128,512]{1,2,0:T(8,128)} reverse(f32[12,128,512]{1,2,0:T(8,128)} %copy.89), dimensions={1} | reverse | bytes 6291456 | tf_op jit(solution)/shard_map/while/body/eval_jaxpr/rev | solution.py:54
  321.9 5.0 all-to-all-start
  328.1 3.9 all-to-all-done
  332.0 4.1 all-to-all-start.2
  336.4 17.3 %all-gather.19.cloned.1.call-done = bf16[768,1,3072]{2,0,1:T(8,128)(2,1)} async-done(((bf16[96,1,3072]{2,0,1:T(8,128)(2,1)}), bf16[768,1,3072]{2,0,1:T(8,128)(2,1)}) %all-gather.19.cloned.1.call-update) | async-done | bytes 4718608 | tf_op jit(solution)/shard_map/all_gather | solution.py:119
  357.0 76.9 %all-gather.21.cloned.1.call-done = bf16[3072,1,768]{2,0,1:T(8,128)(2,1)} async-done(((bf16[384,1,768]{2,0,1:T(8,128)(2,1)}), bf16[3072,1,768]{2,0,1:T(8,128)(2,1)}) %all-gather.21.cloned.1.call-update) | async-done | bytes 4718608 | tf_op jit(solution)/shard_map/all_gather | solution.py:120
  433.9 7.2 fusion.46
  442.1 5.1 convolution_bitcast_fusion.6
  447.2 20.6 %copy.71 = f32[768,1,3072]{2,1,0:T(1,128)} copy(f32[768,1,3072]{0,2,1:T(8,128)} %convolution_bitcast_fusion.6) | data formatting | bytes 18874368 | tf_op jit(solution)/shard_map/sgcd,sgcf->dgf/transpose | solution.py:239
  467.9 7.3 convolution_bitcast_fusion.5
  483.3 8.8 fusion.69
  492.2 5.1 all-to-all-start.1
  497.2 4.8 fusion.72
  502.3 4.1 all-to-all-start.3
  506.4 12.6 reduce-scatter.10.cloned.1.call-start
  530.5 3.4 reshape.334
  542.6 261.4 %while.48 = (s32[]{:T(128)}, bf16[128,12,64]{0,2,1:T(8,128)(2,1)}, bf16[128,12,64]{0,2,1:T(8,128)(2,1)}, f32[128,12,64]{0,2,1:T(8,128)}, bf16[128,12,64]{0,2,1:T...) while((s32[]{:T(128)}, bf16[128,12,64]{0,2,1:T(8,128)(2,1)}, ...), condition=%wide.region_15.16_spmd.clone, body=%wide.region_13.15_spmd.sunk.clone.sunk | while | flops 129473120 | bytes 51984648 | solution.py:322
  551.8 4.9 collective-permute-done
  557.1 8.0 collective-permute-done.1
  569.3 3.4 reshape.374
  584.0 10.9 collective-permute-start.2
  608.5 3.4 reshape.374
  626.5 3.6 collective-permute-start.3
  641.3 3.4 reshape.374
  655.6 3.6 collective-permute-start.2
  659.2 3.9 collective-permute-start.3
  673.2 3.4 reshape.374
  687.4 6.1 collective-permute-start.2
  693.4 3.7 collective-permute-start.3
  722.9 3.8 collective-permute-start.2
  757.0 22.0 %collective-permute-start.2 = (bf16[128,12,64]{0,2,1:T(8,128)(2,1)}, bf16[128,12,64]{0,2,1:T(8,128)(2,1)}, u32[]{:S(2)}, u32[]{:S(2)}) collective-permute-start(bf16[128,12,64]{0,2,1:T(8,128)(2,1)} %get-tuple-element.1155), channel_id=1, source_target_pairs={{0,1},{1,2},{2,3},{3,4},{4,5},{5,6},{6,7},{7,0},{8,9},{9,10},{10,1... | collective-permute-start | bytes 589832 | tf_op jit(solution)/shard_map/while/body/eval_jaxpr/ppermute | solution.py:15
  806.0 9.7 collective-permute-done.5
  821.3 33.3 %collective-permute-done.4 = bf16[128,12,64]{0,2,1:T(8,128)(2,1)S(1)} collective-permute-done((bf16[128,12,64]{0,2,1:T(8,128)(2,1)}, bf16[128,12,64]{0,2,1:T(8,128)(2,1)S(1)}, u32[]{:S(2)}, u32[]{:S(2)}) %collective-permute-start.4) | collective-permute-done | bytes 196640 | tf_op jit(solution)/shard_map/ppermute | solution.py:15
  864.1 60.5 %all-reduce.11 = (f32[768]{0:T(1024)S(1)}, f32[768]{0:T(1024)S(1)}, f32[768,4]{0,1:T(4,128)S(1)}, f32[32,12]{0,1:T(8,128)}) all-reduce(f32[768]{0:T(1024)} %get-tuple-element.859, f32[768]{0:T(1024)} %get-tuple-element.857, f32[768,4]{0,1:T(4,128)S(1)} %fusion.138, ...), channel_id=5, replica_groups=mesh['exp'=4,'ctx'=8] {'exp','ctx'}, use_global_device_ids=true, to_apply=%region_21.22.clone | all-reduce | flops 4992 | bytes 39936
  930.8 97.0 %reduce-scatter.12.cloned.1.call-done = f32[384,1,768]{0,2,1:T(8,128)} async-done(((f32[3072,1,768]{0,2,1:T(8,128)}), f32[384,1,768]{0,2,1:T(8,128)}) %reduce-scatter.12.cloned.1.call-update) | async-done | bytes 1179664 | tf_op jit(solution)/shard_map/reduce_scatter | solution.py:244
  1027.8 4.7 copy.72
  1032.4 97.6 %reduce-scatter.10.cloned.1.call-done = f32[24,768]{1,0:T(8,128)} async-done(((f32[768,768]{1,0:T(8,128)}), f32[24,768]{1,0:T(8,128)}) %reduce-scatter.10.cloned.1.call-update) | async-done | bytes 73744 | tf_op jit(solution)/shard_map/reduce_scatter | solution.py:355
  1130.0 104.7 %reduce-scatter.8.cloned.1.call-done = f32[24,768]{1,0:T(8,128)} async-done(((f32[768,768]{1,0:T(8,128)}), f32[24,768]{1,0:T(8,128)}) %reduce-scatter.8.cloned.1.call-update) | async-done | bytes 73744 | tf_op jit(solution)/shard_map/reduce_scatter | solution.py:354
  1234.7 111.9 %reduce-scatter.6.cloned.1.call-done = f32[24,1536]{1,0:T(8,128)} async-done(((f32[768,1536]{1,0:T(8,128)}), f32[24,1536]{1,0:T(8,128)}) %reduce-scatter.6.cloned.1.call-update) | async-done | bytes 147472 | tf_op jit(solution)/shard_map/reduce_scatter | solution.py:353
  (517 shorter events, 288.8 us)
Async XLA Ops:
  7.2 60.5 %all-gather.13.cloned.1.call-start = ((), (), s32[]{:S(2)}) async-start(), calls=%async_computation.10 | async-start | bytes 1216512 | tf_op jit(solution)/shard_map/all_gather | solution.py:110
  7.9 119.1 %all-gather.9.cloned.1.call-start = ((), (), s32[]{:S(2)}) async-start(), calls=%async_computation.8 | async-start | bytes 2433024 | tf_op jit(solution)/shard_map/all_gather | solution.py:109
  8.7 183.0 %all-gather.15.cloned.1.call-start = ((), (), s32[]{:S(2)}) async-start(), calls=%async_computation.11 | async-start | bytes 1769472 | tf_op jit(solution)/shard_map/all_gather | solution.py:142
  70.2 147.1 %all-gather.11.cloned.1.call-start = ((), (), s32[]{:S(2)}) async-start(), calls=%async_computation.9 | async-start | bytes 1769472 | tf_op jit(solution)/shard_map/all_gather | solution.py:141
  130.0 189.1 %all-gather.17.cloned.1.call-start = ((), (), s32[]{:S(2)}) async-start(), calls=%async_computation.12 | async-start | bytes 1216512 | tf_op jit(solution)/shard_map/all_gather | solution.py:111
  130.6 223.1 %all-gather.19.cloned.1.call-start = ((), (), s32[]{:S(2)}) async-start(), calls=%async_computation.13 | async-start | bytes 5308416 | tf_op jit(solution)/shard_map/all_gather | solution.py:119
  131.1 302.8 %all-gather.21.cloned.1.call-start = ((), (), s32[]{:S(2)}) async-start(), calls=%async_computation.14 | async-start | bytes 5308416 | tf_op jit(solution)/shard_map/all_gather | solution.py:120
  321.9 10.1 all-to-all-start
  332.0 25.0 %all-to-all-start.2 = ((bf16[4,1,40,768]{3,2,1,0:T(8,128)(2,1)}), bf16[4,1,40,768]{3,2,1,0:T(8,128)(2,1)S(1)}, u32[]{:S(2)}, u32[]{:S(2)}) async-start(bf16[4,1,40,768]{3,2,1,0:T(8,128)(2,1)} %fusion.68), calls=%async_computation.2 | async-start | bytes 491520 | tf_op jit(solution)/shard_map/all_to_all | solution.py:216
  336.1 592.3 %all-reduce.15.cloned.1.call-start = ((), (), s32[]{:S(2)}) async-start(), calls=%async_computation.19 | async-start | bytes 18874368
  467.8 559.9 %reduce-scatter.12.cloned.1.call-start = ((), (), s32[]{:S(2)}) async-start(), calls=%async_computation.18 | async-start | bytes 10616832 | tf_op jit(solution)/shard_map/reduce_scatter | solution.py:244
  492.2 10.2 all-to-all-start.1
  502.3 19.1 %all-to-all-start.3 = ((bf16[4,1,40,768]{3,2,1,0:T(8,128)(2,1)}), bf16[4,1,40,768]{3,2,1,0:T(8,128)(2,1)S(1)}, u32[]{:S(2)}, u32[]{:S(2)}) async-start(bf16[4,1,40,768]{3,2,1,0:T(8,128)(2,1)} %fusion.72), calls=%async_computation.3 | async-start | bytes 491520 | tf_op jit(solution)/shard_map/all_to_all | solution.py:216
  506.4 623.6 %reduce-scatter.10.cloned.1.call-start = ((), (), s32[]{:S(2)}) async-start(), calls=%async_computation.17 | async-start | bytes 2433024 | tf_op jit(solution)/shard_map/reduce_scatter | solution.py:355
  542.5 692.2 %reduce-scatter.8.cloned.1.call-start = ((), (), s32[]{:S(2)}) async-start(), calls=%async_computation.16 | async-start | bytes 2433024 | tf_op jit(solution)/shard_map/reduce_scatter | solution.py:354
  542.5 273.1 %copy-start.33 = (f32[768]{0:T(1024)S(1)}, f32[768]{0:T(1024)}, u32[]{:S(2)}) copy-start(f32[768]{0:T(1024)} %copy-done.32) | copy-start | bytes 9220
  542.5 273.1 %copy-start.36 = (f32[128]{0:T(128)S(1)}, f32[128]{0:T(128)}, u32[]{:S(2)}) copy-start(f32[128]{0:T(128)} %copy-done.35) | copy-start | bytes 1540
  542.6 14.1 %collective-permute-start = (bf16[128,12,64]{0,2,1:T(8,128)(2,1)}, bf16[128,12,64]{0,2,1:T(8,128)(2,1)S(1)}, u32[]{:S(2)}, u32[]{:S(2)}) collective-permute-start(bf16[128,12,64]{0,2,1:T(8,128)(2,1)} %get-tuple-element.1152), channel_id=1, source_target_pairs={{0,1},{1,2},{2,3},{3,4},{4,5},{5,6},{6,7},{7,0},{8,9},{9,10},{10,1... | collective-permute-start | bytes 589832 | tf_op jit(solution)/shard_map/while/body/eval_jaxpr/ppermute | solution.py:15
  542.8 22.3 %collective-permute-start.1 = (bf16[128,12,64]{0,2,1:T(8,128)(2,1)}, bf16[128,12,64]{0,2,1:T(8,128)(2,1)S(1)}, u32[]{:S(2)}, u32[]{:S(2)}) collective-permute-start(bf16[128,12,64]{0,2,1:T(8,128)(2,1)} %get-tuple-element.1153), channel_id=1, source_target_pairs={{0,1},{1,2},{2,3},{3,4},{4,5},{5,6},{6,7},{7,0},{8,9},{9,10},{10,1... | collective-permute-start | bytes 589832 | tf_op jit(solution)/shard_map/while/body/eval_jaxpr/ppermute | solution.py:15
  544.1 32.9 %collective-permute-start.2 = (bf16[128,12,64]{0,2,1:T(8,128)(2,1)}, bf16[128,12,64]{0,2,1:T(8,128)(2,1)}, u32[]{:S(2)}, u32[]{:S(2)}) collective-permute-start(bf16[128,12,64]{0,2,1:T(8,128)(2,1)} %get-tuple-element.1155), channel_id=1, source_target_pairs={{0,1},{1,2},{2,3},{3,4},{4,5},{5,6},{6,7},{7,0},{8,9},{9,10},{10,1... | collective-permute-start | bytes 589832 | tf_op jit(solution)/shard_map/while/body/eval_jaxpr/ppermute | solution.py:15
  544.8 37.2 %collective-permute-start.3 = (bf16[128,12,64]{0,2,1:T(8,128)(2,1)}, bf16[128,12,64]{0,2,1:T(8,128)(2,1)}, u32[]{:S(2)}, u32[]{:S(2)}) collective-permute-start(bf16[128,12,64]{0,2,1:T(8,128)(2,1)} %get-tuple-element.1156), channel_id=1, source_target_pairs={{0,1},{1,2},{2,3},{3,4},{4,5},{5,6},{6,7},{7,0},{8,9},{9,10},{10,1... | collective-permute-start | bytes 589832 | tf_op jit(solution)/shard_map/while/body/eval_jaxpr/ppermute | solution.py:15
  584.0 19.3 %collective-permute-start = (bf16[128,12,64]{0,2,1:T(8,128)(2,1)}, bf16[128,12,64]{0,2,1:T(8,128)(2,1)S(1)}, u32[]{:S(2)}, u32[]{:S(2)}) collective-permute-start(bf16[128,12,64]{0,2,1:T(8,128)(2,1)} %get-tuple-element.1152), channel_id=1, source_target_pairs={{0,1},{1,2},{2,3},{3,4},{4,5},{5,6},{6,7},{7,0},{8,9},{9,10},{10,1... | collective-permute-start | bytes 589832 | tf_op jit(solution)/shard_map/while/body/eval_jaxpr/ppermute | solution.py:15
  584.0 20.4 %collective-permute-start.1 = (bf16[128,12,64]{0,2,1:T(8,128)(2,1)}, bf16[128,12,64]{0,2,1:T(8,128)(2,1)S(1)}, u32[]{:S(2)}, u32[]{:S(2)}) collective-permute-start(bf16[128,12,64]{0,2,1:T(8,128)(2,1)} %get-tuple-element.1153), channel_id=1, source_target_pairs={{0,1},{1,2},{2,3},{3,4},{4,5},{5,6},{6,7},{7,0},{8,9},{9,10},{10,1... | collective-permute-start | bytes 589832 | tf_op jit(solution)/shard_map/while/body/eval_jaxpr/ppermute | solution.py:15
  584.0 32.3 %collective-permute-start.2 = (bf16[128,12,64]{0,2,1:T(8,128)(2,1)}, bf16[128,12,64]{0,2,1:T(8,128)(2,1)}, u32[]{:S(2)}, u32[]{:S(2)}) collective-permute-start(bf16[128,12,64]{0,2,1:T(8,128)(2,1)} %get-tuple-element.1155), channel_id=1, source_target_pairs={{0,1},{1,2},{2,3},{3,4},{4,5},{5,6},{6,7},{7,0},{8,9},{9,10},{10,1... | collective-permute-start | bytes 589832 | tf_op jit(solution)/shard_map/while/body/eval_jaxpr/ppermute | solution.py:15
  594.9 23.6 %collective-permute-start.3 = (bf16[128,12,64]{0,2,1:T(8,128)(2,1)}, bf16[128,12,64]{0,2,1:T(8,128)(2,1)}, u32[]{:S(2)}, u32[]{:S(2)}) collective-permute-start(bf16[128,12,64]{0,2,1:T(8,128)(2,1)} %get-tuple-element.1156), channel_id=1, source_target_pairs={{0,1},{1,2},{2,3},{3,4},{4,5},{5,6},{6,7},{7,0},{8,9},{9,10},{10,1... | collective-permute-start | bytes 589832 | tf_op jit(solution)/shard_map/while/body/eval_jaxpr/ppermute | solution.py:15
  620.4 15.0 %collective-permute-start = (bf16[128,12,64]{0,2,1:T(8,128)(2,1)}, bf16[128,12,64]{0,2,1:T(8,128)(2,1)S(1)}, u32[]{:S(2)}, u32[]{:S(2)}) collective-permute-start(bf16[128,12,64]{0,2,1:T(8,128)(2,1)} %get-tuple-element.1152), channel_id=1, source_target_pairs={{0,1},{1,2},{2,3},{3,4},{4,5},{5,6},{6,7},{7,0},{8,9},{9,10},{10,1... | collective-permute-start | bytes 589832 | tf_op jit(solution)/shard_map/while/body/eval_jaxpr/ppermute | solution.py:15
  620.7 16.3 %collective-permute-start.1 = (bf16[128,12,64]{0,2,1:T(8,128)(2,1)}, bf16[128,12,64]{0,2,1:T(8,128)(2,1)S(1)}, u32[]{:S(2)}, u32[]{:S(2)}) collective-permute-start(bf16[128,12,64]{0,2,1:T(8,128)(2,1)} %get-tuple-element.1153), channel_id=1, source_target_pairs={{0,1},{1,2},{2,3},{3,4},{4,5},{5,6},{6,7},{7,0},{8,9},{9,10},{10,1... | collective-permute-start | bytes 589832 | tf_op jit(solution)/shard_map/while/body/eval_jaxpr/ppermute | solution.py:15
  623.9 25.1 %collective-permute-start.2 = (bf16[128,12,64]{0,2,1:T(8,128)(2,1)}, bf16[128,12,64]{0,2,1:T(8,128)(2,1)}, u32[]{:S(2)}, u32[]{:S(2)}) collective-permute-start(bf16[128,12,64]{0,2,1:T(8,128)(2,1)} %get-tuple-element.1155), channel_id=1, source_target_pairs={{0,1},{1,2},{2,3},{3,4},{4,5},{5,6},{6,7},{7,0},{8,9},{9,10},{10,1... | collective-permute-start | bytes 589832 | tf_op jit(solution)/shard_map/while/body/eval_jaxpr/ppermute | solution.py:15
  626.5 27.2 %collective-permute-start.3 = (bf16[128,12,64]{0,2,1:T(8,128)(2,1)}, bf16[128,12,64]{0,2,1:T(8,128)(2,1)}, u32[]{:S(2)}, u32[]{:S(2)}) collective-permute-start(bf16[128,12,64]{0,2,1:T(8,128)(2,1)} %get-tuple-element.1156), channel_id=1, source_target_pairs={{0,1},{1,2},{2,3},{3,4},{4,5},{5,6},{6,7},{7,0},{8,9},{9,10},{10,1... | collective-permute-start | bytes 589832 | tf_op jit(solution)/shard_map/while/body/eval_jaxpr/ppermute | solution.py:15
  655.6 12.9 collective-permute-start
  655.6 13.3 collective-permute-start.1
  655.6 25.2 %collective-permute-start.2 = (bf16[128,12,64]{0,2,1:T(8,128)(2,1)}, bf16[128,12,64]{0,2,1:T(8,128)(2,1)}, u32[]{:S(2)}, u32[]{:S(2)}) collective-permute-start(bf16[128,12,64]{0,2,1:T(8,128)(2,1)} %get-tuple-element.1155), channel_id=1, source_target_pairs={{0,1},{1,2},{2,3},{3,4},{4,5},{5,6},{6,7},{7,0},{8,9},{9,10},{10,1... | collective-permute-start | bytes 589832 | tf_op jit(solution)/shard_map/while/body/eval_jaxpr/ppermute | solution.py:15
  659.2 23.9 %collective-permute-start.3 = (bf16[128,12,64]{0,2,1:T(8,128)(2,1)}, bf16[128,12,64]{0,2,1:T(8,128)(2,1)}, u32[]{:S(2)}, u32[]{:S(2)}) collective-permute-start(bf16[128,12,64]{0,2,1:T(8,128)(2,1)} %get-tuple-element.1156), channel_id=1, source_target_pairs={{0,1},{1,2},{2,3},{3,4},{4,5},{5,6},{6,7},{7,0},{8,9},{9,10},{10,1... | collective-permute-start | bytes 589832 | tf_op jit(solution)/shard_map/while/body/eval_jaxpr/ppermute | solution.py:15
  685.1 17.3 %collective-permute-start = (bf16[128,12,64]{0,2,1:T(8,128)(2,1)}, bf16[128,12,64]{0,2,1:T(8,128)(2,1)S(1)}, u32[]{:S(2)}, u32[]{:S(2)}) collective-permute-start(bf16[128,12,64]{0,2,1:T(8,128)(2,1)} %get-tuple-element.1152), channel_id=1, source_target_pairs={{0,1},{1,2},{2,3},{3,4},{4,5},{5,6},{6,7},{7,0},{8,9},{9,10},{10,1... | collective-permute-start | bytes 589832 | tf_op jit(solution)/shard_map/while/body/eval_jaxpr/ppermute | solution.py:15
  685.2 18.2 %collective-permute-start.1 = (bf16[128,12,64]{0,2,1:T(8,128)(2,1)}, bf16[128,12,64]{0,2,1:T(8,128)(2,1)S(1)}, u32[]{:S(2)}, u32[]{:S(2)}) collective-permute-start(bf16[128,12,64]{0,2,1:T(8,128)(2,1)} %get-tuple-element.1153), channel_id=1, source_target_pairs={{0,1},{1,2},{2,3},{3,4},{4,5},{5,6},{6,7},{7,0},{8,9},{9,10},{10,1... | collective-permute-start | bytes 589832 | tf_op jit(solution)/shard_map/while/body/eval_jaxpr/ppermute | solution.py:15
  687.4 27.9 %collective-permute-start.2 = (bf16[128,12,64]{0,2,1:T(8,128)(2,1)}, bf16[128,12,64]{0,2,1:T(8,128)(2,1)}, u32[]{:S(2)}, u32[]{:S(2)}) collective-permute-start(bf16[128,12,64]{0,2,1:T(8,128)(2,1)} %get-tuple-element.1155), channel_id=1, source_target_pairs={{0,1},{1,2},{2,3},{3,4},{4,5},{5,6},{6,7},{7,0},{8,9},{9,10},{10,1... | collective-permute-start | bytes 589832 | tf_op jit(solution)/shard_map/while/body/eval_jaxpr/ppermute | solution.py:15
  693.4 24.1 %collective-permute-start.3 = (bf16[128,12,64]{0,2,1:T(8,128)(2,1)}, bf16[128,12,64]{0,2,1:T(8,128)(2,1)}, u32[]{:S(2)}, u32[]{:S(2)}) collective-permute-start(bf16[128,12,64]{0,2,1:T(8,128)(2,1)} %get-tuple-element.1156), channel_id=1, source_target_pairs={{0,1},{1,2},{2,3},{3,4},{4,5},{5,6},{6,7},{7,0},{8,9},{9,10},{10,1... | collective-permute-start | bytes 589832 | tf_op jit(solution)/shard_map/while/body/eval_jaxpr/ppermute | solution.py:15
  719.6 15.1 %collective-permute-start = (bf16[128,12,64]{0,2,1:T(8,128)(2,1)}, bf16[128,12,64]{0,2,1:T(8,128)(2,1)S(1)}, u32[]{:S(2)}, u32[]{:S(2)}) collective-permute-start(bf16[128,12,64]{0,2,1:T(8,128)(2,1)} %get-tuple-element.1152), channel_id=1, source_target_pairs={{0,1},{1,2},{2,3},{3,4},{4,5},{5,6},{6,7},{7,0},{8,9},{9,10},{10,1... | collective-permute-start | bytes 589832 | tf_op jit(solution)/shard_map/while/body/eval_jaxpr/ppermute | solution.py:15
  719.6 18.0 %collective-permute-start.1 = (bf16[128,12,64]{0,2,1:T(8,128)(2,1)}, bf16[128,12,64]{0,2,1:T(8,128)(2,1)S(1)}, u32[]{:S(2)}, u32[]{:S(2)}) collective-permute-start(bf16[128,12,64]{0,2,1:T(8,128)(2,1)} %get-tuple-element.1153), channel_id=1, source_target_pairs={{0,1},{1,2},{2,3},{3,4},{4,5},{5,6},{6,7},{7,0},{8,9},{9,10},{10,1... | collective-permute-start | bytes 589832 | tf_op jit(solution)/shard_map/while/body/eval_jaxpr/ppermute | solution.py:15
  722.9 26.7 %collective-permute-start.2 = (bf16[128,12,64]{0,2,1:T(8,128)(2,1)}, bf16[128,12,64]{0,2,1:T(8,128)(2,1)}, u32[]{:S(2)}, u32[]{:S(2)}) collective-permute-start(bf16[128,12,64]{0,2,1:T(8,128)(2,1)} %get-tuple-element.1155), channel_id=1, source_target_pairs={{0,1},{1,2},{2,3},{3,4},{4,5},{5,6},{6,7},{7,0},{8,9},{9,10},{10,1... | collective-permute-start | bytes 589832 | tf_op jit(solution)/shard_map/while/body/eval_jaxpr/ppermute | solution.py:15
  726.6 27.4 %collective-permute-start.3 = (bf16[128,12,64]{0,2,1:T(8,128)(2,1)}, bf16[128,12,64]{0,2,1:T(8,128)(2,1)}, u32[]{:S(2)}, u32[]{:S(2)}) collective-permute-start(bf16[128,12,64]{0,2,1:T(8,128)(2,1)} %get-tuple-element.1156), channel_id=1, source_target_pairs={{0,1},{1,2},{2,3},{3,4},{4,5},{5,6},{6,7},{7,0},{8,9},{9,10},{10,1... | collective-permute-start | bytes 589832 | tf_op jit(solution)/shard_map/while/body/eval_jaxpr/ppermute | solution.py:15
  756.0 31.4 %collective-permute-start = (bf16[128,12,64]{0,2,1:T(8,128)(2,1)}, bf16[128,12,64]{0,2,1:T(8,128)(2,1)S(1)}, u32[]{:S(2)}, u32[]{:S(2)}) collective-permute-start(bf16[128,12,64]{0,2,1:T(8,128)(2,1)} %get-tuple-element.1152), channel_id=1, source_target_pairs={{0,1},{1,2},{2,3},{3,4},{4,5},{5,6},{6,7},{7,0},{8,9},{9,10},{10,1... | collective-permute-start | bytes 589832 | tf_op jit(solution)/shard_map/while/body/eval_jaxpr/ppermute | solution.py:15
  756.0 31.8 %collective-permute-start.1 = (bf16[128,12,64]{0,2,1:T(8,128)(2,1)}, bf16[128,12,64]{0,2,1:T(8,128)(2,1)S(1)}, u32[]{:S(2)}, u32[]{:S(2)}) collective-permute-start(bf16[128,12,64]{0,2,1:T(8,128)(2,1)} %get-tuple-element.1153), channel_id=1, source_target_pairs={{0,1},{1,2},{2,3},{3,4},{4,5},{5,6},{6,7},{7,0},{8,9},{9,10},{10,1... | collective-permute-start | bytes 589832 | tf_op jit(solution)/shard_map/while/body/eval_jaxpr/ppermute | solution.py:15
  757.0 42.8 %collective-permute-start.2 = (bf16[128,12,64]{0,2,1:T(8,128)(2,1)}, bf16[128,12,64]{0,2,1:T(8,128)(2,1)}, u32[]{:S(2)}, u32[]{:S(2)}) collective-permute-start(bf16[128,12,64]{0,2,1:T(8,128)(2,1)} %get-tuple-element.1155), channel_id=1, source_target_pairs={{0,1},{1,2},{2,3},{3,4},{4,5},{5,6},{6,7},{7,0},{8,9},{9,10},{10,1... | collective-permute-start | bytes 589832 | tf_op jit(solution)/shard_map/while/body/eval_jaxpr/ppermute | solution.py:15
  779.0 23.0 %collective-permute-start.3 = (bf16[128,12,64]{0,2,1:T(8,128)(2,1)}, bf16[128,12,64]{0,2,1:T(8,128)(2,1)}, u32[]{:S(2)}, u32[]{:S(2)}) collective-permute-start(bf16[128,12,64]{0,2,1:T(8,128)(2,1)} %get-tuple-element.1156), channel_id=1, source_target_pairs={{0,1},{1,2},{2,3},{3,4},{4,5},{5,6},{6,7},{7,0},{8,9},{9,10},{10,1... | collective-permute-start | bytes 589832 | tf_op jit(solution)/shard_map/while/body/eval_jaxpr/ppermute | solution.py:15
  804.0 11.7 collective-permute-start.5
  818.6 528.0 %reduce-scatter.6.cloned.1.call-start = ((), (), s32[]{:S(2)}) async-start(), calls=%async_computation.15 | async-start | bytes 4866048 | tf_op jit(solution)/shard_map/reduce_scatter | solution.py:353
  818.7 35.9 %collective-permute-start.4 = (bf16[128,12,64]{0,2,1:T(8,128)(2,1)}, bf16[128,12,64]{0,2,1:T(8,128)(2,1)S(1)}, u32[]{:S(2)}, u32[]{:S(2)}) collective-permute-start(bf16[128,12,64]{0,2,1:T(8,128)(2,1)} %get-tuple-element.670), channel_id=1, source_target_pairs={{0,1},{1,2},{2,3},{3,4},{4,5},{5,6},{6,7},{7,0},{8,9},{9,10},{10,1... | collective-permute-start | bytes 589832 | tf_op jit(solution)/shard_map/ppermute | solution.py:15
  (85 other events, 1361.1 us)
Sparse Core Ops, SparseCore 0:
  11.0 56.6 all-gather.12
  70.7 56.2 all-gather.8
  129.8 42.1 all-gather.14
  174.6 42.6 all-gather.10
  220.1 54.0 all-gather.16
  276.3 77.3 all-gather.18
  355.8 78.0 all-gather.20
  468.0 364.5 all-reduce.14
  836.1 191.6 reduce-scatter.11
  1033.5 96.5 reduce-scatter.9
  1136.8 97.9 reduce-scatter.7
  1240.6 105.9 reduce-scatter.5
where the time goes:
time: 1380 us; the launch traced here: 1350 us
  waiting for transfers between devices  674 us (49%)
  local copies, waits for them, and re-layouts  238 us (17%)
  blocking collectives  161 us (12%)
  matrix products  123 us (9%)
  starting transfers between devices  119 us (9%)
  other arithmetic  21.2 us (2%)
  between operations  15.7 us (1%)
    reduce_scatter x1, waiting for transfers between devices, per_device(): lax.psum_scatter(grad_qk, ('exp', 'ctx'), scatter_dimension=0, tiled=True)  112 us
    reduce_scatter x1, waiting for transfers between devices, per_device(): lax.psum_scatter(grad_v, ('exp', 'ctx'), scatter_dimension=0, tiled=True)  105 us
    unnamed x2, blocking collectives  101 us
    reduce_scatter x1, waiting for transfers between devices, per_device(): lax.psum_scatter(grad_o, ('exp', 'ctx'), scatter_dimension=0, tiled=True)  97.6 us
    reduce_scatter x1, waiting for transfers between devices, per_device(): lax.psum_scatter(grad_outer, 'ctx', scatter_dimension=0, tiled=True)  97 us
    ppermute x30, starting transfers between devices, from_behind(): return lax.ppermute(value, axis, pairs)  87.7 us
    all_gather x1, waiting for transfers between devices, per_device(): lax.all_gather(w_out, 'ctx', axis=0, tiled=True)  76.9 us
    ppermute x30, waiting for transfers between devices, from_behind(): return lax.ppermute(value, axis, pairs)  68.1 us
  transfers between devices with their start and end apart: 46, of which 22 were waited for; matrix products, arithmetic and copies ran while one was open for 25% of the time, Pallas kernels for 0%

commit v1 on v0

v1 whole, which is shorter than its diff:
```python
import functools
import math

import jax
import jax.numpy as jnp
import numpy as np
from jax import lax
from jax.experimental import pallas as pl
from jax.experimental.pallas import tpu as pltpu
from jax.sharding import Mesh
from jax.sharding import PartitionSpec as P

EPS = 1e-06
F32 = jnp.float32
BF16 = jnp.bfloat16
EVERY = ("exp", "major", "minor")
VMEM_BYTES = 56 * 1024 * 1024


def bucket_edges(reach):
    magnitude = np.arange(reach)
    spread = 8 + (np.log(np.maximum(magnitude, 1) / 8.0) / np.log(16.0) * 8.0).astype(np.int64)
    bucket = np.where(magnitude < 8, magnitude, np.minimum(spread, 15))
    return [int(np.argmax(bucket >= number)) for number in range(16)]


def dot_t(left, right):
    return lax.dot_general(left, right, (((1,), (1,)), ((), ())), preferred_element_type=F32)


def dot_0(left, right):
    return lax.dot_general(left, right, (((0,), (0,)), ((), ())), preferred_element_type=F32)


def dot_n(left, right):
    return jnp.dot(left, right, preferred_element_type=F32)


def near_bias_kernel(edges, rows, table_ref, out_ref):
    shape = (3 * rows, rows)
    relative = (
        lax.broadcasted_iota(jnp.int32, shape, 0) - rows - lax.broadcasted_iota(jnp.int32, shape, 1)
    )
    magnitude = jnp.abs(relative)
    ahead = relative > 0
    for head in range(out_ref.shape[0]):
        value = jnp.where(ahead, table_ref[16, head], table_ref[0, head])
        for number in range(1, 16):
            value = jnp.where(
                magnitude >= edges[number],
                jnp.where(ahead, table_ref[16 + number, head], table_ref[number, head]),
                value,
            )
        out_ref[head] = value


def bucket_sum_kernel(edges, rows, near_ref, far_ref, out_ref):
    shape = (3 * rows, rows)
    relative = (
        lax.broadcasted_iota(jnp.int32, shape, 0) - rows - lax.broadcasted_iota(jnp.int32, shape, 1)
    )
    magnitude = jnp.abs(relative)
    lanes = lax.broadcasted_iota(jnp.int32, (1, 128), 1)
    for head in range(near_ref.shape[0]):
        grads = near_ref[head]
        behind = jnp.where(relative > 0, 0.0, grads)
        forward = jnp.where(relative > 0, grads, 0.0)
        total = jnp.zeros((1, 128), F32)
        for side, part in enumerate((behind, forward)):
            for number in range(16):
                inside = magnitude >= edges[number]
                if number < 15:
                    inside = inside & (magnitude < edges[number + 1])
                value = jnp.sum(jnp.sum(jnp.where(inside, part, 0.0), axis=0, keepdims=True))
                if number == 15:
                    value = value + jnp.sum(far_ref[head, side : side + 1, :])
                total = jnp.where(lanes == side * 16 + number, value, total)
        out_ref[head : head + 1, :] = total


def biased_scores(raw, far_ref, near_ref, scratch, head, block, rows):
    count = raw.shape[0]
    place = lax.broadcasted_iota(jnp.int32, raw.shape, 0)
    low, high = (block - 1) * rows, (block + 2) * rows
    far = jnp.where(
        place < low, far_ref[0, head], jnp.where(place >= high, far_ref[1, head], 0.0)
    )
    scratch[pl.ds(rows, count), :] = raw + far
    window = pl.ds(pl.multiple_of(block * rows, rows), 3 * rows)
    scratch[window, :] = scratch[window, :] + near_ref[head]
    return scratch[pl.ds(rows, count), :]


def attention_kernel(heads, rows, block_ref, far_ref, q_ref, kv_ref, near_ref, out_ref, lse_ref, scratch):
    block = block_ref[pl.program_id(0)]
    for head in range(heads):
        lanes = slice(head * 128, (head + 1) * 128)
        kv = kv_ref[:, lanes]
        scores = biased_scores(
            dot_t(kv, q_ref[:, lanes]), far_ref, near_ref, scratch.at[head % scratch.shape[0]], head, block, rows
        )
        top = jnp.max(scores, axis=0, keepdims=True)
        weights = jnp.exp(scores - top)
        total = jnp.sum(weights, axis=0, keepdims=True)
        low = (weights * (1.0 / total)).astype(BF16)
        out_ref[:, lanes] = dot_0(low, kv)
        lse_ref[0, head : head + 1, :] = top + jnp.log(total)


def attention_back_kernel(
    heads,
    rows,
    block_ref,
    far_ref,
    q_ref,
    g_ref,
    kv_ref,
    near_ref,
    lse_ref,
    delta_ref,
    dq_ref,
    dkv_ref,
    near_sum_ref,
    far_sum_ref,
    scratch,
    pad_scratch,
):
    step = pl.program_id(0)
    block = block_ref[step]
    count = kv_ref.shape[0]

    @pl.when(step == 0)
    def _():
        dkv_ref[...] = jnp.zeros_like(dkv_ref)
        near_sum_ref[...] = jnp.zeros_like(near_sum_ref)
        far_sum_ref[...] = jnp.zeros_like(far_sum_ref)
        for slot in range(pad_scratch.shape[0]):
            pad_scratch[slot, pl.ds(0, rows), :] = jnp.zeros((rows, rows), F32)
            pad_scratch[slot, pl.ds(rows + count, rows), :] = jnp.zeros((rows, rows), F32)

    place = lax.broadcasted_iota(jnp.int32, (count, rows), 0)
    low, high = (block - 1) * rows, (block + 2) * rows
    window = pl.ds(pl.multiple_of(block * rows, rows), 3 * rows)
    for head in range(heads):
        lanes = slice(head * 128, (head + 1) * 128)
        kv = kv_ref[:, lanes]
        both = jnp.concatenate([q_ref[:, lanes], g_ref[:, lanes]], axis=0)
        products = dot_t(kv, both)
        scores = biased_scores(
            products[:, :rows], far_ref, near_ref, scratch.at[head % scratch.shape[0]], head, block, rows
        )
        chances = jnp.exp(scores - lse_ref[0, head : head + 1, :])
        grads = chances * (products[:, rows:] - delta_ref[0, head : head + 1, :])
        grads_low = grads.astype(BF16)
        slot = head % pad_scratch.shape[0]
        pad_scratch[slot, pl.ds(rows, count), :] = grads
        near_sum_ref[head] += pad_scratch[slot, window, :]
        far_sum_ref[head, 0:1, :] += jnp.sum(jnp.where(place < low, grads, 0.0), axis=0, keepdims=True)
        far_sum_ref[head, 1:2, :] += jnp.sum(jnp.where(place >= high, grads, 0.0), axis=0, keepdims=True)
        pair = jnp.concatenate([grads_low, chances.astype(BF16)], axis=1)
        dkv_ref[:, lanes] += dot_n(pair, both)
        dq_ref[:, lanes] = dot_0(grads_low, kv).astype(BF16)


def whole_block(shape):
    zeros = (0,) * len(shape)
    return pl.BlockSpec(shape, lambda *_: zeros)


def scalars():
    return pl.BlockSpec(memory_space=pltpu.SMEM)


def slot_count(heads, count):
    return heads if count <= 2048 else 1


def forward_attention(queries, keys_values, near, far, blocks, heads, rows):
    count = keys_values.shape[0]
    steps = blocks.shape[0]
    width = heads * 128
    return pl.pallas_call(
        functools.partial(attention_kernel, heads, rows),
        grid=(steps,),
        in_specs=[
            scalars(),
            scalars(),
            pl.BlockSpec((rows, width), lambda i: (i, 0)),
            whole_block((count, width)),
            whole_block(near.shape),
        ],
        out_specs=[
            pl.BlockSpec((rows, width), lambda i: (i, 0)),
            pl.BlockSpec((1, heads, rows), lambda i: (i, 0, 0)),
        ],
        out_shape=[
            jax.ShapeDtypeStruct((steps * rows, width), F32),
            jax.ShapeDtypeStruct((steps, heads, rows), F32),
        ],
        scratch_shapes=[pltpu.VMEM((slot_count(heads, count), count + 2 * rows, rows), F32)],
        compiler_params=pltpu.CompilerParams(vmem_limit_bytes=VMEM_BYTES),
        cost_estimate=pl.CostEstimate(
            flops=4 * steps * rows * count * width, bytes_accessed=8 * count * width, transcendentals=steps * rows * count * heads
        ),
    )(blocks, far, queries, keys_values, near)


def backward_attention(queries, grads, keys_values, near, far, blocks, lse, delta, heads, rows):
    count = keys_values.shape[0]
    steps = blocks.shape[0]
    width = heads * 128
    row_spec = pl.BlockSpec((1, heads, rows), lambda i: (i, 0, 0))
    return pl.pallas_call(
        functools.partial(attention_back_kernel, heads, rows),
        grid=(steps,),
        in_specs=[
            scalars(),
            scalars(),
            pl.BlockSpec((rows, width), lambda i: (i, 0)),
            pl.BlockSpec((rows, width), lambda i: (i, 0)),
            whole_block((count, width)),
            whole_block(near.shape),
            row_spec,
            row_spec,
        ],
        out_specs=[
            pl.BlockSpec((rows, width), lambda i: (i, 0)),
            whole_block((count, width)),
            whole_block(near.shape),
            whole_block((heads, 2, rows)),
        ],
        out_shape=[
            jax.ShapeDtypeStruct((steps * rows, width), BF16),
            jax.ShapeDtypeStruct((count, width), F32),
            jax.ShapeDtypeStruct(near.shape, F32),
            jax.ShapeDtypeStruct((heads, 2, rows), F32),
        ],
        scratch_shapes=[
            pltpu.VMEM((slot_count(heads, count), count + 2 * rows, rows), F32),
            pltpu.VMEM((slot_count(heads, count), count + 2 * rows, rows), F32),
        ],
        compiler_params=pltpu.CompilerParams(vmem_limit_bytes=VMEM_BYTES),
        cost_estimate=pl.CostEstimate(
            flops=10 * steps * rows * count * width, bytes_accessed=8 * count * width, transcendentals=steps * rows * count * heads
        ),
    )(blocks, far, queries, grads, keys_values, near, lse, delta)


def swap_pairs():
    return [(0, 1), (1, 0)]


def gather_minor(value):
    count = lax.axis_size("minor")
    if count != 2:
        return lax.all_gather(value, "minor")
    other = lax.ppermute(value, "minor", swap_pairs())
    first = lax.axis_index("minor") == 0
    return jnp.stack([jnp.where(first, value, other), jnp.where(first, other, value)])


def sum_minor(parts):
    count = lax.axis_size("minor")
    if count != 2:
        arrived = lax.all_to_all(parts.astype(BF16), "minor", 0, 0, tiled=True)
        return jnp.sum(arrived.astype(F32), axis=0)
    first = lax.axis_index("minor") == 0
    sent = jnp.where(first, parts[1], parts[0]).astype(BF16)
    return jnp.where(first, parts[0], parts[1]) + lax.ppermute(sent, "minor", swap_pairs()).astype(F32)


def swap_major(value):
    return lax.all_to_all(value, "major", 0, 0, tiled=True)


def unit(hidden):
    return lax.rsqrt(jnp.mean(hidden * hidden, axis=-1, keepdims=True) + EPS)


def per_device(
    activations,
    cotangent,
    query_key_weight,
    value_weight,
    output_weight,
    norm_first,
    norm_second,
    router_weight,
    bias_table,
    w_in,
    w_out,
    routes,
    slots,
):
    rows, width = activations.shape[1:]
    major = lax.axis_size("major")
    minor = lax.axis_size("minor")
    groups = lax.axis_size("exp")
    devices = groups * major * minor
    experts = router_weight.shape[1]
    capacity = rows * 5 // (4 * experts)
    head_count = bias_table.shape[1]
    heads = head_count // major
    features = value_weight.shape[1]
    head_dim = features // head_count
    shard = query_key_weight.shape[0]
    my_major = lax.axis_index("major")
    my_minor = lax.axis_index("minor")
    my_exp = lax.axis_index("exp")
    edges = bucket_edges(4 * rows)
    kv_width = heads * 2 * head_dim
    q_width = heads * head_dim
    extra_width = 128 - (kv_width + q_width) % 128
    packed_width = kv_width + q_width + extra_width

    column = swap_major(jnp.broadcast_to(activations, (major, rows, width)))

    def by_head(value):
        return value.reshape(shard, major, heads, 1, head_dim)

    key_value = jnp.concatenate(
        [by_head(query_key_weight[:, features:]), by_head(value_weight)], axis=3
    ).reshape(shard, major, kv_width)
    extras = jnp.concatenate([router_weight, norm_first[:, None], norm_second[:, None]], axis=1)
    extras = jnp.pad(extras, ((0, 0), (0, extra_width - experts - 2)))
    packed = jnp.concatenate(
        [
            key_value,
            query_key_weight[:, :features].reshape(shard, major, q_width),
            jnp.broadcast_to(extras[:, None, :], (shard, major, extra_width)),
        ],
        axis=2,
    )
    packed = swap_major(jnp.transpose(packed, (1, 0, 2)))
    packed = gather_minor(packed)
    packed = lax.all_gather(packed, "exp")
    packed = jnp.transpose(packed, (0, 2, 1, 3, 4)).reshape(width, packed_width)
    extras = packed[:, kv_width + q_width :]
    full_router = extras[:, :experts]
    gain_first = extras[:, experts].astype(F32)
    gain_second = extras[:, experts + 1].astype(F32)
    head_weight = packed[:, : kv_width + q_width]

    full_o = lax.all_gather(output_weight, EVERY, axis=0, tiled=True)

    table = lax.dynamic_slice_in_dim(bias_table, my_major * heads, heads, axis=1).astype(F32)
    near = pl.pallas_call(
        functools.partial(near_bias_kernel, edges, rows),
        in_specs=[scalars()],
        out_shape=jax.ShapeDtypeStruct((heads, 3 * rows, rows), F32),
    )(table)
    far = jnp.stack([table[15], table[31]])
    blocks = jnp.arange(major, dtype=jnp.int32) * minor + my_minor

    quarter = w_in.shape[2] // major
    inner = swap_major(jnp.transpose(w_in.reshape(w_in.shape[0], major, quarter), (1, 0, 2)))
    outer = w_out[:, 0, :]
    both = gather_minor(jnp.concatenate([inner.reshape(-1, width), outer], axis=0))
    inner = both[:, : width // minor].reshape(minor, major, width // devices * groups, quarter)
    inner = jnp.transpose(inner, (1, 0, 2, 3)).reshape(width, quarter)
    outer = both[:, width // minor :].reshape(quarter, width)

    expert_ids = jnp.arange(experts, dtype=jnp.int32)
    slot_ids = jnp.arange(capacity, dtype=jnp.int32)
    select = (
        (routes[0][None, None, :] == expert_ids[:, None, None])
        & (slots[0][None, None, :] == slot_ids[None, :, None])
    ).astype(BF16)
    select = select.reshape(experts * capacity, rows)

    def dispatch(value):
        sent = dot_n(select, value).astype(BF16).reshape(groups, 1, capacity, width)
        sent = jnp.broadcast_to(sent, (groups, major, capacity, width))
        sent = sent.reshape(groups * major, capacity, width)
        arrived = lax.all_to_all(sent, ("exp", "major"), 0, 0, tiled=True)
        return arrived.reshape(groups * major * capacity, width)

    def give_back(value):
        arrived = lax.all_to_all(
            value.astype(BF16).reshape(groups * major, capacity, width), ("exp", "major"), 0, 0, tiled=True
        )
        arrived = jnp.sum(arrived.reshape(groups, major, capacity, width).astype(F32), axis=1)
        return dot_0(select, arrived.astype(BF16).reshape(experts * capacity, width))

    sent = dot_n(select, cotangent[0]).astype(BF16).reshape(groups, capacity, width)
    sent = lax.all_to_all(sent, "exp", 0, 0, tiled=True)
    cot_rows = lax.all_gather(sent, "major", axis=1).reshape(groups * major * capacity, width)

    column_hidden = column.reshape(major * rows, width).astype(F32)
    column_unit = unit(column_hidden)
    normed = (column_hidden * column_unit * gain_first).astype(BF16)
    projected = dot_n(normed, head_weight).astype(BF16)
    kv_own = projected[:, :kv_width].reshape(major, rows, kv_width)
    keys_values = jnp.transpose(gather_minor(kv_own), (1, 0, 2, 3)).reshape(-1, kv_width)
    queries = projected[:, kv_width:].reshape(major * rows, heads, head_dim)
    queries = jnp.pad(queries, ((0, 0), (0, 0), (0, head_dim))).reshape(major * rows, kv_width)
    attended_wide, lse = forward_attention(queries, keys_values, near, far, blocks, heads, rows)
    attended_heads = attended_wide.reshape(major * rows, heads, 2, head_dim)[:, :, 1, :]
    attended = swap_major(attended_heads.astype(BF16).reshape(major, rows, q_width))
    attended = jnp.transpose(attended, (1, 0, 2)).reshape(rows, features)

    hidden = activations[0].astype(F32)
    middle = hidden + dot_n(attended, full_o)
    middle_unit = unit(middle)
    mixed = (middle * middle_unit * gain_second).astype(BF16)
    chances = jax.nn.softmax(dot_n(mixed, full_router), axis=-1)
    route_mask = (routes[0][:, None] == expert_ids[None, :]).astype(F32)
    gate = jnp.sum(chances * route_mask, axis=-1, keepdims=True)

    buffer = dispatch(mixed)
    row_chances = jax.nn.softmax(dot_n(buffer, full_router), axis=-1)
    row_mask = (expert_ids == my_exp).astype(F32)[None, :]
    row_gate = jnp.sum(row_chances * row_mask, axis=-1, keepdims=True)
    preact = dot_n(buffer, inner)
    cumulative = 0.5 * (1.0 + lax.erf(preact * math.sqrt(0.5)))
    density = jnp.exp(-0.5 * preact * preact) * (1.0 / math.sqrt(2.0 * math.pi))
    activated_wide = preact * cumulative
    grad_activated = dot_t(cot_rows, outer)
    grad_preact = (row_gate * grad_activated * (cumulative + preact * density)).astype(BF16)
    row_grad_gate = jnp.sum(activated_wide * grad_activated, axis=-1, keepdims=True)
    grad_logits = (row_gate * row_grad_gate * (row_mask - row_chances)).astype(BF16)
    grad_mixed = give_back(dot_t(grad_preact, inner) + dot_t(grad_logits, full_router))

    activated = activated_wide.astype(BF16)
    produced = give_back(dot_n(activated, outer))
    layer_output = (middle + gate * produced).astype(BF16)[None]
    grad_router = dot_0(buffer, grad_logits)
    gated_rows = (row_gate * cot_rows.astype(F32)).astype(BF16)
    grad_outer = dot_0(activated, gated_rows).reshape(minor, -1, width)
    grad_inner = dot_0(buffer, grad_preact).reshape(major, minor, -1, quarter)
    grad_inner = jnp.transpose(grad_inner, (1, 0, 2, 3)).reshape(minor, -1, quarter)
    grad_both = sum_minor(jnp.concatenate([grad_inner, grad_outer], axis=1))
    grad_outer = grad_both[width // minor :][:, None, :]
    grad_inner = swap_major(grad_both[: width // minor].astype(BF16).reshape(major, -1, quarter))
    grad_inner = jnp.transpose(grad_inner, (1, 0, 2)).reshape(-1, 1, major * quarter).astype(F32)

    grad_z = cotangent[0].astype(F32)
    grad_gain_second = jnp.sum(grad_mixed * middle * middle_unit, axis=0)
    scaled = grad_mixed * gain_second
    grad_middle = (
        grad_z
        + middle_unit * scaled
        - middle * middle_unit**3 * jnp.mean(scaled * middle, axis=-1, keepdims=True)
    )
    grad_branch = grad_middle.astype(BF16)
    grad_attended = dot_t(grad_branch, full_o).astype(BF16)
    grad_attended = swap_major(
        jnp.transpose(grad_attended.reshape(rows, major, q_width), (1, 0, 2))
    ).reshape(major * rows, heads, head_dim)
    grad_o = dot_0(attended, grad_branch).astype(BF16).reshape(devices, shard, width)
    grad_o = jnp.sum(lax.all_to_all(grad_o, EVERY, 0, 0, tiled=True).astype(F32), axis=0)

    delta = jnp.sum(grad_attended.astype(F32) * attended_heads, axis=-1)
    delta = jnp.transpose(delta.reshape(major, rows, heads), (0, 2, 1))
    grad_wide = jnp.pad(grad_attended, ((0, 0), (0, 0), (head_dim, 0))).reshape(-1, kv_width)
    dq_wide, dkv, near_sum, far_sum = backward_attention(
        queries, grad_wide, keys_values, near, far, blocks, lse, delta, heads, rows
    )
    sums = pl.pallas_call(
        functools.partial(bucket_sum_kernel, edges, rows),
        out_shape=jax.ShapeDtypeStruct((heads, 128), F32),
    )(near_sum, far_sum)
    grad_table = sums[:, :32].T
    dkv = jnp.transpose(dkv.reshape(major, minor, rows, kv_width), (1, 0, 2, 3))
    dkv = sum_minor(dkv).reshape(major * rows, kv_width).astype(BF16)
    dq = dq_wide.reshape(major * rows, heads, 2, head_dim)[:, :, 0, :].reshape(-1, q_width)
    grad_projected = jnp.concatenate([dkv, dq], axis=1)

    grad_normed = dot_t(grad_projected, head_weight)
    grad_gain_first = jnp.sum(grad_normed * column_hidden * column_unit, axis=0)
    grad_normed = swap_major(grad_normed.astype(BF16).reshape(major, rows, width))
    grad_normed = jnp.sum(grad_normed.astype(F32), axis=0)
    hidden_unit = unit(hidden)
    scaled = grad_normed * gain_first
    grad_activations = (
        grad_middle
        + hidden_unit * scaled
        - hidden * hidden_unit**3 * jnp.mean(scaled * hidden, axis=-1, keepdims=True)
    ).astype(BF16)[None]

    grad_weight = dot_0(normed, grad_projected).astype(BF16).reshape(devices, shard, -1)
    small = jnp.concatenate(
        [grad_router, grad_gain_first[:, None], grad_gain_second[:, None]], axis=1
    ).reshape(devices, shard, experts + 2)
    buckets = bias_table.shape[0]
    table_columns = buckets * heads // shard
    flat_table = jnp.broadcast_to(
        grad_table.reshape(1, shard, table_columns), (devices, shard, table_columns)
    )
    spare = extra_width - experts - 2 - table_columns
    sent = jnp.concatenate(
        [
            grad_weight,
            small.astype(BF16),
            flat_table.astype(BF16),
            jnp.zeros((devices, shard, spare), BF16),
        ],
        axis=2,
    )
    arrived = lax.all_to_all(sent, EVERY, 0, 0, tiled=True).astype(F32)
    arrived = jnp.sum(arrived.reshape(groups, major, minor, shard, packed_width), axis=(0, 2))
    key_value = arrived[:, :, :kv_width].reshape(major, shard, heads, 2, head_dim)

    def side_by_side(value):
        return jnp.transpose(value.reshape(major, shard, q_width), (1, 0, 2)).reshape(shard, features)

    grad_query = side_by_side(arrived[:, :, kv_width : kv_width + q_width])
    grad_key = side_by_side(key_value[:, :, :, 0, :])
    grad_v = side_by_side(key_value[:, :, :, 1, :])
    small = arrived[:, :, kv_width + q_width :]
    summed = jnp.sum(small[:, :, : experts + 2], axis=0)
    grad_table = small[:, :, experts + 2 : experts + 2 + table_columns]
    grad_table = jnp.transpose(grad_table.reshape(major, buckets, heads), (1, 0, 2))
    return (
        layer_output,
        grad_activations,
        jnp.concatenate([grad_query, grad_key], axis=1),
        grad_v,
        grad_o,
        summed[:, experts],
        summed[:, experts + 1],
        summed[:, :experts],
        grad_table.reshape(buckets, head_count),
        grad_inner,
        grad_outer,
    )


def solution(mesh):
    groups, ring = mesh.shape["exp"], mesh.shape["ctx"]
    major = math.gcd(ring, 4)
    split = Mesh(mesh.devices.reshape(groups, major, ring // major), EVERY)
    ctx = ("major", "minor")
    tokens, rows, experts = P("exp", ctx, None), P(EVERY, None), P(ctx, "exp", None)
    return jax.shard_map(
        per_device,
        mesh=split,
        in_specs=(
            tokens,
            tokens,
            rows,
            rows,
            rows,
            P(EVERY),
            P(EVERY),
            rows,
            P(),
            experts,
            experts,
            P("exp", ctx),
            P("exp", ctx),
        ),
        out_specs=(
            tokens,
            tokens,
            rows,
            rows,
            rows,
            P(EVERY),
            P(EVERY),
            rows,
            P(),
            experts,
            experts,
        ),
        check_vma=False,
    )
```

time: 1380 us -> 380 us (0.28); the launches traced: 1350 us -> 377 us
  waiting for transfers between devices: 674 us -> 106 us
  local copies, waits for them, and re-layouts: 238 us -> 48.5 us
  blocking collectives: 161 us -> 49.7 us
  matrix products: 123 us -> 35.1 us
  starting transfers between devices: 119 us -> 64.3 us
  Pallas kernels: 0 us -> 27.4 us
    reduce_scatter x4 -> x0, waiting for transfers between devices: 411 us -> none  [the longest x1 112 us: per_device(): lax.psum_scatter(grad_qk, ('exp', 'ctx'), scatter_dimension=0, tiled=True)]
    all_gather x7 -> x1, waiting for transfers between devices: 187 us -> 0.01 us  [per_device(): full_o = lax.all_gather(output_weight, EVERY, axis=0, tiled=True)]
    unnamed x2 -> x0, blocking collectives: 101 us -> none
    all_to_all x4 -> x13, waiting for transfers between devices: 4.15 us -> 93.5 us  [the longest x7 47.1 us: swap_major(): return lax.all_to_all(value, 'major', 0, 0, tiled=True)]
    dot_general x84 -> x20, matrix products: 123 us -> 35.1 us  [the longest x7 14.3 us: dot_0(): lax.dot_general(left, right, (((0,), (0,)), ((), ())), preferred_element_...]
    ppermute x30 -> x5, starting transfers between devices: 87.7 us -> 5.17 us  [the longest x3 3.71 us: gather_minor(): other = lax.ppermute(value, 'minor', swap_pairs())]
    rev x18 -> x0, local copies, waits for them, and re-layouts: 56.5 us -> none  [the longest x10 53.9 us: spread_offsets(): return sheared[:, ::-1, :]]
    ppermute x30 -> x5, waiting for transfers between devices: 68.1 us -> 11.8 us  [the longest x3 9.35 us: gather_minor(): other = lax.ppermute(value, 'minor', swap_pairs())]
  transfers between devices with their start and end apart: 46 -> 19, of which waited for: 22 -> 12; matrix products, arithmetic and copies ran while one was open for 25% -> 22% of each run, Pallas kernels for 0% -> 7%
where the time goes in v1:
time: 380 us; the launch traced here: 377 us
  waiting for transfers between devices  106 us (28%)
  starting transfers between devices  64.3 us (17%)
  blocking collectives  49.7 us (13%)
  local copies, waits for them, and re-layouts  48.5 us (13%)
  matrix products  35.1 us (9%)
  other arithmetic  30.8 us (8%)
  Pallas kernels  27.4 us (7%)
  between operations  15.1 us (4%)
    all_to_all x7, waiting for transfers between devices, swap_major(): return lax.all_to_all(value, 'major', 0, 0, tiled=True)  47.1 us
    all_gather x1, blocking collectives, per_device(): lax.all_gather(sent, 'major', axis=1)  37 us
    all_to_all x7, starting transfers between devices, swap_major(): return lax.all_to_all(value, 'major', 0, 0, tiled=True)  28.4 us
    all_to_all x2, waiting for transfers between devices, give_back(): lax.all_to_all(value.astype(BF16).reshape(groups * major, capacity, width...  19.7 us
    all_to_all x1, waiting for transfers between devices, per_device(): arrived = lax.all_to_all(sent, EVERY, 0, 0, tiled=True).astype(F32)  14.5 us
    dot_general x7, matrix products, dot_0(): lax.dot_general(left, right, (((0,), (0,)), ((), ())), preferred_element_...  14.3 us
    pallas_call x1, Pallas kernels, backward_attention(): pl.pallas_call(functools.partial(attention_back_kernel, heads, rows), gri...  12.8 us
    all_gather x1, blocking collectives, per_device(): packed = lax.all_gather(packed, 'exp')  12.7 us
  transfers between devices with their start and end apart: 19, of which 12 were waited for; matrix products, arithmetic and copies ran while one was open for 22% of the time, Pallas kernels for 7%

profile of v1, /device:TPU:1, one launch (start us, length us, event | category | flops | bytes accessed | tf_op | source)
XLA Modules:
  0.0 376.8 jit_solution(13342117547363507213)
XLA Ops:
  11.4 5.4 %all-to-all-start.1 = ((bf16[4,24,640]{2,1,0:T(8,128)(2,1)}), bf16[4,24,640]{2,1,0:T(8,128)(2,1)S(1)}, u32[]{:S(2)}, u32[]{:S(2)}) async-start(bf16[4,24,640]{2,1,0:T(8,128)(2,1)} %maximum_bitcast_fusion), calls=%async_computation.1 | async-start | bytes 245760 | tf_op jit(solution)/shard_map/all_to_all | solution.py:273
  17.6 4.0 %all-to-all-done.1 = bf16[4,24,640]{2,1,0:T(8,128)(2,1)S(1)} async-done(((bf16[4,24,640]{2,1,0:T(8,128)(2,1)}), bf16[4,24,640]{2,1,0:T(8,128)(2,1)S(1)}, u32[]{:S(2)}, u32[]{:S(2)}) %all-to-all-start.1) | async-done | bytes 122912 | tf_op jit(solution)/shard_map/all_to_all | solution.py:273
  22.5 3.5 all-to-all-start
  26.8 2.3 shard_map.215.near_ref
  31.2 1.9 collective-permute-done
  33.2 12.7 %all-gather = bf16[8,4,24,640]{3,2,1,0:T(8,128)(2,1)S(1)} all-gather(bf16[2,4,24,640]{3,2,1,0:T(8,128)(2,1)S(1)} %pad_maximum_fusion.7), channel_id=2, replica_groups=mesh['exp'=4,'major'=4,'minor'=2] {'exp'}, dimensions={0}, use_global_device_ids=true | all-gather | bytes 1228800 | tf_op jit(solution)/shard_map/all_gather | solution.py:336
  46.3 4.8 %all-to-all-start.6 = ((bf16[4,40,768]{2,1,0:T(8,128)(2,1)}), bf16[4,40,768]{2,1,0:T(8,128)(2,1)S(1)}, u32[]{:S(2)}, u32[]{:S(2)}) async-start(bf16[4,40,768]{2,1,0:T(8,128)(2,1)} %bitcast.41), calls=%async_computation.6 | async-start | bytes 491520 | tf_op jit(solution)/shard_map/all_to_all | solution.py:386
  56.2 7.4 %collective-permute-done.1 = bf16[4,128,384]{2,1,0:T(8,128)(2,1)S(1)} collective-permute-done((bf16[4,128,384]{2,1,0:T(8,128)(2,1)S(1)}, bf16[4,128,384]{2,1,0:T(8,128)(2,1)S(1)}, u32[]{:S(2)}, u32[]{:S(2)}) %collective-permute-start.1) | collective-permute-done | bytes 393248 | tf_op jit(solution)/shard_map/ppermute | solution.py:257
  64.8 9.1 %shard_map.216 = (f32[512,384]{1,0:T(8,128)}, f32[4,3,128]{2,1,0:T(4,128)}) custom-call(s32[4]{0:T(128)} %multiply_add_fusion.block_ref, f32[2,3]{1,0:T(2,128)} %pad_maximum_fusion.11.far_ref, bf16[512,384]{1,0:T(8,128)(2,1)} %copy.179.q_ref, bf16[1024,384]{1,0:T(8,128)(2,1)} %bitcast.269, f32[3,384,128]{2,1,0:T(8,128)} %shard_map.215.near_ref), custom_call_target="tpu_custom_call" | custom-call | flops 805306368 | bytes 3145728 | tf_op jit(solution)/shard_map/pallas_call | solution.py:182
  77.0 3.4 all-to-all-start.2
  81.7 3.9 %all-to-all-done.2 = bf16[4,128,192]{1,2,0:T(8,128)(2,1)S(1)} async-done(((bf16[4,128,192]{1,2,0:T(8,128)(2,1)}), bf16[4,128,192]{1,2,0:T(8,128)(2,1)S(1)}, u32[]{:S(2)}, u32[]{:S(2)}) %all-to-all-start.2) | async-done | bytes 196640 | tf_op jit(solution)/shard_map/all_to_all | solution.py:273
  85.5 4.4 %all-to-all-start.4 = ((bf16[4,96,768]{2,1,0:T(8,128)(2,1)}), bf16[4,96,768]{2,1,0:T(8,128)(2,1)S(1)}, u32[]{:S(2)}, u32[]{:S(2)}) async-start(bf16[4,96,768]{2,1,0:T(8,128)(2,1)} %bitcast.223), calls=%async_computation.4 | async-start | bytes 1179648 | tf_op jit(solution)/shard_map/all_to_all | solution.py:273
  92.5 12.7 %all-to-all-done.4 = bf16[4,96,768]{2,1,0:T(8,128)(2,1)S(1)} async-done(((bf16[4,96,768]{2,1,0:T(8,128)(2,1)}), bf16[4,96,768]{2,1,0:T(8,128)(2,1)S(1)}, u32[]{:S(2)}, u32[]{:S(2)}) %all-to-all-start.4) | async-done | bytes 589856 | tf_op jit(solution)/shard_map/all_to_all | solution.py:273
  106.1 5.1 %all-to-all-start.3 = ((bf16[16,40,768]{2,1,0:T(8,128)(2,1)}), bf16[16,40,768]{2,1,0:T(8,128)(2,1)S(1)}, u32[]{:S(2)}, u32[]{:S(2)}) async-start(bf16[16,40,768]{2,1,0:T(8,128)(2,1)} %bitcast.244), calls=%async_computation.3 | async-start | bytes 1966080 | tf_op jit(solution)/shard_map/all_to_all | solution.py:375
  113.6 37.0 %all-gather.1 = bf16[4,160,768]{2,1,0:T(8,128)(2,1)} all-gather(bf16[4,40,768]{2,1,0:T(8,128)(2,1)} %copy-done.27), channel_id=3, replica_groups=mesh['exp'=4,'major'=4,'minor'=2] {'major'}, dimensions={1}, use_global_device_ids=true | all-gather | bytes 1228800 | tf_op jit(solution)/shard_map/all_gather | solution.py:387
  155.0 2.0 fusion.11
  159.7 2.5 add_convert_fusion
  162.2 6.4 %all-to-all-start.7 = ((bf16[16,40,768]{2,1,0:T(8,128)(2,1)}), bf16[16,40,768]{2,1,0:T(8,128)(2,1)}, u32[]{:S(2)}, u32[]{:S(2)}) async-start(bf16[16,40,768]{2,1,0:T(8,128)(2,1)} %bitcast.43), calls=%async_computation.7 | async-start | bytes 1966080 | tf_op jit(solution)/shard_map/all_to_all | solution.py:379
  170.2 3.7 convolution_bitcast_fusion
  173.9 19.6 %all-to-all-done.7 = bf16[16,40,768]{2,1,0:T(8,128)(2,1)} async-done(((bf16[16,40,768]{2,1,0:T(8,128)(2,1)}), bf16[16,40,768]{2,1,0:T(8,128)(2,1)}, u32[]{:S(2)}, u32[]{:S(2)}) %all-to-all-start.7) | async-done | bytes 983072 | tf_op jit(solution)/shard_map/all_to_all | solution.py:379
  200.4 4.0 %all-to-all-start.8 = ((bf16[4,128,192]{1,2,0:T(8,128)(2,1)}), bf16[4,128,192]{1,2,0:T(8,128)(2,1)}, u32[]{:S(2)}, u32[]{:S(2)}) async-start(bf16[4,128,192]{1,2,0:T(8,128)(2,1)} %bitcast.47), calls=%async_computation.8 | async-start | bytes 393216 | tf_op jit(solution)/shard_map/all_to_all | solution.py:273
  204.5 3.7 convolution_convert_fusion.1
  210.2 2.0 copy.208
  213.4 5.9 %all-to-all-start.5 = ((bf16[16,40,768]{2,1,0:T(8,128)(2,1)}), bf16[16,40,768]{2,1,0:T(8,128)(2,1)}, u32[]{:S(2)}, u32[]{:S(2)}) async-start(bf16[16,40,768]{2,1,0:T(8,128)(2,1)} %bitcast.264), calls=%async_computation.5 | async-start | bytes 1966080 | tf_op jit(solution)/shard_map/all_to_all | solution.py:379
  219.2 2.6 fusion.67
  224.8 1.8 copy.185
  229.9 1.9 copy.188.g_ref
  231.9 1.8 fusion.38
  233.6 12.8 %shard_map.217 = (bf16[512,384]{1,0:T(8,128)(2,1)}, f32[1024,384]{1,0:T(8,128)}, f32[3,384,128]{2,1,0:T(8,128)}, f32[3,2,128]{2,1,0:T(2,128)}) custom-call(s32[4]{0:T(128)} %multiply_add_fusion.block_ref, f32[2,3]{1,0:T(2,128)} %pad_maximum_fusion.11.far_ref, bf16[512,384]{1,0:T(8,128)(2,1)} %copy.179.q_ref, bf16[512,384]{1,0:T(8,128)(2,1)} %copy.188.g_ref, ...), custom_call_target="tpu_custom_call" | custom-call | flops 2013265920 | bytes 3145728 | tf_op jit(solution)/shard_map/pallas_call | solution.py:213
  246.4 2.2 fusion.37
  248.9 2.4 collective-permute-done.4
  255.3 4.2 %all-to-all-start.12 = ((bf16[4,96,768]{2,1,0:T(8,128)(2,1)}), bf16[4,96,768]{2,1,0:T(8,128)(2,1)S(1)}, u32[]{:S(2)}, u32[]{:S(2)}) async-start(bf16[4,96,768]{2,1,0:T(8,128)(2,1)} %bitcast.91), calls=%async_computation.12 | async-start | bytes 1179648 | tf_op jit(solution)/shard_map/all_to_all | solution.py:273
  262.3 3.1 fusion.16
  265.4 9.5 %all-to-all-done.12 = bf16[4,96,768]{2,1,0:T(8,128)(2,1)S(1)} async-done(((bf16[4,96,768]{2,1,0:T(8,128)(2,1)}), bf16[4,96,768]{2,1,0:T(8,128)(2,1)S(1)}, u32[]{:S(2)}, u32[]{:S(2)}) %all-to-all-start.12) | async-done | bytes 589856 | tf_op jit(solution)/shard_map/all_to_all | solution.py:273
  275.8 3.5 all-to-all-start.9
  279.3 2.5 convolution_convert_fusion
  281.8 17.1 %all-to-all-done.9 = bf16[4,128,768]{2,1,0:T(8,128)(2,1)S(1)} async-done(((bf16[4,128,768]{2,1,0:T(8,128)(2,1)}), bf16[4,128,768]{2,1,0:T(8,128)(2,1)S(1)}, u32[]{:S(2)}, u32[]{:S(2)}) %all-to-all-start.9) | async-done | bytes 786464 | tf_op jit(solution)/shard_map/all_to_all | solution.py:273
  298.8 4.8 %all-to-all-start.11 = ((bf16[32,24,768]{2,1,0:T(8,128)(2,1)}), bf16[32,24,768]{2,1,0:T(8,128)(2,1)}, u32[]{:S(2)}, u32[]{:S(2)}) async-start(bf16[32,24,768]{2,1,0:T(8,128)(2,1)} %bitcast.76), calls=%async_computation.11 | async-start | bytes 2359296 | tf_op jit(solution)/shard_map/all_to_all | solution.py:451
  305.7 1.8 convolution_convert_fusion.7
  309.6 3.2 shard_map.218
  313.6 1.9 convolution_convert_fusion.2
  317.9 3.4 concatenate.39
  321.3 12.2 %all-to-all-done.11 = bf16[32,24,768]{2,1,0:T(8,128)(2,1)} async-done(((bf16[32,24,768]{2,1,0:T(8,128)(2,1)}), bf16[32,24,768]{2,1,0:T(8,128)(2,1)}, u32[]{:S(2)}, u32[]{:S(2)}) %all-to-all-start.11) | async-done | bytes 1179680 | tf_op jit(solution)/shard_map/all_to_all | solution.py:451
  333.5 3.8 all-to-all-start.10
  337.4 2.2 copy.212
  342.8 2.4 reshape.407
  346.4 2.1 convert_reduce_fusion
  348.5 14.5 %all-to-all-done.10 = bf16[32,24,640]{2,1,0:T(8,128)(2,1)} async-done(((bf16[32,24,640]{2,1,0:T(8,128)(2,1)}), bf16[32,24,640]{2,1,0:T(8,128)(2,1)}, u32[]{:S(2)}, u32[]{:S(2)}) %all-to-all-start.10) | async-done | bytes 983072 | tf_op jit(solution)/shard_map/all_to_all | solution.py:500
  (254 shorter events, 76.9 us)
Async XLA Ops:
  7.2 18.8 %copy-start = (bf16[32,12]{0,1:T(8,128)(2,1)S(1)}, bf16[32,12]{0,1:T(8,128)(2,1)}, u32[]{:S(2)}) copy-start(bf16[32,12]{0,1:T(8,128)(2,1)} %param.21) | copy-start | bytes 2308
  7.2 10.3 %copy-start.54 = (s32[1,128]{1,0:T(1,128)S(1)}, s32[1,128]{1,0:T(1,128)}, u32[]{:S(2)}) copy-start(s32[1,128]{1,0:T(1,128)} %param.25) | copy-start | bytes 1540
  7.2 10.4 %copy-start.55 = (s32[1,128]{1,0:T(1,128)S(1)}, s32[1,128]{1,0:T(1,128)}, u32[]{:S(2)}) copy-start(s32[1,128]{1,0:T(1,128)} %param.24) | copy-start | bytes 1540
  7.2 14.4 %copy-start.18 = (bf16[1,128,768]{2,1,0:T(8,128)(2,1)S(1)}, bf16[1,128,768]{2,1,0:T(8,128)(2,1)}, u32[]{:S(2)}) copy-start(bf16[1,128,768]{2,1,0:T(8,128)(2,1)} %param.13) | copy-start | bytes 589828
  10.6 19.7 %copy-start.31 = (bf16[1,128,768]{2,1,0:T(8,128)(2,1)S(1)}, bf16[1,128,768]{2,1,0:T(8,128)(2,1)}, u32[]{:S(2)}) copy-start(bf16[1,128,768]{2,1,0:T(8,128)(2,1)} %param.14) | copy-start | bytes 589828
  11.4 10.2 %all-to-all-start.1 = ((bf16[4,24,640]{2,1,0:T(8,128)(2,1)}), bf16[4,24,640]{2,1,0:T(8,128)(2,1)S(1)}, u32[]{:S(2)}, u32[]{:S(2)}) async-start(bf16[4,24,640]{2,1,0:T(8,128)(2,1)} %maximum_bitcast_fusion), calls=%async_computation.1 | async-start | bytes 245760 | tf_op jit(solution)/shard_map/all_to_all | solution.py:273
  16.8 73.1 %all-gather.4.cloned.1.call-start = ((), (), s32[]{:S(2)}) async-start(), calls=%async_computation.13 | async-start | bytes 1216512 | tf_op jit(solution)/shard_map/all_gather | solution.py:344
  17.5 177.4 %copy-start.38 = (pred[40,128]{1,0:T(8,128)(4,1)}, pred[40,128]{1,0:T(8,128)(4,1)S(1)}, u32[]{:S(2)}) copy-start(pred[40,128]{1,0:T(8,128)(4,1)S(1)} %iota_compare_fusion) | copy-start | bytes 15364
  17.6 177.4 %copy-start.49 = (pred[4,128]{1,0:T(4,128)(4,1)}, pred[4,128]{1,0:T(4,128)(4,1)S(1)}, u32[]{:S(2)}) copy-start(pred[4,128]{1,0:T(4,128)(4,1)S(1)} %iota_compare_fusion.1) | copy-start | bytes 1540
  22.5 23.8 %all-to-all-start = ((bf16[4,128,768]{2,1,0:T(8,128)(2,1)}), bf16[4,128,768]{2,1,0:T(8,128)(2,1)S(1)}, u32[]{:S(2)}, u32[]{:S(2)}) async-start(bf16[4,128,768]{2,1,0:T(8,128)(2,1)} %broadcast_in_dim.22), calls=%async_computation | async-start | bytes 1572864 | tf_op jit(solution)/shard_map/all_to_all | solution.py:273
  29.1 4.0 %collective-permute-start = (bf16[4,24,640]{2,1,0:T(8,128)(2,1)S(1)}, bf16[4,24,640]{2,1,0:T(8,128)(2,1)S(1)}, u32[]{:S(2)}, u32[]{:S(2)}) collective-permute-start(bf16[4,24,640]{2,1,0:T(8,128)(2,1)S(1)} %all-to-all-done.1), channel_id=1, source_target_pairs={{0,1},{1,0},{2,3},{3,2},{4,5},{5,4},{6,7},{7,6},{8,9},{9,8},{10,11... | collective-permute-start | bytes 368648 | tf_op jit(solution)/shard_map/ppermute | solution.py:257
  45.9 6.5 %copy-start.10 = (bf16[4,4,2,24,640]{4,3,2,1,0:T(8,128)(2,1)}, bf16[4,4,2,24,640]{4,3,2,1,0:T(8,128)(2,1)S(1)}, u32[]{:S(2)}) copy-start(bf16[4,4,2,24,640]{4,3,2,1,0:T(8,128)(2,1)S(1)} %copy.174) | copy-start | bytes 2949124
  46.3 5.4 %copy-start.40 = (f32[768]{0:T(1024)}, f32[768]{0:T(1024)S(1)}, u32[]{:S(2)}) copy-start(f32[768]{0:T(1024)S(1)} %get-tuple-element.79) | copy-start | bytes 9220
  46.3 29.9 %all-to-all-start.6 = ((bf16[4,40,768]{2,1,0:T(8,128)(2,1)}), bf16[4,40,768]{2,1,0:T(8,128)(2,1)S(1)}, u32[]{:S(2)}, u32[]{:S(2)}) async-start(bf16[4,40,768]{2,1,0:T(8,128)(2,1)} %bitcast.41), calls=%async_computation.6 | async-start | bytes 491520 | tf_op jit(solution)/shard_map/all_to_all | solution.py:386
  52.9 10.8 %collective-permute-start.1 = (bf16[4,128,384]{2,1,0:T(8,128)(2,1)S(1)}, bf16[4,128,384]{2,1,0:T(8,128)(2,1)S(1)}, u32[]{:S(2)}, u32[]{:S(2)}) collective-permute-start(bf16[4,128,384]{2,1,0:T(8,128)(2,1)S(1)} %bitcast.255), channel_id=1, source_target_pairs={{0,1},{1,0},{2,3},{3,2},{4,5},{5,4},{6,7},{7,6},{8,9},{9,8},{10,11... | collective-permute-start | bytes 1179656 | tf_op jit(solution)/shard_map/ppermute | solution.py:257
  73.9 6.5 %copy-start.33 = (bf16[96,1,3072]{2,0,1:T(8,128)(2,1)S(1)}, bf16[96,1,3072]{2,0,1:T(8,128)(2,1)}, u32[]{:S(2)}) copy-start(bf16[96,1,3072]{2,0,1:T(8,128)(2,1)} %param.22) | copy-start | bytes 1769476
  75.4 6.3 %copy-start.20 = (f32[512,384]{0,1:T(8,128)}, f32[512,384]{0,1:T(8,128)S(1)}, u32[]{:S(2)}) copy-start(f32[512,384]{0,1:T(8,128)S(1)} %copy.180) | copy-start | bytes 2359300
  77.0 8.5 %all-to-all-start.2 = ((bf16[4,128,192]{1,2,0:T(8,128)(2,1)}), bf16[4,128,192]{1,2,0:T(8,128)(2,1)S(1)}, u32[]{:S(2)}, u32[]{:S(2)}) async-start(bf16[4,128,192]{1,2,0:T(8,128)(2,1)} %copy.181), calls=%async_computation.2 | async-start | bytes 393216 | tf_op jit(solution)/shard_map/all_to_all | solution.py:273
  85.5 20.6 %copy-start.24 = (bf16[4,128,192]{1,2,0:T(8,128)(2,1)}, bf16[4,128,192]{1,2,0:T(8,128)(2,1)S(1)}, u32[]{:S(2)}) copy-start(bf16[4,128,192]{1,2,0:T(8,128)(2,1)S(1)} %all-to-all-done.2) | copy-start | bytes 589828
  85.5 19.6 %all-to-all-start.4 = ((bf16[4,96,768]{2,1,0:T(8,128)(2,1)}), bf16[4,96,768]{2,1,0:T(8,128)(2,1)S(1)}, u32[]{:S(2)}, u32[]{:S(2)}) async-start(bf16[4,96,768]{2,1,0:T(8,128)(2,1)} %bitcast.223), calls=%async_computation.4 | async-start | bytes 1179648 | tf_op jit(solution)/shard_map/all_to_all | solution.py:273
  91.6 19.6 %copy-start.21 = (bf16[384,1,768]{2,0,1:T(8,128)(2,1)S(1)}, bf16[384,1,768]{2,0,1:T(8,128)(2,1)}, u32[]{:S(2)}) copy-start(bf16[384,1,768]{2,0,1:T(8,128)(2,1)} %param.23) | copy-start | bytes 1769476
  92.2 102.8 %copy-start.46 = (f32[128]{0:T(128)}, f32[128]{0:T(128)S(1)}, u32[]{:S(2)}) copy-start(f32[128]{0:T(128)S(1)} %get-tuple-element.109) | copy-start | bytes 1540
  106.1 47.4 %all-to-all-start.3 = ((bf16[16,40,768]{2,1,0:T(8,128)(2,1)}), bf16[16,40,768]{2,1,0:T(8,128)(2,1)S(1)}, u32[]{:S(2)}, u32[]{:S(2)}) async-start(bf16[16,40,768]{2,1,0:T(8,128)(2,1)} %bitcast.244), calls=%async_computation.3 | async-start | bytes 1966080 | tf_op jit(solution)/shard_map/all_to_all | solution.py:375
  112.3 38.2 %collective-permute-start.2 = (bf16[768,768]{1,0:T(8,128)(2,1)}, bf16[768,768]{1,0:T(8,128)(2,1)}, u32[]{:S(2)}, u32[]{:S(2)}) collective-permute-start(bf16[768,768]{1,0:T(8,128)(2,1)} %pad_maximum_fusion.2), channel_id=1, source_target_pairs={{0,1},{1,0},{2,3},{3,2},{4,5},{5,4},{6,7},{7,6},{8,9},{9,8},{10,11... | collective-permute-start | bytes 3538952 | tf_op jit(solution)/shard_map/ppermute | solution.py:257
  113.5 46.1 %copy-start.48 = (f32[4]{0:T(128)}, f32[4]{0:T(128)S(1)}, u32[]{:S(2)}) copy-start(f32[4]{0:T(128)S(1)} %compare_convert_fusion) | copy-start | bytes 52
  162.2 31.4 %all-to-all-start.7 = ((bf16[16,40,768]{2,1,0:T(8,128)(2,1)}), bf16[16,40,768]{2,1,0:T(8,128)(2,1)}, u32[]{:S(2)}, u32[]{:S(2)}) async-start(bf16[16,40,768]{2,1,0:T(8,128)(2,1)} %bitcast.43), calls=%async_computation.7 | async-start | bytes 1966080 | tf_op jit(solution)/shard_map/all_to_all | solution.py:379
  173.9 23.6 %copy-start.9 = (bf16[768,768]{1,0:T(8,128)(2,1)S(1)}, bf16[768,768]{1,0:T(8,128)(2,1)}, u32[]{:S(2)}) copy-start(bf16[768,768]{1,0:T(8,128)(2,1)} %all-gather.4.cloned.1.call-done) | copy-start | bytes 3538948
  195.8 8.6 %copy-start.26 = (bf16[2,384,768]{2,1,0:T(8,128)(2,1)S(1)}, bf16[2,384,768]{2,1,0:T(8,128)(2,1)}, u32[]{:S(2)}) copy-start(bf16[2,384,768]{2,1,0:T(8,128)(2,1)} %get-tuple-element.93) | copy-start | bytes 3538948
  200.4 12.9 %all-to-all-start.8 = ((bf16[4,128,192]{1,2,0:T(8,128)(2,1)}), bf16[4,128,192]{1,2,0:T(8,128)(2,1)}, u32[]{:S(2)}, u32[]{:S(2)}) async-start(bf16[4,128,192]{1,2,0:T(8,128)(2,1)} %bitcast.47), calls=%async_computation.8 | async-start | bytes 393216 | tf_op jit(solution)/shard_map/all_to_all | solution.py:273
  204.4 3.7 copy-start.44
  204.4 4.4 %copy-start.28 = (bf16[768,640]{0,1:T(8,128)(2,1)S(1)}, bf16[768,640]{0,1:T(8,128)(2,1)}, u32[]{:S(2)}) copy-start(bf16[768,640]{0,1:T(8,128)(2,1)} %get-tuple-element.118) | copy-start | bytes 2949124
  213.4 41.9 %all-to-all-start.5 = ((bf16[16,40,768]{2,1,0:T(8,128)(2,1)}), bf16[16,40,768]{2,1,0:T(8,128)(2,1)}, u32[]{:S(2)}, u32[]{:S(2)}) async-start(bf16[16,40,768]{2,1,0:T(8,128)(2,1)} %bitcast.264), calls=%async_computation.5 | async-start | bytes 1966080 | tf_op jit(solution)/shard_map/all_to_all | solution.py:379
  223.6 27.7 %collective-permute-start.4 = (bf16[768,768]{1,0:T(8,128)(2,1)}, bf16[768,768]{1,0:T(8,128)(2,1)}, u32[]{:S(2)}, u32[]{:S(2)}) collective-permute-start(bf16[768,768]{1,0:T(8,128)(2,1)} %fusion.19), channel_id=1, source_target_pairs={{0,1},{1,0},{2,3},{3,2},{4,5},{5,4},{6,7},{7,6},{8,9},{9,8},{10,11... | collective-permute-start | bytes 3538952 | tf_op jit(solution)/shard_map/ppermute | solution.py:269
  233.6 17.7 %copy-start.3 = (f32[2,384,768]{2,1,0:T(8,128)S(1)}, f32[2,384,768]{2,1,0:T(8,128)}, u32[]{:S(2)}) copy-start(f32[2,384,768]{2,1,0:T(8,128)} %copy-done.2) | copy-start | bytes 7077892
  248.6 12.0 %collective-permute-start.3 = (bf16[4,128,384]{2,1,0:T(8,128)(2,1)}, bf16[4,128,384]{2,1,0:T(8,128)(2,1)}, u32[]{:S(2)}, u32[]{:S(2)}) collective-permute-start(bf16[4,128,384]{2,1,0:T(8,128)(2,1)} %fusion.37), channel_id=1, source_target_pairs={{0,1},{1,0},{2,3},{3,2},{4,5},{5,4},{6,7},{7,6},{8,9},{9,8},{10,11... | collective-permute-start | bytes 1179656 | tf_op jit(solution)/shard_map/ppermute | solution.py:269
  254.4 5.1 %copy-start.36 = (bf16[512,384]{1,0:T(8,128)(2,1)S(1)}, bf16[512,384]{1,0:T(8,128)(2,1)}, u32[]{:S(2)}) copy-start(bf16[512,384]{1,0:T(8,128)(2,1)} %get-tuple-element.20) | copy-start | bytes 1179652
  255.3 19.6 %all-to-all-start.12 = ((bf16[4,96,768]{2,1,0:T(8,128)(2,1)}), bf16[4,96,768]{2,1,0:T(8,128)(2,1)S(1)}, u32[]{:S(2)}, u32[]{:S(2)}) async-start(bf16[4,96,768]{2,1,0:T(8,128)(2,1)} %bitcast.91), calls=%async_computation.12 | async-start | bytes 1179648 | tf_op jit(solution)/shard_map/all_to_all | solution.py:273
  262.3 17.0 %copy-start.7 = (f32[128,768]{1,0:T(8,128)S(1)}, f32[128,768]{1,0:T(8,128)}, u32[]{:S(2)}) copy-start(f32[128,768]{1,0:T(8,128)} %copy-done.6) | copy-start | bytes 1179652
  275.8 23.1 %all-to-all-start.9 = ((bf16[4,128,768]{2,1,0:T(8,128)(2,1)}), bf16[4,128,768]{2,1,0:T(8,128)(2,1)S(1)}, u32[]{:S(2)}, u32[]{:S(2)}) async-start(bf16[4,128,768]{2,1,0:T(8,128)(2,1)} %bitcast.271), calls=%async_computation.9 | async-start | bytes 1572864 | tf_op jit(solution)/shard_map/all_to_all | solution.py:273
  279.3 26.5 %copy-start.13 = (bf16[768,640]{1,0:T(8,128)(2,1)S(1)}, bf16[768,640]{1,0:T(8,128)(2,1)}, u32[]{:S(2)}) copy-start(bf16[768,640]{1,0:T(8,128)(2,1)} %copy-done.12) | copy-start | bytes 2949124
  298.8 8.8 %copy-start.16 = (bf16[4,128,768]{2,1,0:T(8,128)(2,1)}, bf16[4,128,768]{2,1,0:T(8,128)(2,1)S(1)}, u32[]{:S(2)}) copy-start(bf16[4,128,768]{2,1,0:T(8,128)(2,1)S(1)} %all-to-all-done.9) | copy-start | bytes 2359300
  298.8 14.8 %copy-start.35 = (bf16[4,128,384]{2,1,0:T(8,128)(2,1)S(1)}, bf16[4,128,384]{2,1,0:T(8,128)(2,1)}, u32[]{:S(2)}) copy-start(bf16[4,128,384]{2,1,0:T(8,128)(2,1)} %copy-done.34) | copy-start | bytes 1179652
  298.8 34.6 %all-to-all-start.11 = ((bf16[32,24,768]{2,1,0:T(8,128)(2,1)}), bf16[32,24,768]{2,1,0:T(8,128)(2,1)}, u32[]{:S(2)}, u32[]{:S(2)}) async-start(bf16[32,24,768]{2,1,0:T(8,128)(2,1)} %bitcast.76), calls=%async_computation.11 | async-start | bytes 2359296 | tf_op jit(solution)/shard_map/all_to_all | solution.py:451
  317.9 19.3 %copy-start.5 = (f32[768,768]{1,0:T(8,128)S(1)}, f32[768,768]{1,0:T(8,128)}, u32[]{:S(2)}) copy-start(f32[768,768]{1,0:T(8,128)} %copy-done.4) | copy-start | bytes 7077892
  333.5 29.5 %all-to-all-start.10 = ((bf16[32,24,640]{2,1,0:T(8,128)(2,1)}), bf16[32,24,640]{2,1,0:T(8,128)(2,1)}, u32[]{:S(2)}, u32[]{:S(2)}) async-start(bf16[32,24,640]{2,1,0:T(8,128)(2,1)} %concatenate.39), calls=%async_computation.10 | async-start | bytes 1966080 | tf_op jit(solution)/shard_map/all_to_all | solution.py:500
  337.3 3.6 copy-start.39
  337.4 4.5 %copy-start.23 = (bf16[4,96,768]{2,1,0:T(8,128)(2,1)S(1)}, bf16[4,96,768]{2,1,0:T(8,128)(2,1)}, u32[]{:S(2)}) copy-start(bf16[4,96,768]{2,1,0:T(8,128)(2,1)} %copy-done.22) | copy-start | bytes 1769476
  363.0 6.9 %copy-start.1 = (bf16[32,12]{0,1:T(8,128)(2,1)S(1)}, bf16[32,12]{0,1:T(8,128)(2,1)}, u32[]{:S(2)}) copy-start(bf16[32,12]{0,1:T(8,128)(2,1)} %param.21) | copy-start | bytes 2308
  (29 other events, 60.6 us)
Sparse Core Ops, SparseCore 0:
  20.6 59.4 all-gather.3

commit v2 on v1

v2 whole, which is shorter than its diff:
```python
import functools
import math

import jax
import jax.numpy as jnp
import numpy as np
from jax import lax
from jax.experimental import pallas as pl
from jax.experimental.pallas import tpu as pltpu
from jax.sharding import Mesh
from jax.sharding import PartitionSpec as P

EPS = 1e-06
F32 = jnp.float32
BF16 = jnp.bfloat16
EVERY = ("ey", "ec", "gh", "mj", "rs")
MINOR = ("ec", "rs")
REST = ("ey", "gh", "mj", "rs")
VMEM_BYTES = 56 * 1024 * 1024


def bucket_edges(reach):
    magnitude = np.arange(reach)
    spread = 8 + (np.log(np.maximum(magnitude, 1) / 8.0) / np.log(16.0) * 8.0).astype(np.int64)
    bucket = np.where(magnitude < 8, magnitude, np.minimum(spread, 15))
    return [int(np.argmax(bucket >= number)) for number in range(16)]


def dot_t(left, right):
    return lax.dot_general(left, right, (((1,), (1,)), ((), ())), preferred_element_type=F32)


def dot_0(left, right):
    return lax.dot_general(left, right, (((0,), (0,)), ((), ())), preferred_element_type=F32)


def dot_n(left, right):
    return jnp.dot(left, right, preferred_element_type=F32)


def near_bias_kernel(edges, rows, table_ref, out_ref):
    shape = (3 * rows, rows)
    relative = (
        lax.broadcasted_iota(jnp.int32, shape, 0) - rows - lax.broadcasted_iota(jnp.int32, shape, 1)
    )
    magnitude = jnp.abs(relative)
    ahead = relative > 0
    for head in range(out_ref.shape[0]):
        value = jnp.where(ahead, table_ref[16, head], table_ref[0, head])
        for number in range(1, 16):
            value = jnp.where(
                magnitude >= edges[number],
                jnp.where(ahead, table_ref[16 + number, head], table_ref[number, head]),
                value,
            )
        out_ref[head] = value


def bucket_sum_kernel(edges, rows, near_ref, far_ref, out_ref):
    shape = (3 * rows, rows)
    relative = (
        lax.broadcasted_iota(jnp.int32, shape, 0) - rows - lax.broadcasted_iota(jnp.int32, shape, 1)
    )
    magnitude = jnp.abs(relative)
    lanes = lax.broadcasted_iota(jnp.int32, (1, 128), 1)
    for head in range(near_ref.shape[0]):
        grads = near_ref[head]
        behind = jnp.where(relative > 0, 0.0, grads)
        forward = jnp.where(relative > 0, grads, 0.0)
        total = jnp.zeros((1, 128), F32)
        for side, part in enumerate((behind, forward)):
            for number in range(16):
                inside = magnitude >= edges[number]
                if number < 15:
                    inside = inside & (magnitude < edges[number + 1])
                value = jnp.sum(jnp.sum(jnp.where(inside, part, 0.0), axis=0, keepdims=True))
                if number == 15:
                    value = value + jnp.sum(far_ref[head, side : side + 1, :])
                total = jnp.where(lanes == side * 16 + number, value, total)
        out_ref[head : head + 1, :] = total


def biased_scores(parts, key_ref, place_ref, far_ref, near_ref, scratch, head, block, rows):
    pieces = [
        part[first : first + rows, :] for part in parts for first in range(0, part.shape[0], rows)
    ]
    slots = len(pieces)
    for slot in range(slots):
        far = jnp.where(
            key_ref[slot] < block - 1,
            far_ref[0, head],
            jnp.where(key_ref[slot] > block + 1, far_ref[1, head], 0.0),
        )
        scratch[slot * rows : (slot + 1) * rows, :] = pieces[slot] + far
    for step in range(3):
        window = pl.ds(pl.multiple_of(place_ref[block + step] * rows, rows), rows)
        scratch[window, :] = scratch[window, :] + near_ref[head, step * rows : (step + 1) * rows, :]
    return scratch[0 : slots * rows, :]


def head_queries(q_ref, heads, head):
    first = heads * 128 + head * 64
    query = q_ref[:, first : first + 64]
    return jnp.concatenate([query, jnp.zeros_like(query)], axis=1)


def attention_kernel(
    heads,
    rows,
    block_ref,
    key_ref,
    place_ref,
    far_ref,
    q_ref,
    own_ref,
    other_ref,
    near_ref,
    low_ref,
    wide_ref,
    lse_ref,
    scratch,
):
    block = block_ref[pl.program_id(0)]
    own_rows = own_ref.shape[0]
    for head in range(heads):
        lanes = slice(head * 128, (head + 1) * 128)
        own, other = own_ref[:, lanes], other_ref[:, lanes]
        query = head_queries(q_ref, heads, head)
        scores = biased_scores(
            (dot_t(own, query), dot_t(other, query)),
            key_ref,
            place_ref,
            far_ref,
            near_ref,
            scratch.at[head % scratch.shape[0]],
            head,
            block,
            rows,
        )
        top = jnp.max(scores, axis=0, keepdims=True)
        weights = jnp.exp(scores - top)
        total = jnp.sum(weights, axis=0, keepdims=True)
        low = (weights * (1.0 / total)).astype(BF16)
        result = dot_0(low[:own_rows], own) + dot_0(low[own_rows:], other)
        wide_ref[:, lanes] = result
        low_ref[:, head * 64 : (head + 1) * 64] = result[:, 64:].astype(BF16)
        lse_ref[0, head : head + 1, :] = top + jnp.log(total)


def attention_back_kernel(
    heads,
    rows,
    block_ref,
    key_ref,
    place_ref,
    far_ref,
    q_ref,
    g_ref,
    wide_ref,
    own_ref,
    other_ref,
    near_ref,
    lse_ref,
    dq_ref,
    sum_ref,
    low_ref,
    near_sum_ref,
    far_sum_ref,
    scratch,
    grad_scratch,
    total_scratch,
):
    step = pl.program_id(0)
    block = block_ref[step]
    own_rows = own_ref.shape[0]
    count = own_rows + other_ref.shape[0]
    slots = count // rows

    @pl.when(step == 0)
    def _():
        total_scratch[...] = jnp.zeros_like(total_scratch)
        near_sum_ref[...] = jnp.zeros_like(near_sum_ref)
        far_sum_ref[...] = jnp.zeros_like(far_sum_ref)
        for copy in range(grad_scratch.shape[0]):
            grad_scratch[copy, count : count + rows, :] = jnp.zeros((rows, rows), F32)

    for head in range(heads):
        copy = head % scratch.shape[0]
        lanes = slice(head * 128, (head + 1) * 128)
        own, other = own_ref[:, lanes], other_ref[:, lanes]
        grad = g_ref[:, head * 64 : (head + 1) * 64]
        grad = jnp.concatenate([jnp.zeros_like(grad), grad], axis=1)
        delta = jnp.sum(jnp.transpose(grad.astype(F32) * wide_ref[:, lanes]), axis=0, keepdims=True)
        both = jnp.concatenate([head_queries(q_ref, heads, head), grad], axis=0)
        first, second = dot_t(own, both), dot_t(other, both)
        scores = biased_scores(
            (first[:, :rows], second[:, :rows]),
            key_ref,
            place_ref,
            far_ref,
            near_ref,
            scratch.at[copy],
            head,
            block,
            rows,
        )
        chances = jnp.exp(scores - lse_ref[0, head : head + 1, :])
        products = jnp.concatenate([first[:, rows:], second[:, rows:]], axis=0)
        grads = chances * (products - delta)
        grads_low = grads.astype(BF16)
        grad_scratch[copy, 0:count, :] = grads
        for part in range(3):
            window = pl.ds(pl.multiple_of(place_ref[block + part] * rows, rows), rows)
            near_sum_ref[head, part * rows : (part + 1) * rows, :] += grad_scratch[copy, window, :]
        low_far = jnp.zeros((1, rows), F32)
        high_far = jnp.zeros((1, rows), F32)
        for slot in range(slots):
            line = jnp.sum(grads[slot * rows : (slot + 1) * rows, :], axis=0, keepdims=True)
            low_far = low_far + line * jnp.where(key_ref[slot] < block - 1, 1.0, 0.0)
            high_far = high_far + line * jnp.where(key_ref[slot] > block + 1, 1.0, 0.0)
        far_sum_ref[head, 0:1, :] += low_far
        far_sum_ref[head, 1:2, :] += high_far
        pair = jnp.concatenate([grads_low, chances.astype(BF16)], axis=1)
        total_scratch[:, lanes] += dot_n(pair, both)
        dq = dot_0(grads_low[:own_rows], own) + dot_0(grads_low[own_rows:], other)
        dq_ref[:, head * 64 : (head + 1) * 64] = dq[:, :64].astype(BF16)

    dq_ref[:, heads * 64 :] = jnp.zeros_like(dq_ref[:, heads * 64 :])

    @pl.when(step == pl.num_programs(0) - 1)
    def _():
        sum_ref[...] = total_scratch[0:own_rows, :]
        low_ref[...] = total_scratch[own_rows:count, :].astype(BF16)


def unpack_kernel(cuts, in_ref, out_ref):
    count = in_ref.shape[0]
    step = in_ref.shape[2] // cuts
    for cut in range(cuts):
        for index in range(count):
            first = (cut * count + index) * step
            value = in_ref[index, :, cut * step : (cut + 1) * step].astype(F32)
            out_ref[:, 0, first : first + step] = value


def unpack(value, cuts):
    count, rows, columns = value.shape
    return pl.pallas_call(
        functools.partial(unpack_kernel, cuts),
        out_shape=jax.ShapeDtypeStruct((rows, 1, count * columns), F32),
    )(value)


def whole_block(shape):
    zeros = (0,) * len(shape)
    return pl.BlockSpec(shape, lambda *_: zeros)


def scalars():
    return pl.BlockSpec(memory_space=pltpu.SMEM)


def slot_count(heads, count):
    return heads if count <= 2048 else 1


def estimate(products, steps, rows, count, heads):
    return pl.CostEstimate(
        flops=2 * products * steps * rows * count * heads * 128,
        bytes_accessed=1024 * count * heads,
        transcendentals=steps * rows * count * heads,
    )


def forward_attention(projected, other, near, far, places, heads, rows):
    steps = places[0].shape[0]
    own = steps * rows
    count = own + other.shape[0]
    width = heads * 128
    return pl.pallas_call(
        functools.partial(attention_kernel, heads, rows),
        grid=(steps,),
        in_specs=[scalars()] * 4
        + [
            pl.BlockSpec((rows, projected.shape[1]), lambda i: (i, 0)),
            whole_block((own, width)),
            whole_block((count - own, width)),
            whole_block(near.shape),
        ],
        out_specs=[
            pl.BlockSpec((rows, width // 2), lambda i: (i, 0)),
            pl.BlockSpec((rows, width), lambda i: (i, 0)),
            pl.BlockSpec((1, heads, rows), lambda i: (i, 0, 0)),
        ],
        out_shape=[
            jax.ShapeDtypeStruct((own, width // 2), BF16),
            jax.ShapeDtypeStruct((own, width), F32),
            jax.ShapeDtypeStruct((steps, heads, rows), F32),
        ],
        scratch_shapes=[pltpu.VMEM((slot_count(heads, count), count + rows, rows), F32)],
        compiler_params=pltpu.CompilerParams(vmem_limit_bytes=VMEM_BYTES),
        cost_estimate=estimate(2, steps, rows, count, heads),
    )(*places, far, projected, projected, other, near)


def backward_attention(projected, grads, wide, other, near, far, places, lse, heads, rows):
    steps = places[0].shape[0]
    own = steps * rows
    count = own + other.shape[0]
    width = heads * 128
    dq_width = -(-width // 256) * 128
    slots = slot_count(heads, count)
    return pl.pallas_call(
        functools.partial(attention_back_kernel, heads, rows),
        grid=(steps,),
        in_specs=[scalars()] * 4
        + [
            pl.BlockSpec((rows, projected.shape[1]), lambda i: (i, 0)),
            pl.BlockSpec((rows, width // 2), lambda i: (i, 0)),
            pl.BlockSpec((rows, width), lambda i: (i, 0)),
            whole_block((own, width)),
            whole_block((count - own, width)),
            whole_block(near.shape),
            pl.BlockSpec((1, heads, rows), lambda i: (i, 0, 0)),
        ],
        out_specs=[
            pl.BlockSpec((rows, dq_width), lambda i: (i, 0)),
            whole_block((own, width)),
            whole_block((count - own, width)),
            whole_block(near.shape),
            whole_block((heads, 2, rows)),
        ],
        out_shape=[
            jax.ShapeDtypeStruct((own, dq_width), BF16),
            jax.ShapeDtypeStruct((own, width), F32),
            jax.ShapeDtypeStruct((count - own, width), BF16),
            jax.ShapeDtypeStruct(near.shape, F32),
            jax.ShapeDtypeStruct((heads, 2, rows), F32),
        ],
        scratch_shapes=[
            pltpu.VMEM((slots, count + rows, rows), F32),
            pltpu.VMEM((slots, count + rows, rows), F32),
            pltpu.VMEM((count, width), F32),
        ],
        compiler_params=pltpu.CompilerParams(vmem_limit_bytes=VMEM_BYTES),
        cost_estimate=estimate(5, steps, rows, count, heads),
    )(*places, far, projected, grads, wide, projected, other, near, lse)


def swap(value, axis):
    return lax.ppermute(value, axis, [(0, 1), (1, 0)])


def turn(value):
    return lax.ppermute(value, ("ec", "gh"), [(0, 0), (1, 2), (2, 1), (3, 3)])


def exchange(parts, axis):
    count = len(parts)
    return [parts[0]] + [
        lax.ppermute(parts[step], axis, [(source, source ^ step) for source in range(count)])
        for step in range(1, count)
    ]


def ordered(value, place):
    count = value.shape[0]
    return jnp.take(value, jnp.arange(count) ^ place, axis=0, mode="clip")


def exchange_ordered(value, axis):
    place = lax.axis_index(axis)
    count = value.shape[0]
    parts = exchange(
        [lax.dynamic_index_in_dim(value, place ^ step, keepdims=False) for step in range(count)], axis
    )
    return ordered(jnp.stack(parts), place)


def turn_exchange(parts):
    arrived = []
    for step, part in enumerate(parts):
        pairs = []
        for source in range(8):
            ey, ec, gh = source // 4, source // 2 % 2, source % 2
            pairs.append((source, (ey ^ (step // 2)) * 4 + gh * 2 + (ec ^ (step % 2))))
        arrived.append(lax.ppermute(part, ("ey", "ec", "gh"), pairs))
    return arrived


def in_order(own, other, axis, place=0):
    first = lax.axis_index(axis) == 0
    return jnp.stack([jnp.where(first, own, other), jnp.where(first, other, own)], axis=place)


def gather_pair(value, axis, place=0):
    return in_order(value, swap(value, axis), axis, place)


def gather_minor(value):
    if lax.axis_size("rs") == 1:
        return gather_pair(value, "ec")
    return lax.all_gather(value, MINOR)


def nearest_first(value):
    count = value.shape[0]
    return jnp.take(value, jnp.arange(count) ^ lax.axis_index(MINOR), axis=0, mode="clip")


def other_minor(value, columns):
    if lax.axis_size("rs") == 1:
        return swap(value, "ec")
    return nearest_first(lax.all_gather(value[:, :columns], MINOR))[1:].reshape(-1, columns)


def sum_nearest(own, low):
    if lax.axis_size("rs") == 1:
        return own + swap(low[0], "ec").astype(F32)
    parts = nearest_first(jnp.concatenate([own.astype(BF16)[None], low]))
    return jnp.sum(lax.all_to_all(parts, MINOR, 0, 0, tiled=True).astype(F32), axis=0)


def split_minor(parts):
    if lax.axis_size("rs") != 1:
        return (parts.astype(BF16),)
    first = lax.axis_index("ec") == 0
    sent = jnp.where(first, parts[1], parts[0]).astype(BF16)
    return (jnp.where(first, parts[0], parts[1]), sent)


def sum_split(split):
    if lax.axis_size("rs") != 1:
        arrived = lax.all_to_all(split[0], MINOR, 0, 0, tiled=True)
        return jnp.sum(arrived.astype(F32), axis=0)
    return split[0] + swap(split[1], "ec").astype(F32)


def swap_major(value):
    return lax.all_to_all(value, "mj", 0, 0, tiled=True)


def core_sum(value):
    value = value.reshape(lax.axis_size("ey"), 2, -1, value.shape[1])
    first = lax.axis_index("ec") == 0
    sent = jnp.where(first, value[:, 1], value[:, 0]).astype(BF16)
    value = jnp.where(first, value[:, 0], value[:, 1]) + swap(sent, "ec").astype(F32)
    return value.astype(BF16)


def scatter_rows(value):
    chips = math.prod(lax.axis_size(name) for name in REST)
    value = value.reshape(chips, -1, value.shape[-1])
    return lax.all_to_all(value, REST, 0, 0, tiled=True).astype(F32)


def after(value, *others):
    return lax.optimization_barrier((value, others))[0]


def unit(hidden):
    return lax.rsqrt(jnp.mean(hidden * hidden, axis=-1, keepdims=True) + EPS)


def per_device(
    activations,
    cotangent,
    query_key_weight,
    value_weight,
    output_weight,
    norm_first,
    norm_second,
    router_weight,
    bias_table,
    w_in,
    w_out,
    routes,
    slots,
):
    rows, width = activations.shape[1:]
    major = lax.axis_size("mj")
    rest = lax.axis_size("rs")
    minor = 2 * rest
    ring = 2 * major * rest
    experts = router_weight.shape[1]
    capacity = rows * 5 // (4 * experts)
    head_count = bias_table.shape[1]
    heads = head_count // major
    features = value_weight.shape[1]
    head_dim = features // head_count
    shard = query_key_weight.shape[0]
    my_major = lax.axis_index("mj")
    my_exp = lax.axis_index(("ey", "gh"))
    edges = bucket_edges(4 * rows)
    kv_width = heads * 2 * head_dim
    q_width = heads * head_dim
    extra_width = 128 - (kv_width + q_width) % 128
    packed_width = kv_width + q_width + extra_width

    numbers = jnp.concatenate([routes, slots]).astype(BF16)
    numbers = jnp.pad(numbers, ((0, 14), (0, width - rows)))
    both = jnp.concatenate([activations[0], numbers, w_out[:, 0, :]])
    query_key_weight, value_weight, w_in = after((query_key_weight, value_weight, w_in), both)
    both = turn(both)
    tokens = both[:rows]
    numbers = both[rows : rows + 2, :rows].astype(jnp.int32)
    outer = both[rows + 16 :]

    def by_head(value):
        return value.reshape(shard, major, heads, 1, head_dim)

    key_value = jnp.concatenate(
        [by_head(query_key_weight[:, features:]), by_head(value_weight)], axis=3
    ).reshape(shard, major, kv_width)
    extras = jnp.concatenate([router_weight, norm_first[:, None], norm_second[:, None]], axis=1)
    extras = jnp.pad(extras, ((0, 0), (0, extra_width - experts - 2)))
    packed = jnp.concatenate(
        [
            key_value,
            query_key_weight[:, :features].reshape(shard, major, q_width),
            jnp.broadcast_to(extras[:, None, :], (shard, major, extra_width)),
        ],
        axis=2,
    )
    packed = exchange_ordered(jnp.transpose(packed, (1, 0, 2)), "mj")
    background = packed
    if rest == 1:
        packed = jnp.stack([packed, swap(packed, "gh")])
        background = packed
        packed = jnp.concatenate([packed, swap(packed, "ey")])
        packed = ordered(packed, lax.axis_index(("ey", "gh"))).reshape(2, 2, major, shard, packed_width)
        packed = gather_pair(packed, "ec", 1)
    else:
        packed = lax.all_gather(packed, ("ey", "ec", "gh", "rs"))
        packed = packed.reshape(2, 2, 2, rest, major, shard, packed_width)
        packed = jnp.transpose(packed, (0, 1, 2, 4, 3, 5, 6))
    packed = packed.reshape(width, packed_width)
    extras = packed[:, kv_width + q_width :]
    full_router = extras[:, :experts]
    gain_first = extras[:, experts].astype(F32)
    gain_second = extras[:, experts + 1].astype(F32)

    column = jnp.stack(exchange([tokens] * major, "mj"))
    part = w_in.shape[2] // major
    half = part // 2
    inner = jnp.concatenate(
        [
            jnp.concatenate([w_in[:, 0, (side * major + i) * half :][:, :half] for side in range(2)], axis=1)
            for i in range(major)
        ]
    )
    inner = swap_major(inner.reshape(major, -1, part)).reshape(-1, part)
    inner = turn(after(jnp.concatenate([inner, cotangent[0]]), background))
    cotangent = after(cotangent[0], packed)

    full_o = lax.all_gather(output_weight, EVERY, axis=0, tiled=True)
    near_major = jnp.arange(major, dtype=jnp.int32) ^ my_major

    table = lax.dynamic_slice_in_dim(bias_table, my_major * heads, heads, axis=1).astype(F32)
    near = pl.pallas_call(
        functools.partial(near_bias_kernel, edges, rows),
        in_specs=[scalars()],
        out_shape=jax.ShapeDtypeStruct((heads, 3 * rows, rows), F32),
    )(table)
    far = jnp.stack([table[15], table[31]])
    near_minor = jnp.arange(minor, dtype=jnp.int32) ^ lax.axis_index(MINOR)
    key_blocks = (near_minor // rest)[:, None] * major + near_major[None, :]
    key_blocks = (key_blocks * rest + (near_minor % rest)[:, None]).reshape(-1)
    block_ids = jnp.arange(-1, ring + 1, dtype=jnp.int32)
    found = key_blocks[None, :] == block_ids[:, None]
    key_slots = jnp.where(found, jnp.arange(ring, dtype=jnp.int32)[None, :], 0)
    key_slots = jnp.where(jnp.any(found, axis=1), jnp.sum(key_slots, axis=1), ring)
    places = (key_blocks[:major], key_blocks, key_slots)

    expert_ids = jnp.arange(experts, dtype=jnp.int32)
    slot_ids = jnp.arange(capacity, dtype=jnp.int32)

    def selection(token_routes, token_slots, place):
        chosen = (
            ((token_routes ^ place)[None, None, :] == expert_ids[:, None, None])
            & (token_slots[None, None, :] == slot_ids[None, :, None])
        ).astype(BF16)
        return chosen.reshape(experts * capacity, rows)

    def by_expert(chosen, value):
        sent = dot_n(chosen, value).astype(BF16)
        return [sent[i * capacity : (i + 1) * capacity] for i in range(experts)]

    def gather_rows(parts):
        return exchange([jnp.concatenate(parts)] * major, "mj")

    def sum_parts(value):
        value = value.reshape(major, experts * capacity, width)
        return exchange([value[i] for i in range(major)], "mj")

    def send_back(parts):
        total = sum(part.astype(F32) for part in parts).astype(BF16)
        total = total.reshape(experts, capacity, width)
        return exchange([total[i] for i in range(experts)], ("ey", "gh"))

    sent = by_expert(selection(routes[0], slots[0], lax.axis_index(("ey", "ec"))), cotangent)
    cot_parts = turn_exchange(sent)
    routes, slots = numbers[0], numbers[1]
    select = selection(routes, slots, my_exp)

    column_hidden = column.reshape(major * rows, width).astype(F32)
    column_unit = unit(column_hidden)
    normed = (column_hidden * column_unit * gain_first).astype(BF16)
    projected = dot_n(normed, packed).astype(BF16)
    others = other_minor(projected, kv_width)
    outer = gather_minor(outer).reshape(part, width)
    attended_low, attended_wide, lse = forward_attention(
        projected, others, near, far, places, heads, rows
    )
    attended_low, cot_parts, inner, outer = lax.optimization_barrier(
        (attended_low, cot_parts, inner, outer)
    )
    my_cotangent = inner[-rows:]
    attended = exchange([attended_low[i * rows : (i + 1) * rows] for i in range(major)], "mj")
    attended = ordered(jnp.stack(attended), my_major)
    attended = jnp.transpose(attended, (1, 0, 2)).reshape(rows, features)

    hidden = tokens.astype(F32)
    middle = hidden + dot_n(attended, full_o)
    middle_unit = unit(middle)
    mixed = (middle * middle_unit * gain_second).astype(BF16)
    chances = jax.nn.softmax(dot_n(mixed, full_router), axis=-1)
    route_mask = (routes[:, None] == expert_ids[None, :]).astype(F32)
    gate = jnp.sum(chances * route_mask, axis=-1, keepdims=True)

    mixed_parts = exchange(by_expert(select, mixed), ("ey", "gh"))
    cot_rows = gather_rows(after(cot_parts, attended))
    inner = after(inner[:-rows], attended)
    inner = gather_minor(inner.reshape(major, -1, part)).reshape(2, rest, major, -1, part)
    inner = jnp.transpose(inner, (0, 2, 1, 3, 4)).reshape(width, part)
    buffer = gather_rows(mixed_parts)
    cot_rows = jnp.concatenate(after(cot_rows, mixed_parts))
    buffer = jnp.concatenate(lax.optimization_barrier(buffer))
    row_chances = jax.nn.softmax(dot_n(buffer, full_router), axis=-1)
    row_mask = (expert_ids == my_exp).astype(F32)[None, :]
    row_gate = jnp.sum(row_chances * row_mask, axis=-1, keepdims=True)
    preact = dot_n(buffer, inner)
    cumulative = 0.5 * (1.0 + lax.erf(preact * math.sqrt(0.5)))
    density = jnp.exp(-0.5 * preact * preact) * (1.0 / math.sqrt(2.0 * math.pi))
    activated_wide = preact * cumulative
    grad_activated = dot_t(cot_rows, outer)
    grad_preact = (row_gate * grad_activated * (cumulative + preact * density)).astype(BF16)
    row_grad_gate = jnp.sum(activated_wide * grad_activated, axis=-1, keepdims=True)
    grad_logits = (row_gate * row_grad_gate * (row_mask - row_chances)).astype(BF16)
    grad_mixed = dot_t(grad_preact, inner) + dot_t(grad_logits, full_router)
    grad_mixed = grad_mixed.astype(BF16)
    buffer, activated_wide, grad_preact, cot_rows = after(
        (buffer, activated_wide, grad_preact, cot_rows), grad_mixed
    )

    activated = activated_wide.astype(BF16)
    produced = dot_n(activated, outer).astype(BF16)
    grad_router = dot_0(buffer, grad_logits)
    gated_rows = (row_gate * cot_rows.astype(F32)).astype(BF16)
    grad_outer = dot_0(activated, gated_rows).reshape(minor, -1, width)
    grad_inner = dot_0(buffer, grad_preact).reshape(2, major, rest, -1, part)
    grad_inner = jnp.transpose(grad_inner, (0, 2, 1, 3, 4)).reshape(minor, -1, part)
    grad_outer, grad_inner, produced, grad_parts = lax.optimization_barrier(
        (split_minor(grad_outer), split_minor(grad_inner), produced, sum_parts(grad_mixed))
    )
    grad_parts = send_back(grad_parts)
    grad_outer = sum_split(grad_outer).astype(BF16)
    grad_inner = sum_split(grad_inner).astype(BF16).reshape(major, -1, part)
    grad_parts, grad_outer, grad_inner = lax.optimization_barrier((grad_parts, grad_outer, grad_inner))
    grad_mixed = dot_0(select, jnp.concatenate(grad_parts))
    grad_outer = turn(grad_outer)

    grad_z = my_cotangent.astype(F32)
    grad_gain_second = jnp.sum(grad_mixed * middle * middle_unit, axis=0)
    scaled = grad_mixed * gain_second
    grad_middle = (
        grad_z
        + middle_unit * scaled
        - middle * middle_unit**3 * jnp.mean(scaled * middle, axis=-1, keepdims=True)
    )
    grad_branch = grad_middle.astype(BF16)
    grad_attended = dot_t(grad_branch, full_o).astype(BF16)
    grad_attended = jnp.transpose(grad_attended.reshape(rows, major, q_width), (1, 0, 2))
    grad_attended = ordered(grad_attended, my_major)
    grad_attended = jnp.concatenate(exchange([grad_attended[i] for i in range(major)], "mj"))
    produced_parts = sum_parts(after(produced, grad_attended))
    grad_inner = swap_major(after(grad_inner, grad_mixed)).reshape(-1, part)
    grad_o = core_sum(dot_0(attended, grad_branch))

    dq, dkv, dkv_low, near_sum, far_sum = backward_attention(
        projected, grad_attended, attended_wide, others, near, far, places, lse, heads, rows
    )
    dq, dkv, dkv_low, grad_outer, grad_inner, produced_parts, grad_o = lax.optimization_barrier(
        (dq, dkv, dkv_low, grad_outer, grad_inner, produced_parts, grad_o)
    )
    grad_o = scatter_rows(grad_o)
    grad_inner = turn(grad_inner)
    dkv = sum_nearest(dkv, dkv_low.reshape(minor - 1, major * rows, kv_width)).astype(BF16)
    grad_projected = jnp.concatenate([dkv, dq], axis=1)
    grad_normed = dot_t(grad_projected, packed)
    parts = grad_normed.astype(BF16).reshape(major, rows, width)
    produced_parts, near_sum, normed, grad_projected = after(
        (produced_parts, near_sum, normed, grad_projected), parts
    )
    produced_parts = send_back(produced_parts)

    sums = pl.pallas_call(
        functools.partial(bucket_sum_kernel, edges, rows),
        out_shape=jax.ShapeDtypeStruct((heads, 128), F32),
    )(near_sum, far_sum)
    grad_table = sums[:, :32].T
    grad_gain_first = jnp.sum(grad_normed * column_hidden * column_unit, axis=0)
    grad_parts = exchange([parts[i] for i in range(major)], "mj")
    grad_parts, grad_inner, grad_outer = lax.optimization_barrier((grad_parts, grad_inner, grad_outer))
    grad_normed = sum(part.astype(F32) for part in grad_parts)
    produced = dot_0(select, jnp.concatenate(after(produced_parts, grad_normed)))
    layer_output = (middle + gate * produced).astype(BF16)
    hidden_unit = unit(hidden)
    scaled = grad_normed * gain_first
    grad_activations = (
        grad_middle
        + hidden_unit * scaled
        - hidden * hidden_unit**3 * jnp.mean(scaled * hidden, axis=-1, keepdims=True)
    ).astype(BF16)
    both = turn(jnp.concatenate([grad_activations, layer_output]))
    grad_activations, layer_output = both[None, :rows], both[None, rows:]

    buckets = bias_table.shape[0]
    table_columns = buckets * heads // shard
    flat_table = jnp.tile(
        grad_table.reshape(shard, table_columns), (width // shard, 1)
    )
    small = jnp.concatenate(
        [grad_router, grad_gain_first[:, None], grad_gain_second[:, None], flat_table], axis=1
    )
    small = jnp.pad(small, ((0, 0), (kv_width + q_width, extra_width - small.shape[1])))
    arrived = scatter_rows(core_sum(dot_0(normed, grad_projected) + small))
    arrived = arrived.reshape(4, major, rest, shard, packed_width)
    arrived = jnp.sum(arrived, axis=(0, 2))
    key_value = arrived[:, :, :kv_width].reshape(major, shard, heads, 2, head_dim)

    def side_by_side(value):
        return jnp.transpose(value.reshape(major, shard, q_width), (1, 0, 2)).reshape(shard, features)

    grad_query = side_by_side(arrived[:, :, kv_width : kv_width + q_width])
    grad_key = side_by_side(key_value[:, :, :, 0, :])
    grad_v = side_by_side(key_value[:, :, :, 1, :])
    small = arrived[:, :, kv_width + q_width :]
    summed = jnp.sum(small[:, :, : experts + 2], axis=0)
    grad_table = small[:, :, experts + 2 : experts + 2 + table_columns]
    grad_table = jnp.transpose(grad_table.reshape(major, buckets, heads), (1, 0, 2))
    grad_o = jnp.sum(grad_o, axis=0)
    grad_inner = unpack(grad_inner.reshape(major, w_in.shape[0], part), 2)
    grad_outer = unpack(grad_outer[None], 1)
    return (
        layer_output,
        grad_activations,
        jnp.concatenate([grad_query, grad_key], axis=1),
        grad_v,
        grad_o,
        summed[:, experts],
        summed[:, experts + 1],
        summed[:, :experts],
        grad_table.reshape(buckets, head_count),
        grad_inner,
        grad_outer,
    )


def solution(mesh):
    groups, ring = mesh.shape["exp"], mesh.shape["ctx"]
    split = Mesh(mesh.devices.reshape(groups // 2, 2, 2, 4, ring // 8), EVERY)
    exp, ctx = ("ey", "ec"), ("gh", "mj", "rs")
    tokens, rows, experts = P(exp, ctx, None), P(EVERY, None), P(ctx, exp, None)
    return jax.shard_map(
        per_device,
        mesh=split,
        in_specs=(
            tokens,
            tokens,
            rows,
            rows,
            rows,
            P(EVERY),
            P(EVERY),
            rows,
            P(),
            experts,
            experts,
            P(exp, ctx),
            P(exp, ctx),
        ),
        out_specs=(
            tokens,
            tokens,
            rows,
            rows,
            rows,
            P(EVERY),
            P(EVERY),
            rows,
            P(),
            experts,
            experts,
        ),
        check_vma=False,
    )
```

time: 380 us -> 301 us (0.79)
  blocking collectives: 49.7 us -> 0 us
  waiting for transfers between devices: 106 us -> 63.8 us
  starting transfers between devices: 64.3 us -> 102 us
  local copies, waits for them, and re-layouts: 48.5 us -> 28.5 us
  matrix products: 35.1 us -> 23.1 us
  Pallas kernels: 27.4 us -> 32.7 us
    all_to_all x13 -> x4, waiting for transfers between devices: 93.5 us -> 0.01 us  [the longest x2 0.01 us: swap_major(): return lax.all_to_all(value, 'mj', 0, 0, tiled=True)]
    ppermute x5 -> x56, starting transfers between devices: 5.17 us -> 85.4 us  [the longest x36 41.2 us: exchange(): lax.ppermute(parts[step], axis, [(source, source ^ step) for source in ra...]
    ppermute x5 -> x56, waiting for transfers between devices: 11.8 us -> 63.1 us  [the longest x36 36.3 us: exchange(): lax.ppermute(parts[step], axis, [(source, source ^ step) for source in ra...]
    all_gather x2 -> x0, blocking collectives: 49.7 us -> none  [the longest x1 37 us: per_device(): lax.all_gather(sent, 'major', axis=1)]
    all_to_all x13 -> x4, starting transfers between devices: 59.1 us -> 16.5 us  [the longest x2 8.65 us: scatter_rows(): return lax.all_to_all(value, REST, 0, 0, tiled=True).astype(F32)]
    reduce_sum x6 -> x3, other arithmetic: 8.02 us -> 0.86 us  [the longest x1 0.72 us: per_device(): grad_o = jnp.sum(grad_o, axis=0)]
    reshape x6 -> x0, local copies, waits for them, and re-layouts: 6.05 us -> none  [the longest x1 1.93 us: per_device(): jnp.pad(grad_attended, ((0, 0), (0, 0), (head_dim, 0)))]
    convert_element_type x8 -> x0, local copies, waits for them, and re-layouts: 5.58 us -> none  [the longest x2 3.19 us: per_device(): jnp.transpose(grad_inner, (1, 0, 2)).reshape(-1, 1, major * quarter)]
  transfers between devices with their start and end apart: 19 -> 61, of which waited for: 12 -> 21; matrix products, arithmetic and copies ran while one was open for 22% -> 22% of each run, Pallas kernels for 7% -> 11%
where the time goes in v2:
time: 301 us; the launch traced here: 299 us
  starting transfers between devices  102 us (34%)
  waiting for transfers between devices  63.8 us (21%)
  other arithmetic  33.2 us (11%)
  Pallas kernels  32.7 us (11%)
  local copies, waits for them, and re-layouts  28.5 us (9%)
  matrix products  23.1 us (8%)
  between operations  15.6 us (5%)
    ppermute x36, starting transfers between devices, exchange(): lax.ppermute(parts[step], axis, [(source, source ^ step) for source in ra...  41.2 us
    ppermute x36, waiting for transfers between devices, exchange(): lax.ppermute(parts[step], axis, [(source, source ^ step) for source in ra...  36.3 us
    ppermute x5, starting transfers between devices, turn(): return lax.ppermute(value, ('ec', 'gh'), [(0, 0), (1, 2), (2, 1), (3, 3)])  21.5 us
    ppermute x11, starting transfers between devices, swap(): return lax.ppermute(value, axis, [(0, 1), (1, 0)])  16.8 us
    ppermute x5, waiting for transfers between devices, turn(): return lax.ppermute(value, ('ec', 'gh'), [(0, 0), (1, 2), (2, 1), (3, 3)])  16.4 us
    pallas_call x1, Pallas kernels, backward_attention(): pl.pallas_call(functools.partial(attention_back_kernel, heads, rows), gri...  12.6 us
    ppermute x11, waiting for transfers between devices, swap(): return lax.ppermute(value, axis, [(0, 1), (1, 0)])  10.4 us
    pallas_call x1, Pallas kernels, forward_attention(): pl.pallas_call(functools.partial(attention_kernel, heads, rows), grid=(st...  9.92 us
  transfers between devices with their start and end apart: 61, of which 21 were waited for; matrix products, arithmetic and copies ran while one was open for 22% of the time, Pallas kernels for 11%

profile of v2, /device:TPU:1, one launch (start us, length us, event | category | flops | bytes accessed | tf_op | source)
XLA Modules:
  0.0 298.9 jit_solution(5336792148536722099)
XLA Ops:
  9.4 2.1 pad_maximum_fusion.3
  11.5 5.6 %collective-permute-start = (bf16[528,768]{1,0:T(8,128)(2,1)}, bf16[528,768]{1,0:T(8,128)(2,1)S(1)}, u32[]{:S(2)}, u32[]{:S(2)}) collective-permute-start(bf16[528,768]{1,0:T(8,128)(2,1)} %pad_maximum_fusion.3), channel_id=1, source_target_pairs={{0,0},{4,8},{8,4},{12,12},{1,1},{5,9},{9,5},{13,13},{2,2},{6,10},{... | collective-permute-start | bytes 2433032 | tf_op jit(solution)/shard_map/ppermute | solution.py:355
  18.4 2.3 collective-permute-start.6
  22.3 3.5 %all-to-all-start = ((bf16[4,96,768]{2,1,0:T(8,128)(2,1)}), bf16[4,96,768]{2,1,0:T(8,128)(2,1)S(1)}, u32[]{:S(2)}, u32[]{:S(2)}) async-start(bf16[4,96,768]{2,1,0:T(8,128)(2,1)} %bitcast.38), calls=%async_computation | async-start | bytes 1179648 | tf_op jit(solution)/shard_map/all_to_all | solution.py:440
  28.0 2.4 collective-permute-done.6
  31.7 8.7 %collective-permute-done.7 = bf16[4,24,640]{2,1,0:T(8,128)(2,1)S(1)} collective-permute-done((bf16[4,24,640]{2,1,0:T(8,128)(2,1)S(1)}, bf16[4,24,640]{2,1,0:T(8,128)(2,1)S(1)}, u32[]{:S(2)}, u32[]{:S(2)}) %collective-permute-start.7) | collective-permute-done | bytes 122912 | tf_op jit(solution)/shard_map/ppermute | solution.py:351
  43.0 2.3 shard_map.215.near_ref
  47.7 2.5 collective-permute-start.9
  56.6 3.7 %collective-permute-start.15 = (bf16[512,768]{1,0:T(8,128)(2,1)S(1)}, bf16[512,768]{1,0:T(8,128)(2,1)S(1)}, u32[]{:S(2)}, u32[]{:S(2)}) collective-permute-start(bf16[512,768]{1,0:T(8,128)(2,1)S(1)} %pad_maximum_fusion.5), channel_id=1, source_target_pairs={{0,0},{4,8},{8,4},{12,12},{1,1},{5,9},{9,5},{13,13},{2,2},{6,10},{... | collective-permute-start | bytes 2359304 | tf_op jit(solution)/shard_map/ppermute | solution.py:355
  62.1 2.9 collective-permute-done.3
  75.4 3.4 %collective-permute-start.11 = (bf16[40,768]{1,0:T(8,128)(2,1)S(1)}, bf16[40,768]{1,0:T(8,128)(2,1)S(1)}, u32[]{:S(2)}, u32[]{:S(2)}) collective-permute-start(bf16[40,768]{1,0:T(8,128)(2,1)S(1)} %get-tuple-element.266), channel_id=1, source_target_pairs={{0,0},{4,8},{8,4},{12,12},{16,16},{20,24},{24,20},{28,28},{1,1},{5... | collective-permute-start | bytes 184328 | tf_op jit(solution)/shard_map/ppermute | solution.py:387
  78.7 9.9 %shard_map.216 = (bf16[512,192]{1,0:T(8,128)(2,1)}, f32[512,384]{1,0:T(8,128)}, f32[4,3,128]{2,1,0:T(4,128)}) custom-call(s32[4]{0:T(128)} %slice_bitcast_fusion.14.block_ref, s32[8]{0:T(128)} %copy-done.47, s32[10]{0:T(128)} %broadcast_select_fusion.place_ref, f32[2,3]{1,0:T(2,128)} %pad_maximum_fusion.19.far_ref, bf16[512,640]{1,0:T(8,128)(2,1)} %copy-done.45, ...), custom_call_target="tpu_custom_call" | custom-call | flops 805306368 | bytes 3145728 | tf_op jit(solution)/shard_map/pallas_call | solution.py:280
  90.0 2.0 collective-permute-start.18
  99.7 1.9 collective-permute-start.28
  103.6 1.7 multiply_reduce_fusion.3
  105.6 3.9 %collective-permute-start.22 = (bf16[40,768]{1,0:T(8,128)(2,1)S(1)}, bf16[40,768]{1,0:T(8,128)(2,1)S(1)}, u32[]{:S(2)}, u32[]{:S(2)}) collective-permute-start(bf16[40,768]{1,0:T(8,128)(2,1)S(1)} %get-tuple-element.260), channel_id=1, source_target_pairs={{0,20},{4,16},{16,4},{20,0},{1,21},{5,17},{17,5},{21,1},{2,22},{6,... | collective-permute-start | bytes 184328 | tf_op jit(solution)/shard_map/ppermute | solution.py:361
  112.5 2.6 collective-permute-start.20
  116.8 2.5 collective-permute-start.24
  123.2 5.6 %collective-permute-done.24 = bf16[160,768]{1,0:T(8,128)(2,1)S(1)} collective-permute-done((bf16[160,768]{1,0:T(8,128)(2,1)S(1)}, bf16[160,768]{1,0:T(8,128)(2,1)S(1)}, u32[]{:S(2)}, u32[]{:S(2)}) %collective-permute-start.24) | collective-permute-done | bytes 245792 | tf_op jit(solution)/shard_map/ppermute | solution.py:361
  137.4 3.4 %collective-permute-start.31 = (bf16[160,768]{1,0:T(8,128)(2,1)S(1)}, bf16[160,768]{1,0:T(8,128)(2,1)S(1)}, u32[]{:S(2)}, u32[]{:S(2)}) collective-permute-start(bf16[160,768]{1,0:T(8,128)(2,1)S(1)} %get-tuple-element.233), channel_id=1, source_target_pairs={{0,2},{1,3},{2,0},{3,1},{4,6},{5,7},{6,4},{7,5},{8,10},{9,11},{10,... | collective-permute-start | bytes 737288 | tf_op jit(solution)/shard_map/ppermute | solution.py:361
  140.8 1.9 convolution_convert_fusion
  143.3 7.5 %collective-permute-done.31 = bf16[160,768]{1,0:T(8,128)(2,1)S(1)} collective-permute-done((bf16[160,768]{1,0:T(8,128)(2,1)S(1)}, bf16[160,768]{1,0:T(8,128)(2,1)S(1)}, u32[]{:S(2)}, u32[]{:S(2)}) %collective-permute-start.31) | collective-permute-done | bytes 245792 | tf_op jit(solution)/shard_map/ppermute | solution.py:361
  153.1 2.0 collective-permute-start.35
  164.9 4.4 %all-to-all-start.1 = ((bf16[4,96,768]{2,1,0:T(8,128)(2,1)}), bf16[4,96,768]{2,1,0:T(8,128)(2,1)}, u32[]{:S(2)}, u32[]{:S(2)}) async-start(bf16[4,96,768]{2,1,0:T(8,128)(2,1)} %bitcast.56), calls=%async_computation.1 | async-start | bytes 1179648 | tf_op jit(solution)/shard_map/all_to_all | solution.py:440
  171.5 2.1 collective-permute-start.40
  175.6 3.0 %collective-permute-start.45 = (bf16[2,192,768]{2,1,0:T(8,128)(2,1)}, bf16[2,192,768]{2,1,0:T(8,128)(2,1)}, u32[]{:S(2)}, u32[]{:S(2)}) collective-permute-start(bf16[2,192,768]{2,1,0:T(8,128)(2,1)} %fusion.23), channel_id=1, source_target_pairs={{0,8},{8,0},{1,9},{9,1},{2,10},{10,2},{3,11},{11,3},{4,12},{12,4},... | collective-permute-start | bytes 1769480 | tf_op jit(solution)/shard_map/ppermute | solution.py:351
  180.0 1.9 collective-permute-start.41
  183.6 2.1 fusion.75
  185.6 2.4 collective-permute-start.44
  188.5 12.6 %shard_map.217 = (bf16[512,256]{1,0:T(8,128)(2,1)}, f32[512,384]{1,0:T(8,128)}, bf16[512,384]{1,0:T(8,128)(2,1)}, f32[3,384,128]{2,1,0:T(8,128)}, f32[3,2,128]{2,1,0:T(2,128)}) custom-call(s32[4]{0:T(128)} %slice_bitcast_fusion.14.block_ref, s32[8]{0:T(128)} %copy-done.47, s32[10]{0:T(128)} %broadcast_select_fusion.place_ref, ...), custom_call_target="tpu_custom_call" | custom-call | flops 2013265920 | bytes 3145728 | tf_op jit(solution)/shard_map/pallas_call | solution.py:313
  201.2 2.1 fusion.16
  203.3 4.7 %collective-permute-start.46 = (bf16[512,384]{1,0:T(8,128)(2,1)}, bf16[512,384]{1,0:T(8,128)(2,1)S(1)}, u32[]{:S(2)}, u32[]{:S(2)}) collective-permute-start(bf16[512,384]{1,0:T(8,128)(2,1)} %get-tuple-element.145), channel_id=1, source_target_pairs={{0,8},{8,0},{1,9},{9,1},{2,10},{10,2},{3,11},{11,3},{4,12},{12,4},... | collective-permute-start | bytes 1179656 | tf_op jit(solution)/shard_map/ppermute | solution.py:351
  208.6 2.1 fusion.70
  210.7 4.3 %all-to-all-start.3 = ((bf16[16,24,768]{2,1,0:T(8,128)(2,1)}), bf16[16,24,768]{2,1,0:T(8,128)(2,1)S(1)}, u32[]{:S(2)}, u32[]{:S(2)}) async-start(bf16[16,24,768]{2,1,0:T(8,128)(2,1)} %bitcast.227), calls=%async_computation.3 | async-start | bytes 1179648 | tf_op jit(solution)/shard_map/all_to_all | solution.py:454
  215.0 4.9 %collective-permute-start.50 = (bf16[384,768]{1,0:T(8,128)(2,1)}, bf16[384,768]{1,0:T(8,128)(2,1)}, u32[]{:S(2)}, u32[]{:S(2)}) collective-permute-start(bf16[384,768]{1,0:T(8,128)(2,1)} %bitcast.63), channel_id=1, source_target_pairs={{0,0},{4,8},{8,4},{12,12},{1,1},{5,9},{9,5},{13,13},{2,2},{6,10},{... | collective-permute-start | bytes 1769480 | tf_op jit(solution)/shard_map/ppermute | solution.py:355
  221.1 3.1 %fusion.12 = (f32[768]{0:T(1024)S(1)}, bf16[512,768]{1,0:T(8,128)(2,1)}, bf16[512,768]{1,0:T(8,128)(2,1)}) fusion(f32[512]{0:T(512)S(1)} %copy-done.37, bf16[1,128,768]{2,1,0:T(8,128)(2,1)} %bitcast.6, bf16[1,128,768]{2,1,0:T(8,128)(2,1)S(1)} %bitcast.246, bf16[1,128,768]{2,1,0:T(8,128)(2,1)} %bitcast.4, bf16[1,128,768]{2,1,0:T(8,128)(2,1)S(1)} %get-tuple-element.238, ...), kind=kOutput, calls=%fused_computation.26 | convolution fusion | flops 508951808 | bytes 4005888 | tf_op jit(solution)/shard_map/dot_general | solution.py:30
  224.2 3.2 %shard_map.218 = f32[3,128]{1,0:T(4,128)} custom-call(f32[3,384,128]{2,1,0:T(8,128)} %get-tuple-element.168.near_ref, f32[3,2,128]{2,1,0:T(2,128)} %get-tuple-element.169.far_ref), custom_call_target="tpu_custom_call" | custom-call | tf_op jit(solution)/shard_map/pallas_call | solution.py:707
  230.5 4.4 %collective-permute-start.53 = (bf16[40,768]{1,0:T(8,128)(2,1)}, bf16[40,768]{1,0:T(8,128)(2,1)}, u32[]{:S(2)}, u32[]{:S(2)}) collective-permute-start(bf16[40,768]{1,0:T(8,128)(2,1)} %get-tuple-element.251), channel_id=1, source_target_pairs={{0,20},{4,16},{16,4},{20,0},{1,21},{5,17},{17,5},{21,1},{2,22},{6,... | collective-permute-start | bytes 184328 | tf_op jit(solution)/shard_map/ppermute | solution.py:361
  235.9 2.1 collective-permute-start.49
  238.6 1.9 pad_add_fusion
  240.7 5.2 %collective-permute-done.50 = bf16[384,768]{1,0:T(8,128)(2,1)} collective-permute-done((bf16[384,768]{1,0:T(8,128)(2,1)}, bf16[384,768]{1,0:T(8,128)(2,1)}, u32[]{:S(2)}, u32[]{:S(2)}) %collective-permute-start.50) | collective-permute-done | bytes 589856 | tf_op jit(solution)/shard_map/ppermute | solution.py:355
  247.2 3.5 %collective-permute-done.49 = bf16[128,768]{1,0:T(8,128)(2,1)S(1)} collective-permute-done((bf16[128,768]{1,0:T(8,128)(2,1)}, bf16[128,768]{1,0:T(8,128)(2,1)S(1)}, u32[]{:S(2)}, u32[]{:S(2)}) %collective-permute-start.49) | collective-permute-done | bytes 196640 | tf_op jit(solution)/shard_map/ppermute | solution.py:361
  250.7 4.1 %collective-permute-done.48 = bf16[128,768]{1,0:T(8,128)(2,1)S(1)} collective-permute-done((bf16[128,768]{1,0:T(8,128)(2,1)}, bf16[128,768]{1,0:T(8,128)(2,1)S(1)}, u32[]{:S(2)}, u32[]{:S(2)}) %collective-permute-start.48) | collective-permute-done | bytes 196640 | tf_op jit(solution)/shard_map/ppermute | solution.py:361
  258.2 4.4 %all-to-all-start.2 = ((bf16[16,24,640]{2,1,0:T(8,128)(2,1)}), bf16[16,24,640]{2,1,0:T(8,128)(2,1)S(1)}, u32[]{:S(2)}, u32[]{:S(2)}) async-start(bf16[16,24,640]{2,1,0:T(8,128)(2,1)} %bitcast.84), calls=%async_computation.2 | async-start | bytes 983040 | tf_op jit(solution)/shard_map/all_to_all | solution.py:454
  263.7 5.4 %collective-permute-start.54 = (bf16[256,768]{1,0:T(8,128)(2,1)S(1)}, bf16[256,768]{1,0:T(8,128)(2,1)S(1)}, u32[]{:S(2)}, u32[]{:S(2)}) collective-permute-start(bf16[256,768]{1,0:T(8,128)(2,1)S(1)} %pad_maximum_fusion.8), channel_id=1, source_target_pairs={{0,0},{4,8},{8,4},{12,12},{1,1},{5,9},{9,5},{13,13},{2,2},{6,10},{... | collective-permute-start | bytes 1179656 | tf_op jit(solution)/shard_map/ppermute | solution.py:355
  269.1 2.4 shard_map.219
  271.4 2.3 shard_map.220
  273.8 11.2 %collective-permute-done.54 = bf16[256,768]{1,0:T(8,128)(2,1)S(1)} collective-permute-done((bf16[256,768]{1,0:T(8,128)(2,1)S(1)}, bf16[256,768]{1,0:T(8,128)(2,1)S(1)}, u32[]{:S(2)}, u32[]{:S(2)}) %collective-permute-start.54) | collective-permute-done | bytes 393248 | tf_op jit(solution)/shard_map/ppermute | solution.py:355
  (367 shorter events, 99.4 us)
Async XLA Ops:
  7.2 96.3 %all-gather.2.cloned.1.call-start = ((), (), s32[]{:S(2)}) async-start(), calls=%async_computation.4 | async-start | bytes 1216512 | tf_op jit(solution)/shard_map/all_gather | solution.py:556
  11.5 38.7 %collective-permute-start = (bf16[528,768]{1,0:T(8,128)(2,1)}, bf16[528,768]{1,0:T(8,128)(2,1)S(1)}, u32[]{:S(2)}, u32[]{:S(2)}) collective-permute-start(bf16[528,768]{1,0:T(8,128)(2,1)} %pad_maximum_fusion.3), channel_id=1, source_target_pairs={{0,0},{4,8},{8,4},{12,12},{1,1},{5,9},{9,5},{13,13},{2,2},{6,10},{... | collective-permute-start | bytes 2433032 | tf_op jit(solution)/shard_map/ppermute | solution.py:355
  18.4 12.0 %collective-permute-start.6 = (bf16[24,640]{1,0:T(8,128)(2,1)S(1)}, bf16[24,640]{1,0:T(8,128)(2,1)S(1)}, u32[]{:S(2)}, u32[]{:S(2)}) collective-permute-start(bf16[24,640]{1,0:T(8,128)(2,1)S(1)} %get-tuple-element.272), channel_id=1, source_target_pairs={{0,3},{1,2},{2,1},{3,0},{4,7},{5,6},{6,5},{7,4},{8,11},{9,10},{10,... | collective-permute-start | bytes 92168 | tf_op jit(solution)/shard_map/ppermute | solution.py:361
  20.7 10.3 %collective-permute-start.5 = (bf16[24,640]{1,0:T(8,128)(2,1)S(1)}, bf16[24,640]{1,0:T(8,128)(2,1)S(1)}, u32[]{:S(2)}, u32[]{:S(2)}) collective-permute-start(bf16[24,640]{1,0:T(8,128)(2,1)S(1)} %get-tuple-element.273), channel_id=1, source_target_pairs={{0,2},{1,3},{2,0},{3,1},{4,6},{5,7},{6,4},{7,5},{8,10},{9,11},{10,... | collective-permute-start | bytes 92168 | tf_op jit(solution)/shard_map/ppermute | solution.py:361
  20.9 10.2 %collective-permute-start.4 = (bf16[24,640]{1,0:T(8,128)(2,1)S(1)}, bf16[24,640]{1,0:T(8,128)(2,1)S(1)}, u32[]{:S(2)}, u32[]{:S(2)}) collective-permute-start(bf16[24,640]{1,0:T(8,128)(2,1)S(1)} %get-tuple-element.274), channel_id=1, source_target_pairs={{0,1},{1,0},{2,3},{3,2},{4,5},{5,4},{6,7},{7,6},{8,9},{9,8},{10,11... | collective-permute-start | bytes 92168 | tf_op jit(solution)/shard_map/ppermute | solution.py:361
  22.3 34.1 %all-to-all-start = ((bf16[4,96,768]{2,1,0:T(8,128)(2,1)}), bf16[4,96,768]{2,1,0:T(8,128)(2,1)S(1)}, u32[]{:S(2)}, u32[]{:S(2)}) async-start(bf16[4,96,768]{2,1,0:T(8,128)(2,1)} %bitcast.38), calls=%async_computation | async-start | bytes 1179648 | tf_op jit(solution)/shard_map/all_to_all | solution.py:440
  31.6 8.8 %collective-permute-start.7 = (bf16[4,24,640]{2,1,0:T(8,128)(2,1)S(1)}, bf16[4,24,640]{2,1,0:T(8,128)(2,1)S(1)}, u32[]{:S(2)}, u32[]{:S(2)}) collective-permute-start(bf16[4,24,640]{2,1,0:T(8,128)(2,1)S(1)} %gather_fusion), channel_id=1, source_target_pairs={{0,4},{4,0},{1,5},{5,1},{2,6},{6,2},{3,7},{7,3},{8,12},{12,8},{9,1... | collective-permute-start | bytes 368648 | tf_op jit(solution)/shard_map/ppermute | solution.py:351
  40.5 6.5 %collective-permute-start.8 = (bf16[2,4,24,640]{3,2,1,0:T(8,128)(2,1)S(1)}, bf16[2,4,24,640]{3,2,1,0:T(8,128)(2,1)S(1)}, u32[]{:S(2)}, u32[]{:S(2)}) collective-permute-start(bf16[2,4,24,640]{3,2,1,0:T(8,128)(2,1)S(1)} %pad_maximum_fusion.11), channel_id=1, source_target_pairs={{0,16},{16,0},{1,17},{17,1},{2,18},{18,2},{3,19},{19,3},{4,20},{20... | collective-permute-start | bytes 737288 | tf_op jit(solution)/shard_map/ppermute | solution.py:351
  47.7 8.8 %collective-permute-start.9 = (bf16[2,2,4,24,640]{4,3,2,1,0:T(8,128)(2,1)S(1)}, bf16[2,2,4,24,640]{4,3,2,1,0:T(8,128)(2,1)}, u32[]{:S(2)}, u32[]{:S(2)}) collective-permute-start(bf16[2,2,4,24,640]{4,3,2,1,0:T(8,128)(2,1)S(1)} %bitcast.228), channel_id=1, source_target_pairs={{0,8},{8,0},{1,9},{9,1},{2,10},{10,2},{3,11},{11,3},{4,12},{12,4},... | collective-permute-start | bytes 1474568 | tf_op jit(solution)/shard_map/ppermute | solution.py:351
  51.0 11.1 %collective-permute-start.2 = (bf16[128,768]{1,0:T(8,128)(2,1)}, bf16[128,768]{1,0:T(8,128)(2,1)S(1)}, u32[]{:S(2)}, u32[]{:S(2)}) collective-permute-start(bf16[128,768]{1,0:T(8,128)(2,1)} %get-tuple-element.239), channel_id=1, source_target_pairs={{0,2},{1,3},{2,0},{3,1},{4,6},{5,7},{6,4},{7,5},{8,10},{9,11},{10,... | collective-permute-start | bytes 589832 | tf_op jit(solution)/shard_map/ppermute | solution.py:361
  51.0 11.1 %collective-permute-start.1 = (bf16[128,768]{1,0:T(8,128)(2,1)}, bf16[128,768]{1,0:T(8,128)(2,1)}, u32[]{:S(2)}, u32[]{:S(2)}) collective-permute-start(bf16[128,768]{1,0:T(8,128)(2,1)} %get-tuple-element.239), channel_id=1, source_target_pairs={{0,1},{1,0},{2,3},{3,2},{4,5},{5,4},{6,7},{7,6},{8,9},{9,8},{10,11... | collective-permute-start | bytes 589832 | tf_op jit(solution)/shard_map/ppermute | solution.py:361
  52.0 13.1 %collective-permute-start.3 = (bf16[128,768]{1,0:T(8,128)(2,1)}, bf16[128,768]{1,0:T(8,128)(2,1)}, u32[]{:S(2)}, u32[]{:S(2)}) collective-permute-start(bf16[128,768]{1,0:T(8,128)(2,1)} %get-tuple-element.239), channel_id=1, source_target_pairs={{0,3},{1,2},{2,1},{3,0},{4,7},{5,6},{6,5},{7,4},{8,11},{9,10},{10,... | collective-permute-start | bytes 589832 | tf_op jit(solution)/shard_map/ppermute | solution.py:361
  54.5 18.3 %collective-permute-start.16 = (bf16[384,768]{1,0:T(8,128)(2,1)}, bf16[384,768]{1,0:T(8,128)(2,1)}, u32[]{:S(2)}, u32[]{:S(2)}) collective-permute-start(bf16[384,768]{1,0:T(8,128)(2,1)} %slice.409), channel_id=1, source_target_pairs={{0,8},{8,0},{1,9},{9,1},{2,10},{10,2},{3,11},{11,3},{4,12},{12,4},... | collective-permute-start | bytes 1769480 | tf_op jit(solution)/shard_map/ppermute | solution.py:351
  56.6 32.1 %collective-permute-start.15 = (bf16[512,768]{1,0:T(8,128)(2,1)S(1)}, bf16[512,768]{1,0:T(8,128)(2,1)S(1)}, u32[]{:S(2)}, u32[]{:S(2)}) collective-permute-start(bf16[512,768]{1,0:T(8,128)(2,1)S(1)} %pad_maximum_fusion.5), channel_id=1, source_target_pairs={{0,0},{4,8},{8,4},{12,12},{1,1},{5,9},{9,5},{13,13},{2,2},{6,10},{... | collective-permute-start | bytes 2359304 | tf_op jit(solution)/shard_map/ppermute | solution.py:355
  70.5 18.1 %collective-permute-start.14 = (bf16[40,768]{1,0:T(8,128)(2,1)S(1)}, bf16[40,768]{1,0:T(8,128)(2,1)S(1)}, u32[]{:S(2)}, u32[]{:S(2)}) collective-permute-start(bf16[40,768]{1,0:T(8,128)(2,1)S(1)} %get-tuple-element.263), channel_id=1, source_target_pairs={{0,20},{4,28},{8,16},{12,24},{16,4},{20,12},{24,0},{28,8},{1,21},{... | collective-permute-start | bytes 184328 | tf_op jit(solution)/shard_map/ppermute | solution.py:387
  71.6 17.0 %collective-permute-start.13 = (bf16[40,768]{1,0:T(8,128)(2,1)S(1)}, bf16[40,768]{1,0:T(8,128)(2,1)S(1)}, u32[]{:S(2)}, u32[]{:S(2)}) collective-permute-start(bf16[40,768]{1,0:T(8,128)(2,1)S(1)} %get-tuple-element.264), channel_id=1, source_target_pairs={{0,16},{4,24},{8,20},{12,28},{16,0},{20,8},{24,4},{28,12},{1,17},{... | collective-permute-start | bytes 184328 | tf_op jit(solution)/shard_map/ppermute | solution.py:387
  72.8 15.9 %collective-permute-start.12 = (bf16[40,768]{1,0:T(8,128)(2,1)S(1)}, bf16[40,768]{1,0:T(8,128)(2,1)S(1)}, u32[]{:S(2)}, u32[]{:S(2)}) collective-permute-start(bf16[40,768]{1,0:T(8,128)(2,1)S(1)} %get-tuple-element.265), channel_id=1, source_target_pairs={{0,4},{4,12},{8,0},{12,8},{16,20},{20,28},{24,16},{28,24},{1,5},{5... | collective-permute-start | bytes 184328 | tf_op jit(solution)/shard_map/ppermute | solution.py:387
  75.4 13.3 %collective-permute-start.11 = (bf16[40,768]{1,0:T(8,128)(2,1)S(1)}, bf16[40,768]{1,0:T(8,128)(2,1)S(1)}, u32[]{:S(2)}, u32[]{:S(2)}) collective-permute-start(bf16[40,768]{1,0:T(8,128)(2,1)S(1)} %get-tuple-element.266), channel_id=1, source_target_pairs={{0,0},{4,8},{8,4},{12,12},{16,16},{20,24},{24,20},{28,28},{1,1},{5... | collective-permute-start | bytes 184328 | tf_op jit(solution)/shard_map/ppermute | solution.py:387
  99.7 19.6 %collective-permute-start.29 = (bf16[160,768]{1,0:T(8,128)(2,1)}, bf16[160,768]{1,0:T(8,128)(2,1)}, u32[]{:S(2)}, u32[]{:S(2)}) collective-permute-start(bf16[160,768]{1,0:T(8,128)(2,1)} %constant_dynamic-update-slice_fusion.4), channel_id=1, source_target_pairs={{0,3},{1,2},{2,1},{3,0},{4,7},{5,6},{6,5},{7,4},{8,11},{9,10},{10,... | collective-permute-start | bytes 737288 | tf_op jit(solution)/shard_map/ppermute | solution.py:361
  99.7 19.7 %collective-permute-start.28 = (bf16[160,768]{1,0:T(8,128)(2,1)}, bf16[160,768]{1,0:T(8,128)(2,1)}, u32[]{:S(2)}, u32[]{:S(2)}) collective-permute-start(bf16[160,768]{1,0:T(8,128)(2,1)} %constant_dynamic-update-slice_fusion.4), channel_id=1, source_target_pairs={{0,2},{1,3},{2,0},{3,1},{4,6},{5,7},{6,4},{7,5},{8,10},{9,11},{10,... | collective-permute-start | bytes 737288 | tf_op jit(solution)/shard_map/ppermute | solution.py:361
  101.6 17.8 %collective-permute-start.27 = (bf16[160,768]{1,0:T(8,128)(2,1)}, bf16[160,768]{1,0:T(8,128)(2,1)}, u32[]{:S(2)}, u32[]{:S(2)}) collective-permute-start(bf16[160,768]{1,0:T(8,128)(2,1)} %constant_dynamic-update-slice_fusion.4), channel_id=1, source_target_pairs={{0,1},{1,0},{2,3},{3,2},{4,5},{5,4},{6,7},{7,6},{8,9},{9,8},{10,11... | collective-permute-start | bytes 737288 | tf_op jit(solution)/shard_map/ppermute | solution.py:361
  102.3 7.3 %collective-permute-start.26 = (bf16[4,96,768]{2,1,0:T(8,128)(2,1)S(1)}, bf16[4,96,768]{2,1,0:T(8,128)(2,1)}, u32[]{:S(2)}, u32[]{:S(2)}) collective-permute-start(bf16[4,96,768]{2,1,0:T(8,128)(2,1)S(1)} %bitcast.225), channel_id=1, source_target_pairs={{0,8},{8,0},{1,9},{9,1},{2,10},{10,2},{3,11},{11,3},{4,12},{12,4},... | collective-permute-start | bytes 1769480 | tf_op jit(solution)/shard_map/ppermute | solution.py:351
  105.6 6.8 %collective-permute-start.22 = (bf16[40,768]{1,0:T(8,128)(2,1)S(1)}, bf16[40,768]{1,0:T(8,128)(2,1)S(1)}, u32[]{:S(2)}, u32[]{:S(2)}) collective-permute-start(bf16[40,768]{1,0:T(8,128)(2,1)S(1)} %get-tuple-element.260), channel_id=1, source_target_pairs={{0,20},{4,16},{16,4},{20,0},{1,21},{5,17},{17,5},{21,1},{2,22},{6,... | collective-permute-start | bytes 184328 | tf_op jit(solution)/shard_map/ppermute | solution.py:361
  116.6 6.6 %collective-permute-start.25 = (bf16[160,768]{1,0:T(8,128)(2,1)S(1)}, bf16[160,768]{1,0:T(8,128)(2,1)S(1)}, u32[]{:S(2)}, u32[]{:S(2)}) collective-permute-start(bf16[160,768]{1,0:T(8,128)(2,1)S(1)} %pad_maximum_fusion.12), channel_id=1, source_target_pairs={{0,3},{1,2},{2,1},{3,0},{4,7},{5,6},{6,5},{7,4},{8,11},{9,10},{10,... | collective-permute-start | bytes 737288 | tf_op jit(solution)/shard_map/ppermute | solution.py:361
  116.8 12.0 %collective-permute-start.24 = (bf16[160,768]{1,0:T(8,128)(2,1)S(1)}, bf16[160,768]{1,0:T(8,128)(2,1)S(1)}, u32[]{:S(2)}, u32[]{:S(2)}) collective-permute-start(bf16[160,768]{1,0:T(8,128)(2,1)S(1)} %pad_maximum_fusion.12), channel_id=1, source_target_pairs={{0,2},{1,3},{2,0},{3,1},{4,6},{5,7},{6,4},{7,5},{8,10},{9,11},{10,... | collective-permute-start | bytes 737288 | tf_op jit(solution)/shard_map/ppermute | solution.py:361
  119.3 10.0 %collective-permute-start.23 = (bf16[160,768]{1,0:T(8,128)(2,1)S(1)}, bf16[160,768]{1,0:T(8,128)(2,1)S(1)}, u32[]{:S(2)}, u32[]{:S(2)}) collective-permute-start(bf16[160,768]{1,0:T(8,128)(2,1)S(1)} %pad_maximum_fusion.12), channel_id=1, source_target_pairs={{0,1},{1,0},{2,3},{3,2},{4,5},{5,4},{6,7},{7,6},{8,9},{9,8},{10,11... | collective-permute-start | bytes 737288 | tf_op jit(solution)/shard_map/ppermute | solution.py:361
  137.4 13.5 %collective-permute-start.31 = (bf16[160,768]{1,0:T(8,128)(2,1)S(1)}, bf16[160,768]{1,0:T(8,128)(2,1)S(1)}, u32[]{:S(2)}, u32[]{:S(2)}) collective-permute-start(bf16[160,768]{1,0:T(8,128)(2,1)S(1)} %get-tuple-element.233), channel_id=1, source_target_pairs={{0,2},{1,3},{2,0},{3,1},{4,6},{5,7},{6,4},{7,5},{8,10},{9,11},{10,... | collective-permute-start | bytes 737288 | tf_op jit(solution)/shard_map/ppermute | solution.py:361
  140.8 10.7 %collective-permute-start.30 = (bf16[160,768]{1,0:T(8,128)(2,1)S(1)}, bf16[160,768]{1,0:T(8,128)(2,1)S(1)}, u32[]{:S(2)}, u32[]{:S(2)}) collective-permute-start(bf16[160,768]{1,0:T(8,128)(2,1)S(1)} %get-tuple-element.234), channel_id=1, source_target_pairs={{0,1},{1,0},{2,3},{3,2},{4,5},{5,4},{6,7},{7,6},{8,9},{9,8},{10,11... | collective-permute-start | bytes 737288 | tf_op jit(solution)/shard_map/ppermute | solution.py:361
  153.1 6.6 %collective-permute-start.35 = (bf16[40,768]{1,0:T(8,128)(2,1)S(1)}, bf16[40,768]{1,0:T(8,128)(2,1)S(1)}, u32[]{:S(2)}, u32[]{:S(2)}) collective-permute-start(bf16[40,768]{1,0:T(8,128)(2,1)S(1)} %get-tuple-element.255), channel_id=1, source_target_pairs={{0,20},{4,16},{16,4},{20,0},{1,21},{5,17},{17,5},{21,1},{2,22},{6,... | collective-permute-start | bytes 184328 | tf_op jit(solution)/shard_map/ppermute | solution.py:361
  164.9 38.4 %all-to-all-start.1 = ((bf16[4,96,768]{2,1,0:T(8,128)(2,1)}), bf16[4,96,768]{2,1,0:T(8,128)(2,1)}, u32[]{:S(2)}, u32[]{:S(2)}) async-start(bf16[4,96,768]{2,1,0:T(8,128)(2,1)} %bitcast.56), calls=%async_computation.1 | async-start | bytes 1179648 | tf_op jit(solution)/shard_map/all_to_all | solution.py:440
  171.5 10.4 %collective-permute-start.40 = (bf16[128,192]{1,0:T(8,128)(2,1)}, bf16[128,192]{1,0:T(8,128)(2,1)}, u32[]{:S(2)}, u32[]{:S(2)}) collective-permute-start(bf16[128,192]{1,0:T(8,128)(2,1)} %bitcast.62), channel_id=1, source_target_pairs={{0,3},{1,2},{2,1},{3,0},{4,7},{5,6},{6,5},{7,4},{8,11},{9,10},{10,... | collective-permute-start | bytes 147464 | tf_op jit(solution)/shard_map/ppermute | solution.py:361
  173.6 8.3 %collective-permute-start.38 = (bf16[128,192]{1,0:T(8,128)(2,1)}, bf16[128,192]{1,0:T(8,128)(2,1)}, u32[]{:S(2)}, u32[]{:S(2)}) collective-permute-start(bf16[128,192]{1,0:T(8,128)(2,1)} %bitcast.60), channel_id=1, source_target_pairs={{0,1},{1,0},{2,3},{3,2},{4,5},{5,4},{6,7},{7,6},{8,9},{9,8},{10,11... | collective-permute-start | bytes 147464 | tf_op jit(solution)/shard_map/ppermute | solution.py:361
  173.9 8.1 %collective-permute-start.39 = (bf16[128,192]{1,0:T(8,128)(2,1)}, bf16[128,192]{1,0:T(8,128)(2,1)}, u32[]{:S(2)}, u32[]{:S(2)}) collective-permute-start(bf16[128,192]{1,0:T(8,128)(2,1)} %bitcast.61), channel_id=1, source_target_pairs={{0,2},{1,3},{2,0},{3,1},{4,6},{5,7},{6,4},{7,5},{8,10},{9,11},{10,... | collective-permute-start | bytes 147464 | tf_op jit(solution)/shard_map/ppermute | solution.py:361
  175.6 25.6 %collective-permute-start.45 = (bf16[2,192,768]{2,1,0:T(8,128)(2,1)}, bf16[2,192,768]{2,1,0:T(8,128)(2,1)}, u32[]{:S(2)}, u32[]{:S(2)}) collective-permute-start(bf16[2,192,768]{2,1,0:T(8,128)(2,1)} %fusion.23), channel_id=1, source_target_pairs={{0,8},{8,0},{1,9},{9,1},{2,10},{10,2},{3,11},{11,3},{4,12},{12,4},... | collective-permute-start | bytes 1769480 | tf_op jit(solution)/shard_map/ppermute | solution.py:351
  180.0 23.3 %collective-permute-start.41 = (bf16[384,768]{1,0:T(8,128)(2,1)}, bf16[384,768]{1,0:T(8,128)(2,1)}, u32[]{:S(2)}, u32[]{:S(2)}) collective-permute-start(bf16[384,768]{1,0:T(8,128)(2,1)} %add_convert_fusion.2), channel_id=1, source_target_pairs={{0,0},{4,8},{8,4},{12,12},{1,1},{5,9},{9,5},{13,13},{2,2},{6,10},{... | collective-permute-start | bytes 1769480 | tf_op jit(solution)/shard_map/ppermute | solution.py:355
  185.6 17.6 %collective-permute-start.44 = (bf16[160,768]{1,0:T(8,128)(2,1)S(1)}, bf16[160,768]{1,0:T(8,128)(2,1)}, u32[]{:S(2)}, u32[]{:S(2)}) collective-permute-start(bf16[160,768]{1,0:T(8,128)(2,1)S(1)} %get-tuple-element.228), channel_id=1, source_target_pairs={{0,3},{1,2},{2,1},{3,0},{4,7},{5,6},{6,5},{7,4},{8,11},{9,10},{10,... | collective-permute-start | bytes 737288 | tf_op jit(solution)/shard_map/ppermute | solution.py:361
  188.0 15.3 %collective-permute-start.43 = (bf16[160,768]{1,0:T(8,128)(2,1)S(1)}, bf16[160,768]{1,0:T(8,128)(2,1)}, u32[]{:S(2)}, u32[]{:S(2)}) collective-permute-start(bf16[160,768]{1,0:T(8,128)(2,1)S(1)} %get-tuple-element.229), channel_id=1, source_target_pairs={{0,2},{1,3},{2,0},{3,1},{4,6},{5,7},{6,4},{7,5},{8,10},{9,11},{10,... | collective-permute-start | bytes 737288 | tf_op jit(solution)/shard_map/ppermute | solution.py:361
  188.3 15.0 %collective-permute-start.42 = (bf16[160,768]{1,0:T(8,128)(2,1)S(1)}, bf16[160,768]{1,0:T(8,128)(2,1)}, u32[]{:S(2)}, u32[]{:S(2)}) collective-permute-start(bf16[160,768]{1,0:T(8,128)(2,1)S(1)} %get-tuple-element.230), channel_id=1, source_target_pairs={{0,1},{1,0},{2,3},{3,2},{4,5},{5,4},{6,7},{7,6},{8,9},{9,8},{10,11... | collective-permute-start | bytes 737288 | tf_op jit(solution)/shard_map/ppermute | solution.py:361
  203.3 16.6 %collective-permute-start.46 = (bf16[512,384]{1,0:T(8,128)(2,1)}, bf16[512,384]{1,0:T(8,128)(2,1)S(1)}, u32[]{:S(2)}, u32[]{:S(2)}) collective-permute-start(bf16[512,384]{1,0:T(8,128)(2,1)} %get-tuple-element.145), channel_id=1, source_target_pairs={{0,8},{8,0},{1,9},{9,1},{2,10},{10,2},{3,11},{11,3},{4,12},{12,4},... | collective-permute-start | bytes 1179656 | tf_op jit(solution)/shard_map/ppermute | solution.py:351
  210.7 47.5 %all-to-all-start.3 = ((bf16[16,24,768]{2,1,0:T(8,128)(2,1)}), bf16[16,24,768]{2,1,0:T(8,128)(2,1)S(1)}, u32[]{:S(2)}, u32[]{:S(2)}) async-start(bf16[16,24,768]{2,1,0:T(8,128)(2,1)} %bitcast.227), calls=%async_computation.3 | async-start | bytes 1179648 | tf_op jit(solution)/shard_map/all_to_all | solution.py:454
  215.0 30.9 %collective-permute-start.50 = (bf16[384,768]{1,0:T(8,128)(2,1)}, bf16[384,768]{1,0:T(8,128)(2,1)}, u32[]{:S(2)}, u32[]{:S(2)}) collective-permute-start(bf16[384,768]{1,0:T(8,128)(2,1)} %bitcast.63), channel_id=1, source_target_pairs={{0,0},{4,8},{8,4},{12,12},{1,1},{5,9},{9,5},{13,13},{2,2},{6,10},{... | collective-permute-start | bytes 1769480 | tf_op jit(solution)/shard_map/ppermute | solution.py:355
  230.5 25.5 %collective-permute-start.53 = (bf16[40,768]{1,0:T(8,128)(2,1)}, bf16[40,768]{1,0:T(8,128)(2,1)}, u32[]{:S(2)}, u32[]{:S(2)}) collective-permute-start(bf16[40,768]{1,0:T(8,128)(2,1)} %get-tuple-element.251), channel_id=1, source_target_pairs={{0,20},{4,16},{16,4},{20,0},{1,21},{5,17},{17,5},{21,1},{2,22},{6,... | collective-permute-start | bytes 184328 | tf_op jit(solution)/shard_map/ppermute | solution.py:361
  235.9 14.8 %collective-permute-start.49 = (bf16[128,768]{1,0:T(8,128)(2,1)}, bf16[128,768]{1,0:T(8,128)(2,1)S(1)}, u32[]{:S(2)}, u32[]{:S(2)}) collective-permute-start(bf16[128,768]{1,0:T(8,128)(2,1)} %get-tuple-element.241), channel_id=1, source_target_pairs={{0,3},{1,2},{2,1},{3,0},{4,7},{5,6},{6,5},{7,4},{8,11},{9,10},{10,... | collective-permute-start | bytes 589832 | tf_op jit(solution)/shard_map/ppermute | solution.py:361
  238.0 16.8 %collective-permute-start.48 = (bf16[128,768]{1,0:T(8,128)(2,1)}, bf16[128,768]{1,0:T(8,128)(2,1)S(1)}, u32[]{:S(2)}, u32[]{:S(2)}) collective-permute-start(bf16[128,768]{1,0:T(8,128)(2,1)} %get-tuple-element.242), channel_id=1, source_target_pairs={{0,2},{1,3},{2,0},{3,1},{4,6},{5,7},{6,4},{7,5},{8,10},{9,11},{10,... | collective-permute-start | bytes 589832 | tf_op jit(solution)/shard_map/ppermute | solution.py:361
  238.3 16.5 %collective-permute-start.47 = (bf16[128,768]{1,0:T(8,128)(2,1)}, bf16[128,768]{1,0:T(8,128)(2,1)S(1)}, u32[]{:S(2)}, u32[]{:S(2)}) collective-permute-start(bf16[128,768]{1,0:T(8,128)(2,1)} %get-tuple-element.243), channel_id=1, source_target_pairs={{0,1},{1,0},{2,3},{3,2},{4,5},{5,4},{6,7},{7,6},{8,9},{9,8},{10,11... | collective-permute-start | bytes 589832 | tf_op jit(solution)/shard_map/ppermute | solution.py:361
  245.9 10.1 %collective-permute-start.52 = (bf16[40,768]{1,0:T(8,128)(2,1)S(1)}, bf16[40,768]{1,0:T(8,128)(2,1)S(1)}, u32[]{:S(2)}, u32[]{:S(2)}) collective-permute-start(bf16[40,768]{1,0:T(8,128)(2,1)S(1)} %copy-done.26), channel_id=1, source_target_pairs={{0,16},{4,20},{16,0},{20,4},{1,17},{5,21},{17,1},{21,5},{2,18},{6,... | collective-permute-start | bytes 184328 | tf_op jit(solution)/shard_map/ppermute | solution.py:361
  258.2 28.2 %all-to-all-start.2 = ((bf16[16,24,640]{2,1,0:T(8,128)(2,1)}), bf16[16,24,640]{2,1,0:T(8,128)(2,1)S(1)}, u32[]{:S(2)}, u32[]{:S(2)}) async-start(bf16[16,24,640]{2,1,0:T(8,128)(2,1)} %bitcast.84), calls=%async_computation.2 | async-start | bytes 983040 | tf_op jit(solution)/shard_map/all_to_all | solution.py:454
  263.7 21.2 %collective-permute-start.54 = (bf16[256,768]{1,0:T(8,128)(2,1)S(1)}, bf16[256,768]{1,0:T(8,128)(2,1)S(1)}, u32[]{:S(2)}, u32[]{:S(2)}) collective-permute-start(bf16[256,768]{1,0:T(8,128)(2,1)S(1)} %pad_maximum_fusion.8), channel_id=1, source_target_pairs={{0,0},{4,8},{8,4},{12,12},{1,1},{5,9},{9,5},{13,13},{2,2},{6,10},{... | collective-permute-start | bytes 1179656 | tf_op jit(solution)/shard_map/ppermute | solution.py:355
  (61 other events, 614.1 us)
Sparse Core Ops, SparseCore 0:
  11.1 69.1 all-gather.1

commit v3 on v2

--- a/solution.py
+++ b/solution.py
@@ -231,6 +231,35 @@
     def _():
         sum_ref[...] = total_scratch[0:own_rows, :]
         low_ref[...] = total_scratch[own_rows:count, :].astype(BF16)
+
+
+def column_kernel(major, heads, size, in_ref, qk_ref, v_ref, small_ref):
+    terms = in_ref.shape[0] // major
+    for group in range(major):
+        total = in_ref[group].astype(F32)
+        for term in range(1, terms):
+            total = total + in_ref[term * major + group].astype(F32)
+        queries, start = heads * 2 * size, group * heads * size
+        features = major * heads * size
+        qk_ref[:, start : start + heads * size] = total[:, queries : queries + heads * size]
+        for head in range(heads):
+            first, place = head * 2 * size, start + head * size
+            qk_ref[:, features + place : features + place + size] = total[:, first : first + size]
+            v_ref[:, place : place + size] = total[:, first + size : first + 2 * size]
+        small_ref[group] = total[:, queries + heads * size :]
+
+
+def split_columns(value, major, heads, size):
+    rows, columns = value.shape[1:]
+    features = major * heads * size
+    return pl.pallas_call(
+        functools.partial(column_kernel, major, heads, size),
+        out_shape=[
+            jax.ShapeDtypeStruct((rows, 2 * features), F32),
+            jax.ShapeDtypeStruct((rows, features), F32),
+            jax.ShapeDtypeStruct((major, rows, columns - 3 * heads * size), F32),
+        ],
+    )(value)
 
 
 def unpack_kernel(cuts, in_ref, out_ref):
@@ -451,7 +480,7 @@
 def scatter_rows(value):
     chips = math.prod(lax.axis_size(name) for name in REST)
     value = value.reshape(chips, -1, value.shape[-1])
-    return lax.all_to_all(value, REST, 0, 0, tiled=True).astype(F32)
+    return lax.all_to_all(value, REST, 0, 0, tiled=True)
 
 
 def after(value, *others):
@@ -499,12 +528,11 @@
 
     numbers = jnp.concatenate([routes, slots]).astype(BF16)
     numbers = jnp.pad(numbers, ((0, 14), (0, width - rows)))
-    both = jnp.concatenate([activations[0], numbers, w_out[:, 0, :]])
+    both = jnp.concatenate([activations[0], numbers])
     query_key_weight, value_weight, w_in = after((query_key_weight, value_weight, w_in), both)
     both = turn(both)
     tokens = both[:rows]
     numbers = both[rows : rows + 2, :rows].astype(jnp.int32)
-    outer = both[rows + 16 :]
 
     def by_head(value):
         return value.reshape(shard, major, heads, 1, head_dim)
@@ -523,11 +551,33 @@
         axis=2,
     )
     packed = exchange_ordered(jnp.transpose(packed, (1, 0, 2)), "mj")
+    column = exchange([tokens] * major, "mj")
+
+    expert_ids = jnp.arange(experts, dtype=jnp.int32)
+    slot_ids = jnp.arange(capacity, dtype=jnp.int32)
+
+    def selection(token_routes, token_slots, place):
+        chosen = (
+            ((token_routes ^ place)[None, None, :] == expert_ids[:, None, None])
+            & (token_slots[None, None, :] == slot_ids[None, :, None])
+        ).astype(BF16)
+        return chosen.reshape(experts * capacity, rows)
+
+    def by_expert(chosen, value):
+        sent = dot_n(chosen, value).astype(BF16)
+        return [sent[i * capacity : (i + 1) * capacity] for i in range(experts)]
+
+    sent = by_expert(selection(routes[0], slots[0], lax.axis_index(("ey", "ec"))), cotangent[0])
+    cot_parts = turn_exchange(after(sent, packed))
+    routes, slots = numbers[0], numbers[1]
+    select = selection(routes, slots, my_exp)
+
     background = packed
     if rest == 1:
         packed = jnp.stack([packed, swap(packed, "gh")])
         background = packed
         packed = jnp.concatenate([packed, swap(packed, "ey")])
+        packed, column, cot_parts = lax.optimization_barrier((packed, column, cot_parts))
         packed = ordered(packed, lax.axis_index(("ey", "gh"))).reshape(2, 2, major, shard, packed_width)
         packed = gather_pair(packed, "ec", 1)
     else:
@@ -540,7 +590,7 @@
     gain_first = extras[:, experts].astype(F32)
     gain_second = extras[:, experts + 1].astype(F32)
 
-    column = jnp.stack(exchange([tokens] * major, "mj"))
+    column = jnp.stack(column)
     part = w_in.shape[2] // major
     half = part // 2
     inner = jnp.concatenate(
@@ -550,8 +600,8 @@
         ]
     )
     inner = swap_major(inner.reshape(major, -1, part)).reshape(-1, part)
-    inner = turn(after(jnp.concatenate([inner, cotangent[0]]), background))
-    cotangent = after(cotangent[0], packed)
+    both = jnp.concatenate([inner, w_out[:, 0, :], cotangent[0]])
+    both = turn(after(both, background))
 
     full_o = lax.all_gather(output_weight, EVERY, axis=0, tiled=True)
     near_major = jnp.arange(major, dtype=jnp.int32) ^ my_major
@@ -572,53 +622,33 @@
     key_slots = jnp.where(jnp.any(found, axis=1), jnp.sum(key_slots, axis=1), ring)
     places = (key_blocks[:major], key_blocks, key_slots)
 
-    expert_ids = jnp.arange(experts, dtype=jnp.int32)
-    slot_ids = jnp.arange(capacity, dtype=jnp.int32)
-
-    def selection(token_routes, token_slots, place):
-        chosen = (
-            ((token_routes ^ place)[None, None, :] == expert_ids[:, None, None])
-            & (token_slots[None, None, :] == slot_ids[None, :, None])
-        ).astype(BF16)
-        return chosen.reshape(experts * capacity, rows)
-
-    def by_expert(chosen, value):
-        sent = dot_n(chosen, value).astype(BF16)
-        return [sent[i * capacity : (i + 1) * capacity] for i in range(experts)]
-
     def gather_rows(parts):
         return exchange([jnp.concatenate(parts)] * major, "mj")
 
-    def sum_parts(value):
-        value = value.reshape(major, experts * capacity, width)
-        return exchange([value[i] for i in range(major)], "mj")
+    def in_parts(value):
+        count = experts * capacity
+        return [value[i * count : (i + 1) * count] for i in range(major)]
 
     def send_back(parts):
         total = sum(part.astype(F32) for part in parts).astype(BF16)
         total = total.reshape(experts, capacity, width)
         return exchange([total[i] for i in range(experts)], ("ey", "gh"))
 
-    sent = by_expert(selection(routes[0], slots[0], lax.axis_index(("ey", "ec"))), cotangent)
-    cot_parts = turn_exchange(sent)
-    routes, slots = numbers[0], numbers[1]
-    select = selection(routes, slots, my_exp)
+    cot_rows = gather_rows(cot_parts)
 
     column_hidden = column.reshape(major * rows, width).astype(F32)
     column_unit = unit(column_hidden)
     normed = (column_hidden * column_unit * gain_first).astype(BF16)
     projected = dot_n(normed, packed).astype(BF16)
     others = other_minor(projected, kv_width)
-    outer = gather_minor(outer).reshape(part, width)
     attended_low, attended_wide, lse = forward_attention(
         projected, others, near, far, places, heads, rows
     )
-    attended_low, cot_parts, inner, outer = lax.optimization_barrier(
-        (attended_low, cot_parts, inner, outer)
-    )
-    my_cotangent = inner[-rows:]
+    attended_low, cot_rows = lax.optimization_barrier((attended_low, cot_rows))
     attended = exchange([attended_low[i * rows : (i + 1) * rows] for i in range(major)], "mj")
-    attended = ordered(jnp.stack(attended), my_major)
-    attended = jnp.transpose(attended, (1, 0, 2)).reshape(rows, features)
+    attended = lax.optimization_barrier(attended)
+    attended = lax.optimization_barrier(ordered(jnp.stack(attended), my_major))
+    attended = jnp.concatenate([attended[i] for i in range(major)], axis=1)
 
     hidden = tokens.astype(F32)
     middle = hidden + dot_n(attended, full_o)
@@ -627,10 +657,11 @@
     chances = jax.nn.softmax(dot_n(mixed, full_router), axis=-1)
     route_mask = (routes[:, None] == expert_ids[None, :]).astype(F32)
     gate = jnp.sum(chances * route_mask, axis=-1, keepdims=True)
-
     mixed_parts = exchange(by_expert(select, mixed), ("ey", "gh"))
-    cot_rows = gather_rows(after(cot_parts, attended))
-    inner = after(inner[:-rows], attended)
+    both = after(both, attended)
+    my_cotangent = both[-rows:]
+    inner = both[: major * w_in.shape[0]]
+    outer = gather_minor(both[major * w_in.shape[0] : -rows]).reshape(part, width)
     inner = gather_minor(inner.reshape(major, -1, part)).reshape(2, rest, major, -1, part)
     inner = jnp.transpose(inner, (0, 2, 1, 3, 4)).reshape(width, part)
     buffer = gather_rows(mixed_parts)
@@ -655,20 +686,21 @@
 
     activated = activated_wide.astype(BF16)
     produced = dot_n(activated, outer).astype(BF16)
+    produced = in_parts(produced)
     grad_router = dot_0(buffer, grad_logits)
     gated_rows = (row_gate * cot_rows.astype(F32)).astype(BF16)
     grad_outer = dot_0(activated, gated_rows).reshape(minor, -1, width)
     grad_inner = dot_0(buffer, grad_preact).reshape(2, major, rest, -1, part)
     grad_inner = jnp.transpose(grad_inner, (0, 2, 1, 3, 4)).reshape(minor, -1, part)
     grad_outer, grad_inner, produced, grad_parts = lax.optimization_barrier(
-        (split_minor(grad_outer), split_minor(grad_inner), produced, sum_parts(grad_mixed))
+        (split_minor(grad_outer), split_minor(grad_inner), produced, exchange(in_parts(grad_mixed), "mj"))
     )
     grad_parts = send_back(grad_parts)
+    produced_parts = exchange(produced, "mj")
     grad_outer = sum_split(grad_outer).astype(BF16)
     grad_inner = sum_split(grad_inner).astype(BF16).reshape(major, -1, part)
     grad_parts, grad_outer, grad_inner = lax.optimization_barrier((grad_parts, grad_outer, grad_inner))
     grad_mixed = dot_0(select, jnp.concatenate(grad_parts))
-    grad_outer = turn(grad_outer)
 
     grad_z = my_cotangent.astype(F32)
     grad_gain_second = jnp.sum(grad_mixed * middle * middle_unit, axis=0)
@@ -679,30 +711,35 @@
         - middle * middle_unit**3 * jnp.mean(scaled * middle, axis=-1, keepdims=True)
     )
     grad_branch = grad_middle.astype(BF16)
-    grad_attended = dot_t(grad_branch, full_o).astype(BF16)
-    grad_attended = jnp.transpose(grad_attended.reshape(rows, major, q_width), (1, 0, 2))
-    grad_attended = ordered(grad_attended, my_major)
-    grad_attended = jnp.concatenate(exchange([grad_attended[i] for i in range(major)], "mj"))
-    produced_parts = sum_parts(after(produced, grad_attended))
-    grad_inner = swap_major(after(grad_inner, grad_mixed)).reshape(-1, part)
+    grad_attended = [
+        dot_t(
+            grad_branch, lax.dynamic_slice_in_dim(full_o, (my_major ^ i) * q_width, q_width)
+        ).astype(BF16)
+        for i in range(major)
+    ]
+    grad_inner, grad_outer, attended, grad_branch = after(
+        (grad_inner, grad_outer, attended, grad_branch), grad_attended
+    )
+    grad_attended = exchange(grad_attended, "mj")
+    grad_attended = jnp.concatenate(lax.optimization_barrier(grad_attended))
+    grad_outer = turn(grad_outer)
+    grad_inner = swap_major(grad_inner).reshape(-1, part)
     grad_o = core_sum(dot_0(attended, grad_branch))
 
     dq, dkv, dkv_low, near_sum, far_sum = backward_attention(
         projected, grad_attended, attended_wide, others, near, far, places, lse, heads, rows
     )
-    dq, dkv, dkv_low, grad_outer, grad_inner, produced_parts, grad_o = lax.optimization_barrier(
-        (dq, dkv, dkv_low, grad_outer, grad_inner, produced_parts, grad_o)
-    )
-    grad_o = scatter_rows(grad_o)
+    dq, dkv, dkv_low, grad_inner = lax.optimization_barrier((dq, dkv, dkv_low, grad_inner))
     grad_inner = turn(grad_inner)
     dkv = sum_nearest(dkv, dkv_low.reshape(minor - 1, major * rows, kv_width)).astype(BF16)
     grad_projected = jnp.concatenate([dkv, dq], axis=1)
     grad_normed = dot_t(grad_projected, packed)
     parts = grad_normed.astype(BF16).reshape(major, rows, width)
-    produced_parts, near_sum, normed, grad_projected = after(
-        (produced_parts, near_sum, normed, grad_projected), parts
+    produced_parts, near_sum, normed, grad_projected, grad_o, grad_outer = after(
+        (produced_parts, near_sum, normed, grad_projected, grad_o, grad_outer), parts
     )
     produced_parts = send_back(produced_parts)
+    grad_o = scatter_rows(grad_o)
 
     sums = pl.pallas_call(
         functools.partial(bucket_sum_kernel, edges, rows),
@@ -711,9 +748,20 @@
     grad_table = sums[:, :32].T
     grad_gain_first = jnp.sum(grad_normed * column_hidden * column_unit, axis=0)
     grad_parts = exchange([parts[i] for i in range(major)], "mj")
-    grad_parts, grad_inner, grad_outer = lax.optimization_barrier((grad_parts, grad_inner, grad_outer))
+    grad_outer = unpack(grad_outer[None], 1)
+    grad_parts, grad_outer = lax.optimization_barrier((grad_parts, grad_outer))
     grad_normed = sum(part.astype(F32) for part in grad_parts)
-    produced = dot_0(select, jnp.concatenate(after(produced_parts, grad_normed)))
+    buckets = bias_table.shape[0]
+    table_columns = buckets * heads // shard
+    flat_table = jnp.tile(
+        grad_table.reshape(shard, table_columns), (width // shard, 1)
+    )
+    small = jnp.concatenate(
+        [grad_router, grad_gain_first[:, None], grad_gain_second[:, None], flat_table], axis=1
+    )
+    small = jnp.pad(small, ((0, 0), (kv_width + q_width, extra_width - small.shape[1])))
+    grad_weight = core_sum(dot_0(normed, grad_projected) + small)
+    produced = dot_0(select, jnp.concatenate(after(produced_parts, grad_normed, grad_weight)))
     layer_output = (middle + gate * produced).astype(BF16)
     hidden_unit = unit(hidden)
     scaled = grad_normed * gain_first
@@ -723,39 +771,22 @@
         - hidden * hidden_unit**3 * jnp.mean(scaled * hidden, axis=-1, keepdims=True)
     ).astype(BF16)
     both = turn(jnp.concatenate([grad_activations, layer_output]))
-    grad_activations, layer_output = both[None, :rows], both[None, rows:]
-
-    buckets = bias_table.shape[0]
-    table_columns = buckets * heads // shard
-    flat_table = jnp.tile(
-        grad_table.reshape(shard, table_columns), (width // shard, 1)
-    )
-    small = jnp.concatenate(
-        [grad_router, grad_gain_first[:, None], grad_gain_second[:, None], flat_table], axis=1
-    )
-    small = jnp.pad(small, ((0, 0), (kv_width + q_width, extra_width - small.shape[1])))
-    arrived = scatter_rows(core_sum(dot_0(normed, grad_projected) + small))
-    arrived = arrived.reshape(4, major, rest, shard, packed_width)
-    arrived = jnp.sum(arrived, axis=(0, 2))
-    key_value = arrived[:, :, :kv_width].reshape(major, shard, heads, 2, head_dim)
-
-    def side_by_side(value):
-        return jnp.transpose(value.reshape(major, shard, q_width), (1, 0, 2)).reshape(shard, features)
-
-    grad_query = side_by_side(arrived[:, :, kv_width : kv_width + q_width])
-    grad_key = side_by_side(key_value[:, :, :, 0, :])
-    grad_v = side_by_side(key_value[:, :, :, 1, :])
-    small = arrived[:, :, kv_width + q_width :]
+    arrived = scatter_rows(grad_weight)
+    grad_inner = unpack(grad_inner.reshape(major, w_in.shape[0], part), 2)
+    both, arrived, grad_inner = lax.optimization_barrier((both, arrived, grad_inner))
+    if rest > 1:
+        arrived = jnp.sum(arrived.reshape(4, major, rest, shard, packed_width), axis=2)
+        arrived = arrived.reshape(4 * major, shard, packed_width)
+    grad_qk, grad_v, small = split_columns(arrived, major, heads, head_dim)
     summed = jnp.sum(small[:, :, : experts + 2], axis=0)
     grad_table = small[:, :, experts + 2 : experts + 2 + table_columns]
     grad_table = jnp.transpose(grad_table.reshape(major, buckets, heads), (1, 0, 2))
-    grad_o = jnp.sum(grad_o, axis=0)
-    grad_inner = unpack(grad_inner.reshape(major, w_in.shape[0], part), 2)
-    grad_outer = unpack(grad_outer[None], 1)
+    grad_o = jnp.sum(grad_o.astype(F32), axis=0)
+    grad_activations, layer_output = both[None, :rows], both[None, rows:]
     return (
         layer_output,
         grad_activations,
-        jnp.concatenate([grad_query, grad_key], axis=1),
+        grad_qk,
         grad_v,
         grad_o,
         summed[:, experts],

time: 301 us -> 296 us (0.983)
  local copies, waits for them, and re-layouts: 28.5 us -> 20.7 us
    ppermute x36, waiting for transfers between devices: 36.3 us -> 48.5 us  [exchange(): lax.ppermute(parts[step], axis, [(source, source ^ step) for source in ra...]
    all_to_all x2, starting transfers between devices: 8.65 us -> 16.5 us  [scatter_rows(): return lax.all_to_all(value, REST, 0, 0, tiled=True)]
    ppermute x11, waiting for transfers between devices: 10.4 us -> 2.74 us  [swap(): return lax.ppermute(value, axis, [(0, 1), (1, 0)])]
    ppermute x5, waiting for transfers between devices: 16.4 us -> 11 us  [turn(): return lax.ppermute(value, ('ec', 'gh'), [(0, 0), (1, 2), (2, 1), (3, 3)])]
    ppermute x11, starting transfers between devices: 16.8 us -> 11.7 us  [swap(): return lax.ppermute(value, axis, [(0, 1), (1, 0)])]
    unnamed x112 -> x84, local copies, waits for them, and re-layouts: 8.5 us -> 4.76 us
    ppermute x4, waiting for transfers between devices: 0.01 us -> 3.46 us  [turn_exchange(): arrived.append(lax.ppermute(part, ('ey', 'ec', 'gh'), pairs))]
    dot_general x5 -> x8, matrix products: 6.79 us -> 7.19 us  [dot_t(): lax.dot_general(left, right, (((1,), (1,)), ((), ())), preferred_element_...]
  transfers between devices with their start and end apart: 61 -> 61, of which waited for: 21 -> 23; matrix products, arithmetic and copies ran while one was open for 22% -> 19% of each run, Pallas kernels for 11% -> 11%
where the time goes in v3:
time: 296 us; the launch traced here: 294 us
  starting transfers between devices  103 us (35%)
  waiting for transfers between devices  66.4 us (22%)
  Pallas kernels  34.5 us (12%)
  other arithmetic  30.7 us (10%)
  matrix products  22.9 us (8%)
  local copies, waits for them, and re-layouts  20.7 us (7%)
  between operations  15.4 us (5%)
    ppermute x36, waiting for transfers between devices, exchange(): lax.ppermute(parts[step], axis, [(source, source ^ step) for source in ra...  48.5 us
    ppermute x36, starting transfers between devices, exchange(): lax.ppermute(parts[step], axis, [(source, source ^ step) for source in ra...  39.6 us
    ppermute x5, starting transfers between devices, turn(): return lax.ppermute(value, ('ec', 'gh'), [(0, 0), (1, 2), (2, 1), (3, 3)])  20.1 us
    all_to_all x2, starting transfers between devices, scatter_rows(): return lax.all_to_all(value, REST, 0, 0, tiled=True)  16.5 us
    pallas_call x1, Pallas kernels, backward_attention(): pl.pallas_call(functools.partial(attention_back_kernel, heads, rows), gri...  12.6 us
    ppermute x11, starting transfers between devices, swap(): return lax.ppermute(value, axis, [(0, 1), (1, 0)])  11.7 us
    ppermute x5, waiting for transfers between devices, turn(): return lax.ppermute(value, ('ec', 'gh'), [(0, 0), (1, 2), (2, 1), (3, 3)])  11 us
    pallas_call x1, Pallas kernels, forward_attention(): pl.pallas_call(functools.partial(attention_kernel, heads, rows), grid=(st...  9.92 us
  transfers between devices with their start and end apart: 61, of which 23 were waited for; matrix products, arithmetic and copies ran while one was open for 19% of the time, Pallas kernels for 11%

profile of v3, /device:TPU:1, one launch (start us, length us, event | category | flops | bytes accessed | tf_op | source)
XLA Modules:
  0.0 293.7 jit_solution(16132724881060765176)
XLA Ops:
  10.3 5.6 %collective-permute-start.6 = (bf16[144,768]{1,0:T(8,128)(2,1)S(1)}, bf16[144,768]{1,0:T(8,128)(2,1)S(1)}, u32[]{:S(2)}, u32[]{:S(2)}) collective-permute-start(bf16[144,768]{1,0:T(8,128)(2,1)S(1)} %pad_maximum_fusion.12), channel_id=1, source_target_pairs={{0,0},{4,8},{8,4},{12,12},{1,1},{5,9},{9,5},{13,13},{2,2},{6,10},{... | collective-permute-start | bytes 663560 | tf_op jit(solution)/shard_map/ppermute | solution.py:384
  19.4 2.3 collective-permute-start.2
  23.4 3.5 %all-to-all-start = ((bf16[4,96,768]{2,1,0:T(8,128)(2,1)}), bf16[4,96,768]{2,1,0:T(8,128)(2,1)S(1)}, u32[]{:S(2)}, u32[]{:S(2)}) async-start(bf16[4,96,768]{2,1,0:T(8,128)(2,1)} %bitcast.9), calls=%async_computation | async-start | bytes 1179648 | tf_op jit(solution)/shard_map/all_to_all | solution.py:469
  30.6 2.3 shard_map.215.near_ref
  32.9 3.0 %collective-permute-start.10 = (bf16[40,768]{1,0:T(8,128)(2,1)S(1)}, bf16[40,768]{1,0:T(8,128)(2,1)S(1)}, u32[]{:S(2)}, u32[]{:S(2)}) collective-permute-start(bf16[40,768]{1,0:T(8,128)(2,1)S(1)} %get-tuple-element.116), channel_id=1, source_target_pairs={{0,0},{4,8},{8,4},{12,12},{16,16},{20,24},{24,20},{28,28},{1,1},{5... | collective-permute-start | bytes 184328 | tf_op jit(solution)/shard_map/ppermute | solution.py:416
  42.1 2.7 collective-permute-start.12
  46.9 2.4 collective-permute-done.12
  50.4 2.0 collective-permute-done.8
  60.9 3.1 %collective-permute-start.4 = (bf16[896,768]{1,0:T(8,128)(2,1)}, bf16[896,768]{1,0:T(8,128)(2,1)S(1)}, u32[]{:S(2)}, u32[]{:S(2)}) collective-permute-start(bf16[896,768]{1,0:T(8,128)(2,1)} %pad_maximum_fusion), channel_id=1, source_target_pairs={{0,0},{4,8},{8,4},{12,12},{1,1},{5,9},{9,5},{13,13},{2,2},{6,10},{... | collective-permute-start | bytes 4128776 | tf_op jit(solution)/shard_map/ppermute | solution.py:384
  65.2 2.2 collective-permute-start.18
  67.9 9.9 %shard_map.216 = (bf16[512,192]{1,0:T(8,128)(2,1)}, f32[512,384]{1,0:T(8,128)}, f32[4,3,128]{2,1,0:T(4,128)}) custom-call(s32[4]{0:T(128)} %slice_bitcast_fusion.18.block_ref, s32[8]{0:T(128)} %copy-done.35, s32[10]{0:T(128)} %broadcast_select_fusion.place_ref, f32[2,3]{1,0:T(2,128)} %pad_maximum_fusion.19.far_ref, ...), custom_call_target="tpu_custom_call" | custom-call | flops 805306368 | bytes 3145728 | tf_op jit(solution)/shard_map/pallas_call | solution.py:309
  77.8 10.7 %collective-permute-done.18 = bf16[160,768]{1,0:T(8,128)(2,1)S(1)} collective-permute-done((bf16[160,768]{1,0:T(8,128)(2,1)}, bf16[160,768]{1,0:T(8,128)(2,1)S(1)}, u32[]{:S(2)}, u32[]{:S(2)}) %collective-permute-start.18) | collective-permute-done | bytes 245792 | tf_op jit(solution)/shard_map/ppermute | solution.py:390
  88.5 3.3 %collective-permute-done.17 = bf16[160,768]{1,0:T(8,128)(2,1)S(1)} collective-permute-done((bf16[160,768]{1,0:T(8,128)(2,1)}, bf16[160,768]{1,0:T(8,128)(2,1)S(1)}, u32[]{:S(2)}, u32[]{:S(2)}) %collective-permute-start.17) | collective-permute-done | bytes 245792 | tf_op jit(solution)/shard_map/ppermute | solution.py:390
  93.0 2.8 collective-permute-start.21
  96.2 2.2 collective-permute-done.21
  103.8 4.1 %collective-permute-start.24 = (bf16[40,768]{1,0:T(8,128)(2,1)S(1)}, bf16[40,768]{1,0:T(8,128)(2,1)S(1)}, u32[]{:S(2)}, u32[]{:S(2)}) collective-permute-start(bf16[40,768]{1,0:T(8,128)(2,1)S(1)} %get-tuple-element.303), channel_id=1, source_target_pairs={{0,20},{4,16},{16,4},{20,0},{1,21},{5,17},{17,5},{21,1},{2,22},{6,... | collective-permute-start | bytes 184328 | tf_op jit(solution)/shard_map/ppermute | solution.py:390
  108.7 2.5 collective-permute-done.24
  113.8 1.9 collective-permute-start.26
  117.5 3.9 %collective-permute-done.27 = bf16[160,768]{1,0:T(8,128)(2,1)S(1)} collective-permute-done((bf16[160,768]{1,0:T(8,128)(2,1)S(1)}, bf16[160,768]{1,0:T(8,128)(2,1)S(1)}, u32[]{:S(2)}, u32[]{:S(2)}) %collective-permute-start.27) | collective-permute-done | bytes 245792 | tf_op jit(solution)/shard_map/ppermute | solution.py:390
  121.5 4.8 %collective-permute-done.26 = bf16[160,768]{1,0:T(8,128)(2,1)S(1)} collective-permute-done((bf16[160,768]{1,0:T(8,128)(2,1)S(1)}, bf16[160,768]{1,0:T(8,128)(2,1)S(1)}, u32[]{:S(2)}, u32[]{:S(2)}) %collective-permute-start.26) | collective-permute-done | bytes 245792 | tf_op jit(solution)/shard_map/ppermute | solution.py:390
  140.0 1.9 collective-permute-start.31
  143.6 4.5 %collective-permute-done.32 = bf16[160,768]{1,0:T(8,128)(2,1)S(1)} collective-permute-done((bf16[160,768]{1,0:T(8,128)(2,1)S(1)}, bf16[160,768]{1,0:T(8,128)(2,1)S(1)}, u32[]{:S(2)}, u32[]{:S(2)}) %collective-permute-start.32) | collective-permute-done | bytes 245792 | tf_op jit(solution)/shard_map/ppermute | solution.py:390
  148.1 4.9 %collective-permute-done.31 = bf16[160,768]{1,0:T(8,128)(2,1)S(1)} collective-permute-done((bf16[160,768]{1,0:T(8,128)(2,1)S(1)}, bf16[160,768]{1,0:T(8,128)(2,1)S(1)}, u32[]{:S(2)}, u32[]{:S(2)}) %collective-permute-start.31) | collective-permute-done | bytes 245792 | tf_op jit(solution)/shard_map/ppermute | solution.py:390
  163.1 1.9 fusion.76
  165.3 1.8 collective-permute-start.38
  170.3 4.4 %all-to-all-start.1 = ((bf16[4,96,768]{2,1,0:T(8,128)(2,1)}), bf16[4,96,768]{2,1,0:T(8,128)(2,1)}, u32[]{:S(2)}, u32[]{:S(2)}) async-start(bf16[4,96,768]{2,1,0:T(8,128)(2,1)} %bitcast.58), calls=%async_computation.1 | async-start | bytes 1179648 | tf_op jit(solution)/shard_map/all_to_all | solution.py:469
  177.1 2.4 collective-permute-start.48
  181.8 12.6 %shard_map.217 = (bf16[512,256]{1,0:T(8,128)(2,1)}, f32[512,384]{1,0:T(8,128)}, bf16[512,384]{1,0:T(8,128)(2,1)}, f32[3,384,128]{2,1,0:T(8,128)}, f32[3,2,128]{2,1,0:T(2,128)}) custom-call(s32[4]{0:T(128)} %slice_bitcast_fusion.18.block_ref, s32[8]{0:T(128)} %copy-done.35, s32[10]{0:T(128)} %broadcast_select_fusion.place_ref, ...), custom_call_target="tpu_custom_call" | custom-call | flops 2013265920 | bytes 3145728 | tf_op jit(solution)/shard_map/pallas_call | solution.py:342
  198.7 4.3 %collective-permute-start.49 = (bf16[384,768]{1,0:T(8,128)(2,1)}, bf16[384,768]{1,0:T(8,128)(2,1)}, u32[]{:S(2)}, u32[]{:S(2)}) collective-permute-start(bf16[384,768]{1,0:T(8,128)(2,1)} %add_convert_fusion.2), channel_id=1, source_target_pairs={{0,0},{4,8},{8,4},{12,12},{1,1},{5,9},{9,5},{13,13},{2,2},{6,10},{... | collective-permute-start | bytes 1769480 | tf_op jit(solution)/shard_map/ppermute | solution.py:384
  203.0 2.1 fusion.16
  205.2 2.4 collective-permute-start.55
  207.7 1.8 fusion.12
  210.4 2.3 collective-permute-start.44
  213.0 1.8 collective-permute-done.47
  214.8 2.6 collective-permute-start.42
  217.4 3.2 %shard_map.219 = f32[3,128]{1,0:T(4,128)} custom-call(f32[3,384,128]{2,1,0:T(8,128)} %get-tuple-element.198.near_ref, f32[3,2,128]{2,1,0:T(2,128)} %get-tuple-element.199.far_ref), custom_call_target="tpu_custom_call" | custom-call | tf_op jit(solution)/shard_map/pallas_call | solution.py:744
  221.2 9.9 %all-to-all-start.3 = ((bf16[16,24,768]{2,1,0:T(8,128)(2,1)}), bf16[16,24,768]{2,1,0:T(8,128)(2,1)}, u32[]{:S(2)}, u32[]{:S(2)}) async-start(bf16[16,24,768]{2,1,0:T(8,128)(2,1)} %bitcast.77), calls=%async_computation.3 | async-start | bytes 1179648 | tf_op jit(solution)/shard_map/all_to_all | solution.py:483
  233.4 3.1 %collective-permute-start.52 = (bf16[40,768]{1,0:T(8,128)(2,1)}, bf16[40,768]{1,0:T(8,128)(2,1)}, u32[]{:S(2)}, u32[]{:S(2)}) collective-permute-start(bf16[40,768]{1,0:T(8,128)(2,1)} %get-tuple-element.294), channel_id=1, source_target_pairs={{0,20},{4,16},{16,4},{20,0},{1,21},{5,17},{17,5},{21,1},{2,22},{6,... | collective-permute-start | bytes 184328 | tf_op jit(solution)/shard_map/ppermute | solution.py:390
  237.5 2.1 pad_add_fusion
  240.4 2.3 shard_map.218
  243.2 4.4 %collective-permute-start.53 = (bf16[2,192,640]{2,1,0:T(8,128)(2,1)}, bf16[2,192,640]{2,1,0:T(8,128)(2,1)S(1)}, u32[]{:S(2)}, u32[]{:S(2)}) collective-permute-start(bf16[2,192,640]{2,1,0:T(8,128)(2,1)} %fusion.22), channel_id=1, source_target_pairs={{0,8},{8,0},{1,9},{9,1},{2,10},{10,2},{3,11},{11,3},{4,12},{12,4},... | collective-permute-start | bytes 1474568 | tf_op jit(solution)/shard_map/ppermute | solution.py:380
  247.7 2.0 fusion.25
  250.6 6.6 %all-to-all-start.2 = ((bf16[16,24,640]{2,1,0:T(8,128)(2,1)}), bf16[16,24,640]{2,1,0:T(8,128)(2,1)S(1)}, u32[]{:S(2)}, u32[]{:S(2)}) async-start(bf16[16,24,640]{2,1,0:T(8,128)(2,1)} %bitcast.73), calls=%async_computation.2 | async-start | bytes 983040 | tf_op jit(solution)/shard_map/all_to_all | solution.py:483
  259.7 4.7 %collective-permute-start.54 = (bf16[256,768]{1,0:T(8,128)(2,1)S(1)}, bf16[256,768]{1,0:T(8,128)(2,1)S(1)}, u32[]{:S(2)}, u32[]{:S(2)}) collective-permute-start(bf16[256,768]{1,0:T(8,128)(2,1)S(1)} %pad_maximum_fusion.7), channel_id=1, source_target_pairs={{0,0},{4,8},{8,4},{12,12},{1,1},{5,9},{9,5},{13,13},{2,2},{6,10},{... | collective-permute-start | bytes 1179656 | tf_op jit(solution)/shard_map/ppermute | solution.py:384
  264.4 2.4 shard_map.220
  266.8 1.8 convert_reduce_fusion
  268.5 11.0 %collective-permute-done.54 = bf16[256,768]{1,0:T(8,128)(2,1)S(1)} collective-permute-done((bf16[256,768]{1,0:T(8,128)(2,1)S(1)}, bf16[256,768]{1,0:T(8,128)(2,1)S(1)}, u32[]{:S(2)}, u32[]{:S(2)}) %collective-permute-start.54) | collective-permute-done | bytes 393248 | tf_op jit(solution)/shard_map/ppermute | solution.py:384
  280.4 1.8 shard_map.221
  (326 shorter events, 95.9 us)
Async XLA Ops:
  7.2 94.6 %all-gather.2.cloned.1.call-start = ((), (), s32[]{:S(2)}) async-start(), calls=%async_computation.4 | async-start | bytes 1216512 | tf_op jit(solution)/shard_map/all_gather | solution.py:606
  10.3 28.3 %collective-permute-start.6 = (bf16[144,768]{1,0:T(8,128)(2,1)S(1)}, bf16[144,768]{1,0:T(8,128)(2,1)S(1)}, u32[]{:S(2)}, u32[]{:S(2)}) collective-permute-start(bf16[144,768]{1,0:T(8,128)(2,1)S(1)} %pad_maximum_fusion.12), channel_id=1, source_target_pairs={{0,0},{4,8},{8,4},{12,12},{1,1},{5,9},{9,5},{13,13},{2,2},{6,10},{... | collective-permute-start | bytes 663560 | tf_op jit(solution)/shard_map/ppermute | solution.py:384
  19.4 9.3 %collective-permute-start.2 = (bf16[24,640]{1,0:T(8,128)(2,1)S(1)}, bf16[24,640]{1,0:T(8,128)(2,1)S(1)}, u32[]{:S(2)}, u32[]{:S(2)}) collective-permute-start(bf16[24,640]{1,0:T(8,128)(2,1)S(1)} %get-tuple-element.311), channel_id=1, source_target_pairs={{0,3},{1,2},{2,1},{3,0},{4,7},{5,6},{6,5},{7,4},{8,11},{9,10},{10,... | collective-permute-start | bytes 92168 | tf_op jit(solution)/shard_map/ppermute | solution.py:390
  21.7 7.1 %collective-permute-start.1 = (bf16[24,640]{1,0:T(8,128)(2,1)S(1)}, bf16[24,640]{1,0:T(8,128)(2,1)S(1)}, u32[]{:S(2)}, u32[]{:S(2)}) collective-permute-start(bf16[24,640]{1,0:T(8,128)(2,1)S(1)} %get-tuple-element.312), channel_id=1, source_target_pairs={{0,2},{1,3},{2,0},{3,1},{4,6},{5,7},{6,4},{7,5},{8,10},{9,11},{10,... | collective-permute-start | bytes 92168 | tf_op jit(solution)/shard_map/ppermute | solution.py:390
  21.9 6.9 %collective-permute-start = (bf16[24,640]{1,0:T(8,128)(2,1)S(1)}, bf16[24,640]{1,0:T(8,128)(2,1)S(1)}, u32[]{:S(2)}, u32[]{:S(2)}) collective-permute-start(bf16[24,640]{1,0:T(8,128)(2,1)S(1)} %get-tuple-element.313), channel_id=1, source_target_pairs={{0,1},{1,0},{2,3},{3,2},{4,5},{5,4},{6,7},{7,6},{8,9},{9,8},{10,11... | collective-permute-start | bytes 92168 | tf_op jit(solution)/shard_map/ppermute | solution.py:390
  23.4 36.3 %all-to-all-start = ((bf16[4,96,768]{2,1,0:T(8,128)(2,1)}), bf16[4,96,768]{2,1,0:T(8,128)(2,1)S(1)}, u32[]{:S(2)}, u32[]{:S(2)}) async-start(bf16[4,96,768]{2,1,0:T(8,128)(2,1)} %bitcast.9), calls=%async_computation | async-start | bytes 1179648 | tf_op jit(solution)/shard_map/all_to_all | solution.py:469
  29.4 7.9 %collective-permute-start.3 = (bf16[4,24,640]{2,1,0:T(8,128)(2,1)S(1)}, bf16[4,24,640]{2,1,0:T(8,128)(2,1)S(1)}, u32[]{:S(2)}, u32[]{:S(2)}) collective-permute-start(bf16[4,24,640]{2,1,0:T(8,128)(2,1)S(1)} %gather_fusion), channel_id=1, source_target_pairs={{0,4},{4,0},{1,5},{5,1},{2,6},{6,2},{3,7},{7,3},{8,12},{12,8},{9,1... | collective-permute-start | bytes 368648 | tf_op jit(solution)/shard_map/ppermute | solution.py:380
  32.9 9.2 %collective-permute-start.10 = (bf16[40,768]{1,0:T(8,128)(2,1)S(1)}, bf16[40,768]{1,0:T(8,128)(2,1)S(1)}, u32[]{:S(2)}, u32[]{:S(2)}) collective-permute-start(bf16[40,768]{1,0:T(8,128)(2,1)S(1)} %get-tuple-element.116), channel_id=1, source_target_pairs={{0,0},{4,8},{8,4},{12,12},{16,16},{20,24},{24,20},{28,28},{1,1},{5... | collective-permute-start | bytes 184328 | tf_op jit(solution)/shard_map/ppermute | solution.py:416
  37.3 8.1 %collective-permute-start.5 = (bf16[2,4,24,640]{3,2,1,0:T(8,128)(2,1)S(1)}, bf16[2,4,24,640]{3,2,1,0:T(8,128)(2,1)S(1)}, u32[]{:S(2)}, u32[]{:S(2)}) collective-permute-start(bf16[2,4,24,640]{3,2,1,0:T(8,128)(2,1)S(1)} %pad_maximum_fusion.10), channel_id=1, source_target_pairs={{0,16},{16,0},{1,17},{17,1},{2,18},{18,2},{3,19},{19,3},{4,20},{20... | collective-permute-start | bytes 737288 | tf_op jit(solution)/shard_map/ppermute | solution.py:380
  38.6 11.8 %collective-permute-start.9 = (bf16[128,768]{1,0:T(8,128)(2,1)S(1)}, bf16[128,768]{1,0:T(8,128)(2,1)S(1)}, u32[]{:S(2)}, u32[]{:S(2)}) collective-permute-start(bf16[128,768]{1,0:T(8,128)(2,1)S(1)} %slice.374), channel_id=1, source_target_pairs={{0,3},{1,2},{2,1},{3,0},{4,7},{5,6},{6,5},{7,4},{8,11},{9,10},{10,... | collective-permute-start | bytes 589832 | tf_op jit(solution)/shard_map/ppermute | solution.py:390
  40.1 12.3 %collective-permute-start.8 = (bf16[128,768]{1,0:T(8,128)(2,1)S(1)}, bf16[128,768]{1,0:T(8,128)(2,1)S(1)}, u32[]{:S(2)}, u32[]{:S(2)}) collective-permute-start(bf16[128,768]{1,0:T(8,128)(2,1)S(1)} %slice.374), channel_id=1, source_target_pairs={{0,2},{1,3},{2,0},{3,1},{4,6},{5,7},{6,4},{7,5},{8,10},{9,11},{10,... | collective-permute-start | bytes 589832 | tf_op jit(solution)/shard_map/ppermute | solution.py:390
  42.1 10.3 %collective-permute-start.7 = (bf16[128,768]{1,0:T(8,128)(2,1)S(1)}, bf16[128,768]{1,0:T(8,128)(2,1)S(1)}, u32[]{:S(2)}, u32[]{:S(2)}) collective-permute-start(bf16[128,768]{1,0:T(8,128)(2,1)S(1)} %slice.374), channel_id=1, source_target_pairs={{0,1},{1,0},{2,3},{3,2},{4,5},{5,4},{6,7},{7,6},{8,9},{9,8},{10,11... | collective-permute-start | bytes 589832 | tf_op jit(solution)/shard_map/ppermute | solution.py:390
  42.1 7.2 %collective-permute-start.12 = (bf16[40,768]{1,0:T(8,128)(2,1)S(1)}, bf16[40,768]{1,0:T(8,128)(2,1)S(1)}, u32[]{:S(2)}, u32[]{:S(2)}) collective-permute-start(bf16[40,768]{1,0:T(8,128)(2,1)S(1)} %get-tuple-element.118), channel_id=1, source_target_pairs={{0,16},{4,24},{8,20},{12,28},{16,0},{20,8},{24,4},{28,12},{1,17},{... | collective-permute-start | bytes 184328 | tf_op jit(solution)/shard_map/ppermute | solution.py:416
  58.7 9.2 %collective-permute-start.15 = (bf16[512,640]{1,0:T(8,128)(2,1)}, bf16[512,640]{1,0:T(8,128)(2,1)}, u32[]{:S(2)}, u32[]{:S(2)}) collective-permute-start(bf16[512,640]{1,0:T(8,128)(2,1)} %convolution_convert_fusion.1.q_ref.own_ref), channel_id=1, source_target_pairs={{0,8},{8,0},{1,9},{9,1},{2,10},{10,2},{3,11},{11,3},{4,12},{12,4},... | collective-permute-start | bytes 1966088 | tf_op jit(solution)/shard_map/ppermute | solution.py:380
  60.9 39.5 %collective-permute-start.4 = (bf16[896,768]{1,0:T(8,128)(2,1)}, bf16[896,768]{1,0:T(8,128)(2,1)S(1)}, u32[]{:S(2)}, u32[]{:S(2)}) collective-permute-start(bf16[896,768]{1,0:T(8,128)(2,1)} %pad_maximum_fusion), channel_id=1, source_target_pairs={{0,0},{4,8},{8,4},{12,12},{1,1},{5,9},{9,5},{13,13},{2,2},{6,10},{... | collective-permute-start | bytes 4128776 | tf_op jit(solution)/shard_map/ppermute | solution.py:384
  65.2 23.3 %collective-permute-start.18 = (bf16[160,768]{1,0:T(8,128)(2,1)}, bf16[160,768]{1,0:T(8,128)(2,1)S(1)}, u32[]{:S(2)}, u32[]{:S(2)}) collective-permute-start(bf16[160,768]{1,0:T(8,128)(2,1)} %constant_dynamic-update-slice_fusion), channel_id=1, source_target_pairs={{0,3},{1,2},{2,1},{3,0},{4,7},{5,6},{6,5},{7,4},{8,11},{9,10},{10,... | collective-permute-start | bytes 737288 | tf_op jit(solution)/shard_map/ppermute | solution.py:390
  67.5 24.4 %collective-permute-start.17 = (bf16[160,768]{1,0:T(8,128)(2,1)}, bf16[160,768]{1,0:T(8,128)(2,1)S(1)}, u32[]{:S(2)}, u32[]{:S(2)}) collective-permute-start(bf16[160,768]{1,0:T(8,128)(2,1)} %constant_dynamic-update-slice_fusion), channel_id=1, source_target_pairs={{0,2},{1,3},{2,0},{3,1},{4,6},{5,7},{6,4},{7,5},{8,10},{9,11},{10,... | collective-permute-start | bytes 737288 | tf_op jit(solution)/shard_map/ppermute | solution.py:390
  67.7 24.2 %collective-permute-start.16 = (bf16[160,768]{1,0:T(8,128)(2,1)}, bf16[160,768]{1,0:T(8,128)(2,1)S(1)}, u32[]{:S(2)}, u32[]{:S(2)}) collective-permute-start(bf16[160,768]{1,0:T(8,128)(2,1)} %constant_dynamic-update-slice_fusion), channel_id=1, source_target_pairs={{0,1},{1,0},{2,3},{3,2},{4,5},{5,4},{6,7},{7,6},{8,9},{9,8},{10,11... | collective-permute-start | bytes 737288 | tf_op jit(solution)/shard_map/ppermute | solution.py:390
  101.4 26.6 %collective-permute-start.29 = (bf16[384,768]{1,0:T(8,128)(2,1)}, bf16[384,768]{1,0:T(8,128)(2,1)}, u32[]{:S(2)}, u32[]{:S(2)}) collective-permute-start(bf16[384,768]{1,0:T(8,128)(2,1)} %slice.322), channel_id=1, source_target_pairs={{0,8},{8,0},{1,9},{9,1},{2,10},{10,2},{3,11},{11,3},{4,12},{12,4},... | collective-permute-start | bytes 1769480 | tf_op jit(solution)/shard_map/ppermute | solution.py:380
  103.8 7.3 %collective-permute-start.24 = (bf16[40,768]{1,0:T(8,128)(2,1)S(1)}, bf16[40,768]{1,0:T(8,128)(2,1)S(1)}, u32[]{:S(2)}, u32[]{:S(2)}) collective-permute-start(bf16[40,768]{1,0:T(8,128)(2,1)S(1)} %get-tuple-element.303), channel_id=1, source_target_pairs={{0,20},{4,16},{16,4},{20,0},{1,21},{5,17},{17,5},{21,1},{2,22},{6,... | collective-permute-start | bytes 184328 | tf_op jit(solution)/shard_map/ppermute | solution.py:390
  113.7 7.7 %collective-permute-start.27 = (bf16[160,768]{1,0:T(8,128)(2,1)S(1)}, bf16[160,768]{1,0:T(8,128)(2,1)S(1)}, u32[]{:S(2)}, u32[]{:S(2)}) collective-permute-start(bf16[160,768]{1,0:T(8,128)(2,1)S(1)} %pad_maximum_fusion.11), channel_id=1, source_target_pairs={{0,3},{1,2},{2,1},{3,0},{4,7},{5,6},{6,5},{7,4},{8,11},{9,10},{10,... | collective-permute-start | bytes 737288 | tf_op jit(solution)/shard_map/ppermute | solution.py:390
  113.8 12.5 %collective-permute-start.26 = (bf16[160,768]{1,0:T(8,128)(2,1)S(1)}, bf16[160,768]{1,0:T(8,128)(2,1)S(1)}, u32[]{:S(2)}, u32[]{:S(2)}) collective-permute-start(bf16[160,768]{1,0:T(8,128)(2,1)S(1)} %pad_maximum_fusion.11), channel_id=1, source_target_pairs={{0,2},{1,3},{2,0},{3,1},{4,6},{5,7},{6,4},{7,5},{8,10},{9,11},{10,... | collective-permute-start | bytes 737288 | tf_op jit(solution)/shard_map/ppermute | solution.py:390
  115.7 12.1 %collective-permute-start.25 = (bf16[160,768]{1,0:T(8,128)(2,1)S(1)}, bf16[160,768]{1,0:T(8,128)(2,1)S(1)}, u32[]{:S(2)}, u32[]{:S(2)}) collective-permute-start(bf16[160,768]{1,0:T(8,128)(2,1)S(1)} %pad_maximum_fusion.11), channel_id=1, source_target_pairs={{0,1},{1,0},{2,3},{3,2},{4,5},{5,4},{6,7},{7,6},{8,9},{9,8},{10,11... | collective-permute-start | bytes 737288 | tf_op jit(solution)/shard_map/ppermute | solution.py:390
  139.9 8.2 %collective-permute-start.32 = (bf16[160,768]{1,0:T(8,128)(2,1)S(1)}, bf16[160,768]{1,0:T(8,128)(2,1)S(1)}, u32[]{:S(2)}, u32[]{:S(2)}) collective-permute-start(bf16[160,768]{1,0:T(8,128)(2,1)S(1)} %get-tuple-element.269), channel_id=1, source_target_pairs={{0,3},{1,2},{2,1},{3,0},{4,7},{5,6},{6,5},{7,4},{8,11},{9,10},{10,... | collective-permute-start | bytes 737288 | tf_op jit(solution)/shard_map/ppermute | solution.py:390
  140.0 12.9 %collective-permute-start.31 = (bf16[160,768]{1,0:T(8,128)(2,1)S(1)}, bf16[160,768]{1,0:T(8,128)(2,1)S(1)}, u32[]{:S(2)}, u32[]{:S(2)}) collective-permute-start(bf16[160,768]{1,0:T(8,128)(2,1)S(1)} %get-tuple-element.270), channel_id=1, source_target_pairs={{0,2},{1,3},{2,0},{3,1},{4,6},{5,7},{6,4},{7,5},{8,10},{9,11},{10,... | collective-permute-start | bytes 737288 | tf_op jit(solution)/shard_map/ppermute | solution.py:390
  141.9 12.1 %collective-permute-start.30 = (bf16[160,768]{1,0:T(8,128)(2,1)S(1)}, bf16[160,768]{1,0:T(8,128)(2,1)S(1)}, u32[]{:S(2)}, u32[]{:S(2)}) collective-permute-start(bf16[160,768]{1,0:T(8,128)(2,1)S(1)} %get-tuple-element.271), channel_id=1, source_target_pairs={{0,1},{1,0},{2,3},{3,2},{4,5},{5,4},{6,7},{7,6},{8,9},{9,8},{10,11... | collective-permute-start | bytes 737288 | tf_op jit(solution)/shard_map/ppermute | solution.py:390
  155.3 6.2 %collective-permute-start.35 = (bf16[40,768]{1,0:T(8,128)(2,1)S(1)}, bf16[40,768]{1,0:T(8,128)(2,1)S(1)}, u32[]{:S(2)}, u32[]{:S(2)}) collective-permute-start(bf16[40,768]{1,0:T(8,128)(2,1)S(1)} %get-tuple-element.298), channel_id=1, source_target_pairs={{0,20},{4,16},{16,4},{20,0},{1,21},{5,17},{17,5},{21,1},{2,22},{6,... | collective-permute-start | bytes 184328 | tf_op jit(solution)/shard_map/ppermute | solution.py:390
  165.3 14.8 %collective-permute-start.38 = (bf16[128,192]{1,0:T(8,128)(2,1)S(1)}, bf16[128,192]{1,0:T(8,128)(2,1)}, u32[]{:S(2)}, u32[]{:S(2)}) collective-permute-start(bf16[128,192]{1,0:T(8,128)(2,1)S(1)} %convolution_convert_fusion.6), channel_id=1, source_target_pairs={{0,1},{1,0},{2,3},{3,2},{4,5},{5,4},{6,7},{7,6},{8,9},{9,8},{10,11... | collective-permute-start | bytes 147464 | tf_op jit(solution)/shard_map/ppermute | solution.py:390
  168.0 12.1 %collective-permute-start.39 = (bf16[128,192]{1,0:T(8,128)(2,1)}, bf16[128,192]{1,0:T(8,128)(2,1)}, u32[]{:S(2)}, u32[]{:S(2)}) collective-permute-start(bf16[128,192]{1,0:T(8,128)(2,1)} %convolution_convert_fusion.5), channel_id=1, source_target_pairs={{0,2},{1,3},{2,0},{3,1},{4,6},{5,7},{6,4},{7,5},{8,10},{9,11},{10,... | collective-permute-start | bytes 147464 | tf_op jit(solution)/shard_map/ppermute | solution.py:390
  168.9 11.2 %collective-permute-start.40 = (bf16[128,192]{1,0:T(8,128)(2,1)}, bf16[128,192]{1,0:T(8,128)(2,1)}, u32[]{:S(2)}, u32[]{:S(2)}) collective-permute-start(bf16[128,192]{1,0:T(8,128)(2,1)} %convolution_convert_fusion.4), channel_id=1, source_target_pairs={{0,3},{1,2},{2,1},{3,0},{4,7},{5,6},{6,5},{7,4},{8,11},{9,10},{10,... | collective-permute-start | bytes 147464 | tf_op jit(solution)/shard_map/ppermute | solution.py:390
  170.3 24.0 %all-to-all-start.1 = ((bf16[4,96,768]{2,1,0:T(8,128)(2,1)}), bf16[4,96,768]{2,1,0:T(8,128)(2,1)}, u32[]{:S(2)}, u32[]{:S(2)}) async-start(bf16[4,96,768]{2,1,0:T(8,128)(2,1)} %bitcast.58), calls=%async_computation.1 | async-start | bytes 1179648 | tf_op jit(solution)/shard_map/all_to_all | solution.py:469
  177.1 21.5 %collective-permute-start.48 = (bf16[2,192,768]{2,1,0:T(8,128)(2,1)}, bf16[2,192,768]{2,1,0:T(8,128)(2,1)}, u32[]{:S(2)}, u32[]{:S(2)}) collective-permute-start(bf16[2,192,768]{2,1,0:T(8,128)(2,1)} %fusion.21), channel_id=1, source_target_pairs={{0,8},{8,0},{1,9},{9,1},{2,10},{10,2},{3,11},{11,3},{4,12},{12,4},... | collective-permute-start | bytes 1769480 | tf_op jit(solution)/shard_map/ppermute | solution.py:380
  194.4 10.8 %collective-permute-start.41 = (bf16[512,384]{1,0:T(8,128)(2,1)}, bf16[512,384]{1,0:T(8,128)(2,1)S(1)}, u32[]{:S(2)}, u32[]{:S(2)}) collective-permute-start(bf16[512,384]{1,0:T(8,128)(2,1)} %get-tuple-element.177), channel_id=1, source_target_pairs={{0,8},{8,0},{1,9},{9,1},{2,10},{10,2},{3,11},{11,3},{4,12},{12,4},... | collective-permute-start | bytes 1179656 | tf_op jit(solution)/shard_map/ppermute | solution.py:380
  195.9 14.5 %collective-permute-start.45 = (bf16[160,768]{1,0:T(8,128)(2,1)}, bf16[160,768]{1,0:T(8,128)(2,1)S(1)}, u32[]{:S(2)}, u32[]{:S(2)}) collective-permute-start(bf16[160,768]{1,0:T(8,128)(2,1)} %get-tuple-element.180), channel_id=1, source_target_pairs={{0,1},{1,0},{2,3},{3,2},{4,5},{5,4},{6,7},{7,6},{8,9},{9,8},{10,11... | collective-permute-start | bytes 737288 | tf_op jit(solution)/shard_map/ppermute | solution.py:390
  197.4 15.4 %collective-permute-start.46 = (bf16[160,768]{1,0:T(8,128)(2,1)}, bf16[160,768]{1,0:T(8,128)(2,1)}, u32[]{:S(2)}, u32[]{:S(2)}) collective-permute-start(bf16[160,768]{1,0:T(8,128)(2,1)} %get-tuple-element.181), channel_id=1, source_target_pairs={{0,2},{1,3},{2,0},{3,1},{4,6},{5,7},{6,4},{7,5},{8,10},{9,11},{10,... | collective-permute-start | bytes 737288 | tf_op jit(solution)/shard_map/ppermute | solution.py:390
  198.6 16.2 %collective-permute-start.47 = (bf16[160,768]{1,0:T(8,128)(2,1)}, bf16[160,768]{1,0:T(8,128)(2,1)}, u32[]{:S(2)}, u32[]{:S(2)}) collective-permute-start(bf16[160,768]{1,0:T(8,128)(2,1)} %get-tuple-element.182), channel_id=1, source_target_pairs={{0,3},{1,2},{2,1},{3,0},{4,7},{5,6},{6,5},{7,4},{8,11},{9,10},{10,... | collective-permute-start | bytes 737288 | tf_op jit(solution)/shard_map/ppermute | solution.py:390
  198.7 18.7 %collective-permute-start.49 = (bf16[384,768]{1,0:T(8,128)(2,1)}, bf16[384,768]{1,0:T(8,128)(2,1)}, u32[]{:S(2)}, u32[]{:S(2)}) collective-permute-start(bf16[384,768]{1,0:T(8,128)(2,1)} %add_convert_fusion.2), channel_id=1, source_target_pairs={{0,0},{4,8},{8,4},{12,12},{1,1},{5,9},{9,5},{13,13},{2,2},{6,10},{... | collective-permute-start | bytes 1769480 | tf_op jit(solution)/shard_map/ppermute | solution.py:384
  205.2 59.2 %collective-permute-start.55 = (bf16[384,768]{1,0:T(8,128)(2,1)}, bf16[384,768]{1,0:T(8,128)(2,1)}, u32[]{:S(2)}, u32[]{:S(2)}) collective-permute-start(bf16[384,768]{1,0:T(8,128)(2,1)} %bitcast.59), channel_id=1, source_target_pairs={{0,0},{4,8},{8,4},{12,12},{1,1},{5,9},{9,5},{13,13},{2,2},{6,10},{... | collective-permute-start | bytes 1769480 | tf_op jit(solution)/shard_map/ppermute | solution.py:384
  210.4 32.3 %collective-permute-start.44 = (bf16[128,768]{1,0:T(8,128)(2,1)}, bf16[128,768]{1,0:T(8,128)(2,1)}, u32[]{:S(2)}, u32[]{:S(2)}) collective-permute-start(bf16[128,768]{1,0:T(8,128)(2,1)} %get-tuple-element.280), channel_id=1, source_target_pairs={{0,3},{1,2},{2,1},{3,0},{4,7},{5,6},{6,5},{7,4},{8,11},{9,10},{10,... | collective-permute-start | bytes 589832 | tf_op jit(solution)/shard_map/ppermute | solution.py:390
  212.8 30.3 %collective-permute-start.43 = (bf16[128,768]{1,0:T(8,128)(2,1)}, bf16[128,768]{1,0:T(8,128)(2,1)}, u32[]{:S(2)}, u32[]{:S(2)}) collective-permute-start(bf16[128,768]{1,0:T(8,128)(2,1)} %get-tuple-element.281), channel_id=1, source_target_pairs={{0,2},{1,3},{2,0},{3,1},{4,6},{5,7},{6,4},{7,5},{8,10},{9,11},{10,... | collective-permute-start | bytes 589832 | tf_op jit(solution)/shard_map/ppermute | solution.py:390
  214.8 28.4 %collective-permute-start.42 = (bf16[128,768]{1,0:T(8,128)(2,1)}, bf16[128,768]{1,0:T(8,128)(2,1)}, u32[]{:S(2)}, u32[]{:S(2)}) collective-permute-start(bf16[128,768]{1,0:T(8,128)(2,1)} %get-tuple-element.282), channel_id=1, source_target_pairs={{0,1},{1,0},{2,3},{3,2},{4,5},{5,4},{6,7},{7,6},{8,9},{9,8},{10,11... | collective-permute-start | bytes 589832 | tf_op jit(solution)/shard_map/ppermute | solution.py:390
  221.2 29.4 %all-to-all-start.3 = ((bf16[16,24,768]{2,1,0:T(8,128)(2,1)}), bf16[16,24,768]{2,1,0:T(8,128)(2,1)}, u32[]{:S(2)}, u32[]{:S(2)}) async-start(bf16[16,24,768]{2,1,0:T(8,128)(2,1)} %bitcast.77), calls=%async_computation.3 | async-start | bytes 1179648 | tf_op jit(solution)/shard_map/all_to_all | solution.py:483
  233.4 25.1 %collective-permute-start.52 = (bf16[40,768]{1,0:T(8,128)(2,1)}, bf16[40,768]{1,0:T(8,128)(2,1)}, u32[]{:S(2)}, u32[]{:S(2)}) collective-permute-start(bf16[40,768]{1,0:T(8,128)(2,1)} %get-tuple-element.294), channel_id=1, source_target_pairs={{0,20},{4,16},{16,4},{20,0},{1,21},{5,17},{17,5},{21,1},{2,22},{6,... | collective-permute-start | bytes 184328 | tf_op jit(solution)/shard_map/ppermute | solution.py:390
  242.8 15.7 %collective-permute-start.51 = (bf16[40,768]{1,0:T(8,128)(2,1)S(1)}, bf16[40,768]{1,0:T(8,128)(2,1)}, u32[]{:S(2)}, u32[]{:S(2)}) collective-permute-start(bf16[40,768]{1,0:T(8,128)(2,1)S(1)} %copy-done.28), channel_id=1, source_target_pairs={{0,16},{4,20},{16,0},{20,4},{1,17},{5,21},{17,1},{21,5},{2,18},{6,... | collective-permute-start | bytes 184328 | tf_op jit(solution)/shard_map/ppermute | solution.py:390
  243.1 15.4 %collective-permute-start.50 = (bf16[40,768]{1,0:T(8,128)(2,1)S(1)}, bf16[40,768]{1,0:T(8,128)(2,1)}, u32[]{:S(2)}, u32[]{:S(2)}) collective-permute-start(bf16[40,768]{1,0:T(8,128)(2,1)S(1)} %copy-done.27), channel_id=1, source_target_pairs={{0,4},{4,0},{16,20},{20,16},{1,5},{5,1},{17,21},{21,17},{2,6},{6,2... | collective-permute-start | bytes 184328 | tf_op jit(solution)/shard_map/ppermute | solution.py:390
  243.2 6.5 %collective-permute-start.53 = (bf16[2,192,640]{2,1,0:T(8,128)(2,1)}, bf16[2,192,640]{2,1,0:T(8,128)(2,1)S(1)}, u32[]{:S(2)}, u32[]{:S(2)}) collective-permute-start(bf16[2,192,640]{2,1,0:T(8,128)(2,1)} %fusion.22), channel_id=1, source_target_pairs={{0,8},{8,0},{1,9},{9,1},{2,10},{10,2},{3,11},{11,3},{4,12},{12,4},... | collective-permute-start | bytes 1474568 | tf_op jit(solution)/shard_map/ppermute | solution.py:380
  250.6 29.0 %all-to-all-start.2 = ((bf16[16,24,640]{2,1,0:T(8,128)(2,1)}), bf16[16,24,640]{2,1,0:T(8,128)(2,1)S(1)}, u32[]{:S(2)}, u32[]{:S(2)}) async-start(bf16[16,24,640]{2,1,0:T(8,128)(2,1)} %bitcast.73), calls=%async_computation.2 | async-start | bytes 983040 | tf_op jit(solution)/shard_map/all_to_all | solution.py:483
  259.7 19.9 %collective-permute-start.54 = (bf16[256,768]{1,0:T(8,128)(2,1)S(1)}, bf16[256,768]{1,0:T(8,128)(2,1)S(1)}, u32[]{:S(2)}, u32[]{:S(2)}) collective-permute-start(bf16[256,768]{1,0:T(8,128)(2,1)S(1)} %pad_maximum_fusion.7), channel_id=1, source_target_pairs={{0,0},{4,8},{8,4},{12,12},{1,1},{5,9},{9,5},{13,13},{2,2},{6,10},{... | collective-permute-start | bytes 1179656 | tf_op jit(solution)/shard_map/ppermute | solution.py:384
  (49 other events, 436.3 us)
Sparse Core Ops, SparseCore 0:
  11.0 59.8 all-gather.1

commit v4 on v3

--- a/solution.py
+++ b/solution.py
@@ -711,10 +711,9 @@
         - middle * middle_unit**3 * jnp.mean(scaled * middle, axis=-1, keepdims=True)
     )
     grad_branch = grad_middle.astype(BF16)
+    grad_attended = dot_t(grad_branch, full_o).astype(BF16)
     grad_attended = [
-        dot_t(
-            grad_branch, lax.dynamic_slice_in_dim(full_o, (my_major ^ i) * q_width, q_width)
-        ).astype(BF16)
+        lax.dynamic_slice_in_dim(grad_attended, (my_major ^ i) * q_width, q_width, axis=1)
         for i in range(major)
     ]
     grad_inner, grad_outer, attended, grad_branch = after(

time: 296 us -> 293 us (0.990)
  waiting for transfers between devices: 66.4 us -> 72.7 us
  starting transfers between devices: 103 us -> 98.5 us
  other arithmetic: 30.7 us -> 27.6 us
    ppermute x5, waiting for transfers between devices: 11 us -> 16.1 us  [turn(): return lax.ppermute(value, ('ec', 'gh'), [(0, 0), (1, 2), (2, 1), (3, 3)])]
    all_to_all x2, starting transfers between devices: 16.5 us -> 11.8 us  [scatter_rows(): return lax.all_to_all(value, REST, 0, 0, tiled=True)]
    dot_general x8 -> x5, matrix products: 7.19 us -> 5.47 us  [dot_t(): lax.dot_general(left, right, (((1,), (1,)), ((), ())), preferred_element_...]
  transfers between devices with their start and end apart: 61 -> 61, of which waited for: 23 -> 26; matrix products, arithmetic and copies ran while one was open for 19% -> 18% of each run, Pallas kernels for 11% -> 11%
where the time goes in v4:
time: 293 us; the launch traced here: 291 us
  starting transfers between devices  98.5 us (34%)
  waiting for transfers between devices  72.7 us (25%)
  Pallas kernels  34.6 us (12%)
  other arithmetic  27.6 us (9%)
  local copies, waits for them, and re-layouts  21.5 us (7%)
  matrix products  20.7 us (7%)
  between operations  15.3 us (5%)
    ppermute x36, waiting for transfers between devices, exchange(): lax.ppermute(parts[step], axis, [(source, source ^ step) for source in ra...  48.3 us
    ppermute x36, starting transfers between devices, exchange(): lax.ppermute(parts[step], axis, [(source, source ^ step) for source in ra...  39.2 us
    ppermute x5, starting transfers between devices, turn(): return lax.ppermute(value, ('ec', 'gh'), [(0, 0), (1, 2), (2, 1), (3, 3)])  20.4 us
    ppermute x5, waiting for transfers between devices, turn(): return lax.ppermute(value, ('ec', 'gh'), [(0, 0), (1, 2), (2, 1), (3, 3)])  16.1 us
    pallas_call x1, Pallas kernels, backward_attention(): pl.pallas_call(functools.partial(attention_back_kernel, heads, rows), gri...  12.6 us
    ppermute x11, starting transfers between devices, swap(): return lax.ppermute(value, axis, [(0, 1), (1, 0)])  11.9 us
    all_to_all x2, starting transfers between devices, scatter_rows(): return lax.all_to_all(value, REST, 0, 0, tiled=True)  11.8 us
    pallas_call x1, Pallas kernels, forward_attention(): pl.pallas_call(functools.partial(attention_kernel, heads, rows), grid=(st...  9.92 us
  transfers between devices with their start and end apart: 61, of which 26 were waited for; matrix products, arithmetic and copies ran while one was open for 18% of the time, Pallas kernels for 11%

profile of v4, /device:TPU:1, one launch (start us, length us, event | category | flops | bytes accessed | tf_op | source)
XLA Modules:
  0.0 290.8 jit_solution(18078535331666278711)
XLA Ops:
  10.3 5.6 %collective-permute-start.6 = (bf16[144,768]{1,0:T(8,128)(2,1)S(1)}, bf16[144,768]{1,0:T(8,128)(2,1)S(1)}, u32[]{:S(2)}, u32[]{:S(2)}) collective-permute-start(bf16[144,768]{1,0:T(8,128)(2,1)S(1)} %pad_maximum_fusion.12), channel_id=1, source_target_pairs={{0,0},{4,8},{8,4},{12,12},{1,1},{5,9},{9,5},{13,13},{2,2},{6,10},{... | collective-permute-start | bytes 663560 | tf_op jit(solution)/shard_map/ppermute | solution.py:384
  19.4 2.3 collective-permute-start.2
  23.4 3.5 %all-to-all-start = ((bf16[4,96,768]{2,1,0:T(8,128)(2,1)}), bf16[4,96,768]{2,1,0:T(8,128)(2,1)S(1)}, u32[]{:S(2)}, u32[]{:S(2)}) async-start(bf16[4,96,768]{2,1,0:T(8,128)(2,1)} %bitcast.9), calls=%async_computation | async-start | bytes 1179648 | tf_op jit(solution)/shard_map/all_to_all | solution.py:469
  30.6 2.3 shard_map.215.near_ref
  33.0 3.0 %collective-permute-start.10 = (bf16[40,768]{1,0:T(8,128)(2,1)S(1)}, bf16[40,768]{1,0:T(8,128)(2,1)S(1)}, u32[]{:S(2)}, u32[]{:S(2)}) collective-permute-start(bf16[40,768]{1,0:T(8,128)(2,1)S(1)} %get-tuple-element.116), channel_id=1, source_target_pairs={{0,0},{4,8},{8,4},{12,12},{16,16},{20,24},{24,20},{28,28},{1,1},{5... | collective-permute-start | bytes 184328 | tf_op jit(solution)/shard_map/ppermute | solution.py:416
  41.7 2.7 collective-permute-start.12
  46.9 2.5 collective-permute-done.12
  50.5 1.9 collective-permute-done.8
  53.0 1.7 collective-permute-start.14
  60.2 2.3 pad_maximum_fusion
  62.4 3.1 %collective-permute-start.4 = (bf16[896,768]{1,0:T(8,128)(2,1)}, bf16[896,768]{1,0:T(8,128)(2,1)S(1)}, u32[]{:S(2)}, u32[]{:S(2)}) collective-permute-start(bf16[896,768]{1,0:T(8,128)(2,1)} %pad_maximum_fusion), channel_id=1, source_target_pairs={{0,0},{4,8},{8,4},{12,12},{1,1},{5,9},{9,5},{13,13},{2,2},{6,10},{... | collective-permute-start | bytes 4128776 | tf_op jit(solution)/shard_map/ppermute | solution.py:384
  66.8 2.2 collective-permute-start.18
  69.5 9.9 %shard_map.216 = (bf16[512,192]{1,0:T(8,128)(2,1)}, f32[512,384]{1,0:T(8,128)}, f32[4,3,128]{2,1,0:T(4,128)}) custom-call(s32[4]{0:T(128)} %slice_bitcast_fusion.18.block_ref, s32[8]{0:T(128)} %copy-done.32, s32[10]{0:T(128)} %broadcast_select_fusion.place_ref, f32[2,3]{1,0:T(2,128)} %pad_maximum_fusion.19.far_ref, ...), custom_call_target="tpu_custom_call" | custom-call | flops 805306368 | bytes 3145728 | tf_op jit(solution)/shard_map/pallas_call | solution.py:309
  79.4 10.3 %collective-permute-done.18 = bf16[160,768]{1,0:T(8,128)(2,1)S(1)} collective-permute-done((bf16[160,768]{1,0:T(8,128)(2,1)}, bf16[160,768]{1,0:T(8,128)(2,1)S(1)}, u32[]{:S(2)}, u32[]{:S(2)}) %collective-permute-start.18) | collective-permute-done | bytes 245792 | tf_op jit(solution)/shard_map/ppermute | solution.py:390
  89.8 3.3 %collective-permute-done.17 = bf16[160,768]{1,0:T(8,128)(2,1)S(1)} collective-permute-done((bf16[160,768]{1,0:T(8,128)(2,1)}, bf16[160,768]{1,0:T(8,128)(2,1)S(1)}, u32[]{:S(2)}, u32[]{:S(2)}) %collective-permute-start.17) | collective-permute-done | bytes 245792 | tf_op jit(solution)/shard_map/ppermute | solution.py:390
  94.2 2.8 collective-permute-start.21
  97.4 2.3 collective-permute-done.21
  102.9 1.7 multiply_reduce_fusion.3
  105.0 4.0 %collective-permute-start.24 = (bf16[40,768]{1,0:T(8,128)(2,1)S(1)}, bf16[40,768]{1,0:T(8,128)(2,1)S(1)}, u32[]{:S(2)}, u32[]{:S(2)}) collective-permute-start(bf16[40,768]{1,0:T(8,128)(2,1)S(1)} %get-tuple-element.303), channel_id=1, source_target_pairs={{0,20},{4,16},{16,4},{20,0},{1,21},{5,17},{17,5},{21,1},{2,22},{6,... | collective-permute-start | bytes 184328 | tf_op jit(solution)/shard_map/ppermute | solution.py:390
  109.7 2.6 collective-permute-done.24
  114.9 2.2 collective-permute-start.26
  118.6 3.9 %collective-permute-done.27 = bf16[160,768]{1,0:T(8,128)(2,1)S(1)} collective-permute-done((bf16[160,768]{1,0:T(8,128)(2,1)S(1)}, bf16[160,768]{1,0:T(8,128)(2,1)S(1)}, u32[]{:S(2)}, u32[]{:S(2)}) %collective-permute-start.27) | collective-permute-done | bytes 245792 | tf_op jit(solution)/shard_map/ppermute | solution.py:390
  122.5 5.1 %collective-permute-done.26 = bf16[160,768]{1,0:T(8,128)(2,1)S(1)} collective-permute-done((bf16[160,768]{1,0:T(8,128)(2,1)S(1)}, bf16[160,768]{1,0:T(8,128)(2,1)S(1)}, u32[]{:S(2)}, u32[]{:S(2)}) %collective-permute-start.26) | collective-permute-done | bytes 245792 | tf_op jit(solution)/shard_map/ppermute | solution.py:390
  141.1 2.2 collective-permute-start.31
  144.7 4.5 %collective-permute-done.32 = bf16[160,768]{1,0:T(8,128)(2,1)S(1)} collective-permute-done((bf16[160,768]{1,0:T(8,128)(2,1)S(1)}, bf16[160,768]{1,0:T(8,128)(2,1)S(1)}, u32[]{:S(2)}, u32[]{:S(2)}) %collective-permute-start.32) | collective-permute-done | bytes 245792 | tf_op jit(solution)/shard_map/ppermute | solution.py:390
  149.2 5.1 %collective-permute-done.31 = bf16[160,768]{1,0:T(8,128)(2,1)S(1)} collective-permute-done((bf16[160,768]{1,0:T(8,128)(2,1)S(1)}, bf16[160,768]{1,0:T(8,128)(2,1)S(1)}, u32[]{:S(2)}, u32[]{:S(2)}) %collective-permute-start.31) | collective-permute-done | bytes 245792 | tf_op jit(solution)/shard_map/ppermute | solution.py:390
  169.4 4.4 %all-to-all-start.1 = ((bf16[4,96,768]{2,1,0:T(8,128)(2,1)}), bf16[4,96,768]{2,1,0:T(8,128)(2,1)}, u32[]{:S(2)}, u32[]{:S(2)}) async-start(bf16[4,96,768]{2,1,0:T(8,128)(2,1)} %bitcast.58), calls=%async_computation.1 | async-start | bytes 1179648 | tf_op jit(solution)/shard_map/all_to_all | solution.py:469
  176.1 2.4 collective-permute-start.48
  180.2 12.6 %shard_map.217 = (bf16[512,256]{1,0:T(8,128)(2,1)}, f32[512,384]{1,0:T(8,128)}, bf16[512,384]{1,0:T(8,128)(2,1)}, f32[3,384,128]{2,1,0:T(8,128)}, f32[3,2,128]{2,1,0:T(2,128)}) custom-call(s32[4]{0:T(128)} %slice_bitcast_fusion.18.block_ref, s32[8]{0:T(128)} %copy-done.32, s32[10]{0:T(128)} %broadcast_select_fusion.place_ref, ...), custom_call_target="tpu_custom_call" | custom-call | flops 2013265920 | bytes 3145728 | tf_op jit(solution)/shard_map/pallas_call | solution.py:342
  197.1 3.4 %collective-permute-start.49 = (bf16[384,768]{1,0:T(8,128)(2,1)}, bf16[384,768]{1,0:T(8,128)(2,1)}, u32[]{:S(2)}, u32[]{:S(2)}) collective-permute-start(bf16[384,768]{1,0:T(8,128)(2,1)} %add_convert_fusion.2), channel_id=1, source_target_pairs={{0,0},{4,8},{8,4},{12,12},{1,1},{5,9},{9,5},{13,13},{2,2},{6,10},{... | collective-permute-start | bytes 1769480 | tf_op jit(solution)/shard_map/ppermute | solution.py:384
  200.6 2.1 fusion.16
  202.8 3.3 %collective-permute-start.55 = (bf16[384,768]{1,0:T(8,128)(2,1)}, bf16[384,768]{1,0:T(8,128)(2,1)}, u32[]{:S(2)}, u32[]{:S(2)}) collective-permute-start(bf16[384,768]{1,0:T(8,128)(2,1)} %bitcast.59), channel_id=1, source_target_pairs={{0,0},{4,8},{8,4},{12,12},{1,1},{5,9},{9,5},{13,13},{2,2},{6,10},{... | collective-permute-start | bytes 1769480 | tf_op jit(solution)/shard_map/ppermute | solution.py:384
  206.2 1.8 fusion.12
  209.0 2.3 collective-permute-start.44
  212.6 2.6 collective-permute-start.42
  215.2 4.3 %collective-permute-done.49 = bf16[384,768]{1,0:T(8,128)(2,1)} collective-permute-done((bf16[384,768]{1,0:T(8,128)(2,1)}, bf16[384,768]{1,0:T(8,128)(2,1)}, u32[]{:S(2)}, u32[]{:S(2)}) %collective-permute-start.49) | collective-permute-done | bytes 589856 | tf_op jit(solution)/shard_map/ppermute | solution.py:384
  219.5 3.2 %shard_map.219 = f32[3,128]{1,0:T(4,128)} custom-call(f32[3,384,128]{2,1,0:T(8,128)} %get-tuple-element.198.near_ref, f32[3,2,128]{2,1,0:T(2,128)} %get-tuple-element.199.far_ref), custom_call_target="tpu_custom_call" | custom-call | tf_op jit(solution)/shard_map/pallas_call | solution.py:743
  223.3 5.2 %all-to-all-start.3 = ((bf16[16,24,768]{2,1,0:T(8,128)(2,1)}), bf16[16,24,768]{2,1,0:T(8,128)(2,1)}, u32[]{:S(2)}, u32[]{:S(2)}) async-start(bf16[16,24,768]{2,1,0:T(8,128)(2,1)} %bitcast.77), calls=%async_computation.3 | async-start | bytes 1179648 | tf_op jit(solution)/shard_map/all_to_all | solution.py:483
  230.8 3.1 %collective-permute-start.52 = (bf16[40,768]{1,0:T(8,128)(2,1)}, bf16[40,768]{1,0:T(8,128)(2,1)}, u32[]{:S(2)}, u32[]{:S(2)}) collective-permute-start(bf16[40,768]{1,0:T(8,128)(2,1)} %get-tuple-element.294), channel_id=1, source_target_pairs={{0,20},{4,16},{16,4},{20,0},{1,21},{5,17},{17,5},{21,1},{2,22},{6,... | collective-permute-start | bytes 184328 | tf_op jit(solution)/shard_map/ppermute | solution.py:390
  234.9 2.1 pad_add_fusion
  237.8 2.3 shard_map.218
  240.6 4.5 %collective-permute-start.53 = (bf16[2,192,640]{2,1,0:T(8,128)(2,1)}, bf16[2,192,640]{2,1,0:T(8,128)(2,1)S(1)}, u32[]{:S(2)}, u32[]{:S(2)}) collective-permute-start(bf16[2,192,640]{2,1,0:T(8,128)(2,1)} %fusion.22), channel_id=1, source_target_pairs={{0,8},{8,0},{1,9},{9,1},{2,10},{10,2},{3,11},{11,3},{4,12},{12,4},... | collective-permute-start | bytes 1474568 | tf_op jit(solution)/shard_map/ppermute | solution.py:380
  247.7 6.6 %all-to-all-start.2 = ((bf16[16,24,640]{2,1,0:T(8,128)(2,1)}), bf16[16,24,640]{2,1,0:T(8,128)(2,1)S(1)}, u32[]{:S(2)}, u32[]{:S(2)}) async-start(bf16[16,24,640]{2,1,0:T(8,128)(2,1)} %bitcast.73), calls=%async_computation.2 | async-start | bytes 983040 | tf_op jit(solution)/shard_map/all_to_all | solution.py:483
  255.7 5.0 %collective-permute-start.54 = (bf16[256,768]{1,0:T(8,128)(2,1)S(1)}, bf16[256,768]{1,0:T(8,128)(2,1)S(1)}, u32[]{:S(2)}, u32[]{:S(2)}) collective-permute-start(bf16[256,768]{1,0:T(8,128)(2,1)S(1)} %pad_maximum_fusion.7), channel_id=1, source_target_pairs={{0,0},{4,8},{8,4},{12,12},{1,1},{5,9},{9,5},{13,13},{2,2},{6,10},{... | collective-permute-start | bytes 1179656 | tf_op jit(solution)/shard_map/ppermute | solution.py:384
  260.8 2.4 shard_map.220
  263.1 1.8 convert_reduce_fusion
  264.9 11.8 %collective-permute-done.54 = bf16[256,768]{1,0:T(8,128)(2,1)S(1)} collective-permute-done((bf16[256,768]{1,0:T(8,128)(2,1)S(1)}, bf16[256,768]{1,0:T(8,128)(2,1)S(1)}, u32[]{:S(2)}, u32[]{:S(2)}) %collective-permute-start.54) | collective-permute-done | bytes 393248 | tf_op jit(solution)/shard_map/ppermute | solution.py:384
  277.5 1.8 shard_map.221
  (318 shorter events, 93.2 us)
Async XLA Ops:
  7.2 95.7 %all-gather.2.cloned.1.call-start = ((), (), s32[]{:S(2)}) async-start(), calls=%async_computation.4 | async-start | bytes 1216512 | tf_op jit(solution)/shard_map/all_gather | solution.py:606
  10.3 28.3 %collective-permute-start.6 = (bf16[144,768]{1,0:T(8,128)(2,1)S(1)}, bf16[144,768]{1,0:T(8,128)(2,1)S(1)}, u32[]{:S(2)}, u32[]{:S(2)}) collective-permute-start(bf16[144,768]{1,0:T(8,128)(2,1)S(1)} %pad_maximum_fusion.12), channel_id=1, source_target_pairs={{0,0},{4,8},{8,4},{12,12},{1,1},{5,9},{9,5},{13,13},{2,2},{6,10},{... | collective-permute-start | bytes 663560 | tf_op jit(solution)/shard_map/ppermute | solution.py:384
  19.4 9.3 %collective-permute-start.2 = (bf16[24,640]{1,0:T(8,128)(2,1)S(1)}, bf16[24,640]{1,0:T(8,128)(2,1)S(1)}, u32[]{:S(2)}, u32[]{:S(2)}) collective-permute-start(bf16[24,640]{1,0:T(8,128)(2,1)S(1)} %get-tuple-element.315), channel_id=1, source_target_pairs={{0,3},{1,2},{2,1},{3,0},{4,7},{5,6},{6,5},{7,4},{8,11},{9,10},{10,... | collective-permute-start | bytes 92168 | tf_op jit(solution)/shard_map/ppermute | solution.py:390
  21.7 7.1 %collective-permute-start.1 = (bf16[24,640]{1,0:T(8,128)(2,1)S(1)}, bf16[24,640]{1,0:T(8,128)(2,1)S(1)}, u32[]{:S(2)}, u32[]{:S(2)}) collective-permute-start(bf16[24,640]{1,0:T(8,128)(2,1)S(1)} %get-tuple-element.316), channel_id=1, source_target_pairs={{0,2},{1,3},{2,0},{3,1},{4,6},{5,7},{6,4},{7,5},{8,10},{9,11},{10,... | collective-permute-start | bytes 92168 | tf_op jit(solution)/shard_map/ppermute | solution.py:390
  21.9 6.9 %collective-permute-start = (bf16[24,640]{1,0:T(8,128)(2,1)S(1)}, bf16[24,640]{1,0:T(8,128)(2,1)S(1)}, u32[]{:S(2)}, u32[]{:S(2)}) collective-permute-start(bf16[24,640]{1,0:T(8,128)(2,1)S(1)} %get-tuple-element.317), channel_id=1, source_target_pairs={{0,1},{1,0},{2,3},{3,2},{4,5},{5,4},{6,7},{7,6},{8,9},{9,8},{10,11... | collective-permute-start | bytes 92168 | tf_op jit(solution)/shard_map/ppermute | solution.py:390
  23.4 36.8 %all-to-all-start = ((bf16[4,96,768]{2,1,0:T(8,128)(2,1)}), bf16[4,96,768]{2,1,0:T(8,128)(2,1)S(1)}, u32[]{:S(2)}, u32[]{:S(2)}) async-start(bf16[4,96,768]{2,1,0:T(8,128)(2,1)} %bitcast.9), calls=%async_computation | async-start | bytes 1179648 | tf_op jit(solution)/shard_map/all_to_all | solution.py:469
  29.4 7.9 %collective-permute-start.3 = (bf16[4,24,640]{2,1,0:T(8,128)(2,1)S(1)}, bf16[4,24,640]{2,1,0:T(8,128)(2,1)S(1)}, u32[]{:S(2)}, u32[]{:S(2)}) collective-permute-start(bf16[4,24,640]{2,1,0:T(8,128)(2,1)S(1)} %gather_fusion), channel_id=1, source_target_pairs={{0,4},{4,0},{1,5},{5,1},{2,6},{6,2},{3,7},{7,3},{8,12},{12,8},{9,1... | collective-permute-start | bytes 368648 | tf_op jit(solution)/shard_map/ppermute | solution.py:380
  33.0 8.6 %collective-permute-start.10 = (bf16[40,768]{1,0:T(8,128)(2,1)S(1)}, bf16[40,768]{1,0:T(8,128)(2,1)S(1)}, u32[]{:S(2)}, u32[]{:S(2)}) collective-permute-start(bf16[40,768]{1,0:T(8,128)(2,1)S(1)} %get-tuple-element.116), channel_id=1, source_target_pairs={{0,0},{4,8},{8,4},{12,12},{16,16},{20,24},{24,20},{28,28},{1,1},{5... | collective-permute-start | bytes 184328 | tf_op jit(solution)/shard_map/ppermute | solution.py:416
  37.3 8.1 %collective-permute-start.5 = (bf16[2,4,24,640]{3,2,1,0:T(8,128)(2,1)S(1)}, bf16[2,4,24,640]{3,2,1,0:T(8,128)(2,1)S(1)}, u32[]{:S(2)}, u32[]{:S(2)}) collective-permute-start(bf16[2,4,24,640]{3,2,1,0:T(8,128)(2,1)S(1)} %pad_maximum_fusion.10), channel_id=1, source_target_pairs={{0,16},{16,0},{1,17},{17,1},{2,18},{18,2},{3,19},{19,3},{4,20},{20... | collective-permute-start | bytes 737288 | tf_op jit(solution)/shard_map/ppermute | solution.py:380
  38.6 11.9 %collective-permute-start.9 = (bf16[128,768]{1,0:T(8,128)(2,1)S(1)}, bf16[128,768]{1,0:T(8,128)(2,1)S(1)}, u32[]{:S(2)}, u32[]{:S(2)}) collective-permute-start(bf16[128,768]{1,0:T(8,128)(2,1)S(1)} %slice.374), channel_id=1, source_target_pairs={{0,3},{1,2},{2,1},{3,0},{4,7},{5,6},{6,5},{7,4},{8,11},{9,10},{10,... | collective-permute-start | bytes 589832 | tf_op jit(solution)/shard_map/ppermute | solution.py:390
  40.2 12.2 %collective-permute-start.8 = (bf16[128,768]{1,0:T(8,128)(2,1)S(1)}, bf16[128,768]{1,0:T(8,128)(2,1)S(1)}, u32[]{:S(2)}, u32[]{:S(2)}) collective-permute-start(bf16[128,768]{1,0:T(8,128)(2,1)S(1)} %slice.374), channel_id=1, source_target_pairs={{0,2},{1,3},{2,0},{3,1},{4,6},{5,7},{6,4},{7,5},{8,10},{9,11},{10,... | collective-permute-start | bytes 589832 | tf_op jit(solution)/shard_map/ppermute | solution.py:390
  41.6 10.8 %collective-permute-start.7 = (bf16[128,768]{1,0:T(8,128)(2,1)S(1)}, bf16[128,768]{1,0:T(8,128)(2,1)S(1)}, u32[]{:S(2)}, u32[]{:S(2)}) collective-permute-start(bf16[128,768]{1,0:T(8,128)(2,1)S(1)} %slice.374), channel_id=1, source_target_pairs={{0,1},{1,0},{2,3},{3,2},{4,5},{5,4},{6,7},{7,6},{8,9},{9,8},{10,11... | collective-permute-start | bytes 589832 | tf_op jit(solution)/shard_map/ppermute | solution.py:390
  41.7 7.7 %collective-permute-start.12 = (bf16[40,768]{1,0:T(8,128)(2,1)S(1)}, bf16[40,768]{1,0:T(8,128)(2,1)S(1)}, u32[]{:S(2)}, u32[]{:S(2)}) collective-permute-start(bf16[40,768]{1,0:T(8,128)(2,1)S(1)} %get-tuple-element.118), channel_id=1, source_target_pairs={{0,16},{4,24},{8,20},{12,28},{16,0},{20,8},{24,4},{28,12},{1,17},{... | collective-permute-start | bytes 184328 | tf_op jit(solution)/shard_map/ppermute | solution.py:416
  59.2 10.3 %collective-permute-start.15 = (bf16[512,640]{1,0:T(8,128)(2,1)}, bf16[512,640]{1,0:T(8,128)(2,1)}, u32[]{:S(2)}, u32[]{:S(2)}) collective-permute-start(bf16[512,640]{1,0:T(8,128)(2,1)} %convolution_convert_fusion.1.q_ref.own_ref), channel_id=1, source_target_pairs={{0,8},{8,0},{1,9},{9,1},{2,10},{10,2},{3,11},{11,3},{4,12},{12,4},... | collective-permute-start | bytes 1966088 | tf_op jit(solution)/shard_map/ppermute | solution.py:380
  62.4 39.2 %collective-permute-start.4 = (bf16[896,768]{1,0:T(8,128)(2,1)}, bf16[896,768]{1,0:T(8,128)(2,1)S(1)}, u32[]{:S(2)}, u32[]{:S(2)}) collective-permute-start(bf16[896,768]{1,0:T(8,128)(2,1)} %pad_maximum_fusion), channel_id=1, source_target_pairs={{0,0},{4,8},{8,4},{12,12},{1,1},{5,9},{9,5},{13,13},{2,2},{6,10},{... | collective-permute-start | bytes 4128776 | tf_op jit(solution)/shard_map/ppermute | solution.py:384
  66.8 22.9 %collective-permute-start.18 = (bf16[160,768]{1,0:T(8,128)(2,1)}, bf16[160,768]{1,0:T(8,128)(2,1)S(1)}, u32[]{:S(2)}, u32[]{:S(2)}) collective-permute-start(bf16[160,768]{1,0:T(8,128)(2,1)} %constant_dynamic-update-slice_fusion), channel_id=1, source_target_pairs={{0,3},{1,2},{2,1},{3,0},{4,7},{5,6},{6,5},{7,4},{8,11},{9,10},{10,... | collective-permute-start | bytes 737288 | tf_op jit(solution)/shard_map/ppermute | solution.py:390
  69.1 24.0 %collective-permute-start.17 = (bf16[160,768]{1,0:T(8,128)(2,1)}, bf16[160,768]{1,0:T(8,128)(2,1)S(1)}, u32[]{:S(2)}, u32[]{:S(2)}) collective-permute-start(bf16[160,768]{1,0:T(8,128)(2,1)} %constant_dynamic-update-slice_fusion), channel_id=1, source_target_pairs={{0,2},{1,3},{2,0},{3,1},{4,6},{5,7},{6,4},{7,5},{8,10},{9,11},{10,... | collective-permute-start | bytes 737288 | tf_op jit(solution)/shard_map/ppermute | solution.py:390
  69.3 23.8 %collective-permute-start.16 = (bf16[160,768]{1,0:T(8,128)(2,1)}, bf16[160,768]{1,0:T(8,128)(2,1)S(1)}, u32[]{:S(2)}, u32[]{:S(2)}) collective-permute-start(bf16[160,768]{1,0:T(8,128)(2,1)} %constant_dynamic-update-slice_fusion), channel_id=1, source_target_pairs={{0,1},{1,0},{2,3},{3,2},{4,5},{5,4},{6,7},{7,6},{8,9},{9,8},{10,11... | collective-permute-start | bytes 737288 | tf_op jit(solution)/shard_map/ppermute | solution.py:390
  102.5 26.5 %collective-permute-start.29 = (bf16[384,768]{1,0:T(8,128)(2,1)}, bf16[384,768]{1,0:T(8,128)(2,1)}, u32[]{:S(2)}, u32[]{:S(2)}) collective-permute-start(bf16[384,768]{1,0:T(8,128)(2,1)} %slice.322), channel_id=1, source_target_pairs={{0,8},{8,0},{1,9},{9,1},{2,10},{10,2},{3,11},{11,3},{4,12},{12,4},... | collective-permute-start | bytes 1769480 | tf_op jit(solution)/shard_map/ppermute | solution.py:380
  105.0 7.3 %collective-permute-start.24 = (bf16[40,768]{1,0:T(8,128)(2,1)S(1)}, bf16[40,768]{1,0:T(8,128)(2,1)S(1)}, u32[]{:S(2)}, u32[]{:S(2)}) collective-permute-start(bf16[40,768]{1,0:T(8,128)(2,1)S(1)} %get-tuple-element.303), channel_id=1, source_target_pairs={{0,20},{4,16},{16,4},{20,0},{1,21},{5,17},{17,5},{21,1},{2,22},{6,... | collective-permute-start | bytes 184328 | tf_op jit(solution)/shard_map/ppermute | solution.py:390
  114.8 7.7 %collective-permute-start.27 = (bf16[160,768]{1,0:T(8,128)(2,1)S(1)}, bf16[160,768]{1,0:T(8,128)(2,1)S(1)}, u32[]{:S(2)}, u32[]{:S(2)}) collective-permute-start(bf16[160,768]{1,0:T(8,128)(2,1)S(1)} %pad_maximum_fusion.11), channel_id=1, source_target_pairs={{0,3},{1,2},{2,1},{3,0},{4,7},{5,6},{6,5},{7,4},{8,11},{9,10},{10,... | collective-permute-start | bytes 737288 | tf_op jit(solution)/shard_map/ppermute | solution.py:390
  114.9 12.8 %collective-permute-start.26 = (bf16[160,768]{1,0:T(8,128)(2,1)S(1)}, bf16[160,768]{1,0:T(8,128)(2,1)S(1)}, u32[]{:S(2)}, u32[]{:S(2)}) collective-permute-start(bf16[160,768]{1,0:T(8,128)(2,1)S(1)} %pad_maximum_fusion.11), channel_id=1, source_target_pairs={{0,2},{1,3},{2,0},{3,1},{4,6},{5,7},{6,4},{7,5},{8,10},{9,11},{10,... | collective-permute-start | bytes 737288 | tf_op jit(solution)/shard_map/ppermute | solution.py:390
  117.1 11.8 %collective-permute-start.25 = (bf16[160,768]{1,0:T(8,128)(2,1)S(1)}, bf16[160,768]{1,0:T(8,128)(2,1)S(1)}, u32[]{:S(2)}, u32[]{:S(2)}) collective-permute-start(bf16[160,768]{1,0:T(8,128)(2,1)S(1)} %pad_maximum_fusion.11), channel_id=1, source_target_pairs={{0,1},{1,0},{2,3},{3,2},{4,5},{5,4},{6,7},{7,6},{8,9},{9,8},{10,11... | collective-permute-start | bytes 737288 | tf_op jit(solution)/shard_map/ppermute | solution.py:390
  141.0 8.2 %collective-permute-start.32 = (bf16[160,768]{1,0:T(8,128)(2,1)S(1)}, bf16[160,768]{1,0:T(8,128)(2,1)S(1)}, u32[]{:S(2)}, u32[]{:S(2)}) collective-permute-start(bf16[160,768]{1,0:T(8,128)(2,1)S(1)} %get-tuple-element.269), channel_id=1, source_target_pairs={{0,3},{1,2},{2,1},{3,0},{4,7},{5,6},{6,5},{7,4},{8,11},{9,10},{10,... | collective-permute-start | bytes 737288 | tf_op jit(solution)/shard_map/ppermute | solution.py:390
  141.1 13.2 %collective-permute-start.31 = (bf16[160,768]{1,0:T(8,128)(2,1)S(1)}, bf16[160,768]{1,0:T(8,128)(2,1)S(1)}, u32[]{:S(2)}, u32[]{:S(2)}) collective-permute-start(bf16[160,768]{1,0:T(8,128)(2,1)S(1)} %get-tuple-element.270), channel_id=1, source_target_pairs={{0,2},{1,3},{2,0},{3,1},{4,6},{5,7},{6,4},{7,5},{8,10},{9,11},{10,... | collective-permute-start | bytes 737288 | tf_op jit(solution)/shard_map/ppermute | solution.py:390
  143.3 11.8 %collective-permute-start.30 = (bf16[160,768]{1,0:T(8,128)(2,1)S(1)}, bf16[160,768]{1,0:T(8,128)(2,1)S(1)}, u32[]{:S(2)}, u32[]{:S(2)}) collective-permute-start(bf16[160,768]{1,0:T(8,128)(2,1)S(1)} %get-tuple-element.271), channel_id=1, source_target_pairs={{0,1},{1,0},{2,3},{3,2},{4,5},{5,4},{6,7},{7,6},{8,9},{9,8},{10,11... | collective-permute-start | bytes 737288 | tf_op jit(solution)/shard_map/ppermute | solution.py:390
  155.9 6.5 %collective-permute-start.35 = (bf16[40,768]{1,0:T(8,128)(2,1)S(1)}, bf16[40,768]{1,0:T(8,128)(2,1)S(1)}, u32[]{:S(2)}, u32[]{:S(2)}) collective-permute-start(bf16[40,768]{1,0:T(8,128)(2,1)S(1)} %get-tuple-element.298), channel_id=1, source_target_pairs={{0,20},{4,16},{16,4},{20,0},{1,21},{5,17},{17,5},{21,1},{2,22},{6,... | collective-permute-start | bytes 184328 | tf_op jit(solution)/shard_map/ppermute | solution.py:390
  166.7 11.8 %collective-permute-start.40 = (bf16[128,192]{1,0:T(8,128)(2,1)}, bf16[128,192]{1,0:T(8,128)(2,1)}, u32[]{:S(2)}, u32[]{:S(2)}) collective-permute-start(bf16[128,192]{1,0:T(8,128)(2,1)} %get-tuple-element.310), channel_id=1, source_target_pairs={{0,3},{1,2},{2,1},{3,0},{4,7},{5,6},{6,5},{7,4},{8,11},{9,10},{10,... | collective-permute-start | bytes 147464 | tf_op jit(solution)/shard_map/ppermute | solution.py:390
  167.1 11.4 %collective-permute-start.39 = (bf16[128,192]{1,0:T(8,128)(2,1)}, bf16[128,192]{1,0:T(8,128)(2,1)}, u32[]{:S(2)}, u32[]{:S(2)}) collective-permute-start(bf16[128,192]{1,0:T(8,128)(2,1)} %get-tuple-element.311), channel_id=1, source_target_pairs={{0,2},{1,3},{2,0},{3,1},{4,6},{5,7},{6,4},{7,5},{8,10},{9,11},{10,... | collective-permute-start | bytes 147464 | tf_op jit(solution)/shard_map/ppermute | solution.py:390
  168.6 9.9 %collective-permute-start.38 = (bf16[128,192]{1,0:T(8,128)(2,1)}, bf16[128,192]{1,0:T(8,128)(2,1)}, u32[]{:S(2)}, u32[]{:S(2)}) collective-permute-start(bf16[128,192]{1,0:T(8,128)(2,1)} %get-tuple-element.312), channel_id=1, source_target_pairs={{0,1},{1,0},{2,3},{3,2},{4,5},{5,4},{6,7},{7,6},{8,9},{9,8},{10,11... | collective-permute-start | bytes 147464 | tf_op jit(solution)/shard_map/ppermute | solution.py:390
  169.4 23.5 %all-to-all-start.1 = ((bf16[4,96,768]{2,1,0:T(8,128)(2,1)}), bf16[4,96,768]{2,1,0:T(8,128)(2,1)}, u32[]{:S(2)}, u32[]{:S(2)}) async-start(bf16[4,96,768]{2,1,0:T(8,128)(2,1)} %bitcast.58), calls=%async_computation.1 | async-start | bytes 1179648 | tf_op jit(solution)/shard_map/all_to_all | solution.py:469
  176.1 21.0 %collective-permute-start.48 = (bf16[2,192,768]{2,1,0:T(8,128)(2,1)}, bf16[2,192,768]{2,1,0:T(8,128)(2,1)}, u32[]{:S(2)}, u32[]{:S(2)}) collective-permute-start(bf16[2,192,768]{2,1,0:T(8,128)(2,1)} %fusion.21), channel_id=1, source_target_pairs={{0,8},{8,0},{1,9},{9,1},{2,10},{10,2},{3,11},{11,3},{4,12},{12,4},... | collective-permute-start | bytes 1769480 | tf_op jit(solution)/shard_map/ppermute | solution.py:380
  192.9 9.9 %collective-permute-start.41 = (bf16[512,384]{1,0:T(8,128)(2,1)}, bf16[512,384]{1,0:T(8,128)(2,1)S(1)}, u32[]{:S(2)}, u32[]{:S(2)}) collective-permute-start(bf16[512,384]{1,0:T(8,128)(2,1)} %get-tuple-element.177), channel_id=1, source_target_pairs={{0,8},{8,0},{1,9},{9,1},{2,10},{10,2},{3,11},{11,3},{4,12},{12,4},... | collective-permute-start | bytes 1179656 | tf_op jit(solution)/shard_map/ppermute | solution.py:380
  194.4 14.6 %collective-permute-start.45 = (bf16[160,768]{1,0:T(8,128)(2,1)}, bf16[160,768]{1,0:T(8,128)(2,1)S(1)}, u32[]{:S(2)}, u32[]{:S(2)}) collective-permute-start(bf16[160,768]{1,0:T(8,128)(2,1)} %get-tuple-element.180), channel_id=1, source_target_pairs={{0,1},{1,0},{2,3},{3,2},{4,5},{5,4},{6,7},{7,6},{8,9},{9,8},{10,11... | collective-permute-start | bytes 737288 | tf_op jit(solution)/shard_map/ppermute | solution.py:390
  195.9 15.4 %collective-permute-start.46 = (bf16[160,768]{1,0:T(8,128)(2,1)}, bf16[160,768]{1,0:T(8,128)(2,1)}, u32[]{:S(2)}, u32[]{:S(2)}) collective-permute-start(bf16[160,768]{1,0:T(8,128)(2,1)} %get-tuple-element.181), channel_id=1, source_target_pairs={{0,2},{1,3},{2,0},{3,1},{4,6},{5,7},{6,4},{7,5},{8,10},{9,11},{10,... | collective-permute-start | bytes 737288 | tf_op jit(solution)/shard_map/ppermute | solution.py:390
  197.1 15.5 %collective-permute-start.47 = (bf16[160,768]{1,0:T(8,128)(2,1)}, bf16[160,768]{1,0:T(8,128)(2,1)}, u32[]{:S(2)}, u32[]{:S(2)}) collective-permute-start(bf16[160,768]{1,0:T(8,128)(2,1)} %get-tuple-element.182), channel_id=1, source_target_pairs={{0,3},{1,2},{2,1},{3,0},{4,7},{5,6},{6,5},{7,4},{8,11},{9,10},{10,... | collective-permute-start | bytes 737288 | tf_op jit(solution)/shard_map/ppermute | solution.py:390
  197.1 22.3 %collective-permute-start.49 = (bf16[384,768]{1,0:T(8,128)(2,1)}, bf16[384,768]{1,0:T(8,128)(2,1)}, u32[]{:S(2)}, u32[]{:S(2)}) collective-permute-start(bf16[384,768]{1,0:T(8,128)(2,1)} %add_convert_fusion.2), channel_id=1, source_target_pairs={{0,0},{4,8},{8,4},{12,12},{1,1},{5,9},{9,5},{13,13},{2,2},{6,10},{... | collective-permute-start | bytes 1769480 | tf_op jit(solution)/shard_map/ppermute | solution.py:384
  202.8 58.0 %collective-permute-start.55 = (bf16[384,768]{1,0:T(8,128)(2,1)}, bf16[384,768]{1,0:T(8,128)(2,1)}, u32[]{:S(2)}, u32[]{:S(2)}) collective-permute-start(bf16[384,768]{1,0:T(8,128)(2,1)} %bitcast.59), channel_id=1, source_target_pairs={{0,0},{4,8},{8,4},{12,12},{1,1},{5,9},{9,5},{13,13},{2,2},{6,10},{... | collective-permute-start | bytes 1769480 | tf_op jit(solution)/shard_map/ppermute | solution.py:384
  209.0 31.2 %collective-permute-start.44 = (bf16[128,768]{1,0:T(8,128)(2,1)}, bf16[128,768]{1,0:T(8,128)(2,1)}, u32[]{:S(2)}, u32[]{:S(2)}) collective-permute-start(bf16[128,768]{1,0:T(8,128)(2,1)} %get-tuple-element.280), channel_id=1, source_target_pairs={{0,3},{1,2},{2,1},{3,0},{4,7},{5,6},{6,5},{7,4},{8,11},{9,10},{10,... | collective-permute-start | bytes 589832 | tf_op jit(solution)/shard_map/ppermute | solution.py:390
  211.3 29.1 %collective-permute-start.43 = (bf16[128,768]{1,0:T(8,128)(2,1)}, bf16[128,768]{1,0:T(8,128)(2,1)}, u32[]{:S(2)}, u32[]{:S(2)}) collective-permute-start(bf16[128,768]{1,0:T(8,128)(2,1)} %get-tuple-element.281), channel_id=1, source_target_pairs={{0,2},{1,3},{2,0},{3,1},{4,6},{5,7},{6,4},{7,5},{8,10},{9,11},{10,... | collective-permute-start | bytes 589832 | tf_op jit(solution)/shard_map/ppermute | solution.py:390
  212.6 28.0 %collective-permute-start.42 = (bf16[128,768]{1,0:T(8,128)(2,1)}, bf16[128,768]{1,0:T(8,128)(2,1)}, u32[]{:S(2)}, u32[]{:S(2)}) collective-permute-start(bf16[128,768]{1,0:T(8,128)(2,1)} %get-tuple-element.282), channel_id=1, source_target_pairs={{0,1},{1,0},{2,3},{3,2},{4,5},{5,4},{6,7},{7,6},{8,9},{9,8},{10,11... | collective-permute-start | bytes 589832 | tf_op jit(solution)/shard_map/ppermute | solution.py:390
  223.3 24.4 %all-to-all-start.3 = ((bf16[16,24,768]{2,1,0:T(8,128)(2,1)}), bf16[16,24,768]{2,1,0:T(8,128)(2,1)}, u32[]{:S(2)}, u32[]{:S(2)}) async-start(bf16[16,24,768]{2,1,0:T(8,128)(2,1)} %bitcast.77), calls=%async_computation.3 | async-start | bytes 1179648 | tf_op jit(solution)/shard_map/all_to_all | solution.py:483
  230.8 23.8 %collective-permute-start.52 = (bf16[40,768]{1,0:T(8,128)(2,1)}, bf16[40,768]{1,0:T(8,128)(2,1)}, u32[]{:S(2)}, u32[]{:S(2)}) collective-permute-start(bf16[40,768]{1,0:T(8,128)(2,1)} %get-tuple-element.294), channel_id=1, source_target_pairs={{0,20},{4,16},{16,4},{20,0},{1,21},{5,17},{17,5},{21,1},{2,22},{6,... | collective-permute-start | bytes 184328 | tf_op jit(solution)/shard_map/ppermute | solution.py:390
  240.2 14.4 %collective-permute-start.51 = (bf16[40,768]{1,0:T(8,128)(2,1)}, bf16[40,768]{1,0:T(8,128)(2,1)}, u32[]{:S(2)}, u32[]{:S(2)}) collective-permute-start(bf16[40,768]{1,0:T(8,128)(2,1)} %get-tuple-element.295), channel_id=1, source_target_pairs={{0,16},{4,20},{16,0},{20,4},{1,17},{5,21},{17,1},{21,5},{2,18},{6,... | collective-permute-start | bytes 184328 | tf_op jit(solution)/shard_map/ppermute | solution.py:390
  240.4 14.1 %collective-permute-start.50 = (bf16[40,768]{1,0:T(8,128)(2,1)}, bf16[40,768]{1,0:T(8,128)(2,1)}, u32[]{:S(2)}, u32[]{:S(2)}) collective-permute-start(bf16[40,768]{1,0:T(8,128)(2,1)} %get-tuple-element.296), channel_id=1, source_target_pairs={{0,4},{4,0},{16,20},{20,16},{1,5},{5,1},{17,21},{21,17},{2,6},{6,2... | collective-permute-start | bytes 184328 | tf_op jit(solution)/shard_map/ppermute | solution.py:390
  240.6 6.2 %collective-permute-start.53 = (bf16[2,192,640]{2,1,0:T(8,128)(2,1)}, bf16[2,192,640]{2,1,0:T(8,128)(2,1)S(1)}, u32[]{:S(2)}, u32[]{:S(2)}) collective-permute-start(bf16[2,192,640]{2,1,0:T(8,128)(2,1)} %fusion.22), channel_id=1, source_target_pairs={{0,8},{8,0},{1,9},{9,1},{2,10},{10,2},{3,11},{11,3},{4,12},{12,4},... | collective-permute-start | bytes 1474568 | tf_op jit(solution)/shard_map/ppermute | solution.py:380
  247.7 29.0 %all-to-all-start.2 = ((bf16[16,24,640]{2,1,0:T(8,128)(2,1)}), bf16[16,24,640]{2,1,0:T(8,128)(2,1)S(1)}, u32[]{:S(2)}, u32[]{:S(2)}) async-start(bf16[16,24,640]{2,1,0:T(8,128)(2,1)} %bitcast.73), calls=%async_computation.2 | async-start | bytes 983040 | tf_op jit(solution)/shard_map/all_to_all | solution.py:483
  255.7 21.0 %collective-permute-start.54 = (bf16[256,768]{1,0:T(8,128)(2,1)S(1)}, bf16[256,768]{1,0:T(8,128)(2,1)S(1)}, u32[]{:S(2)}, u32[]{:S(2)}) collective-permute-start(bf16[256,768]{1,0:T(8,128)(2,1)S(1)} %pad_maximum_fusion.7), channel_id=1, source_target_pairs={{0,0},{4,8},{8,4},{12,12},{1,1},{5,9},{9,5},{13,13},{2,2},{6,10},{... | collective-permute-start | bytes 1179656 | tf_op jit(solution)/shard_map/ppermute | solution.py:384
  (46 other events, 396.0 us)
Sparse Core Ops, SparseCore 0:
  11.0 58.9 all-gather.1
